TPU v7x, 512 devices: a whole 4x4x16 slice. The times are simulated.
512 devices in a mesh: batch: 32 (over z, core), feat: 16 (over y, x).
Axes of the slice: x: 4, y: 4, z: 16, core: 2. Of those that a mesh axis runs over, the one named last changes fastest.
Arguments:
- vertex_embeddings: bfloat16 [32768, 768], P('batch', 'feat'), may hold values from -6 to 6
- adjacent_vertices: int32 [64, 5, 512, 8], P('batch'), may hold values from -1 to 511
- node_counts: int32 [64], P('batch'), may hold values from 64 to 512, as said below
- target_offsets: int32 [64], P('batch'), may hold values from 0 to 448, as said below
- weight_one: bfloat16 [6, 768, 1024], P(None, 'feat'), may hold values from -0.09375 to 0.09375
- bias_one: float32 [1024], P('feat'), may hold values from -3 to 3
- weight_two: bfloat16 [6, 1024, 153], P(None, 'feat'), may hold values from -0.078125 to 0.078125
- score_derivative: bfloat16 [4096, 153], P('batch'), may hold values from -6 to 6
Outputs:
- logits: float32 [4096, 153], P('batch')
- grad_one: float32 [6, 768, 1024], P(None, 'feat')
- grad_two: float32 [6, 1024, 153], P(None, 'feat')
Inputs may be any that keep to these rules, and one draw needn't show every extreme that they name: `node_counts`: in the 2 subgraphs of each index of batch one holds exactly 512 live nodes. `target_offsets`: the 64 targets of a subgraph are live nodes. `adjacent_vertices`: -1 marks an empty slot; slots naming a node at or beyond the subgraph's count, and rows of such nodes, are ignored.
All inputs are finite; a program needn't handle non-finite values.
Results may differ from a plain program's by a relative error of at most 0.012.
The roundings to bfloat16 on the way count: a program that leaves them out, or rounds other values in their place, can miss the bound.
Values may be sent and summed in bfloat16 or wider, within the bound.
No kernel may reach another device: no remote copies, remote signals or barrier semaphores. Data moves between devices by JAX's collectives and lax.ppermute only.
A program may use at most 64 MiB of HBM per device.

v0:
```python
import jax
import jax.numpy as jnp
from jax import lax
from jax.sharding import PartitionSpec as P

SEED_VERTICES = 64


def node_masks(neighbor_ids, counts):
    capacity = neighbor_ids.shape[2]
    position = jnp.arange(capacity, dtype=jnp.int32)
    live_rows = position[None, :] < counts[:, None]
    adjacency = jnp.zeros(neighbor_ids.shape[:3] + (capacity,), jnp.bfloat16)
    for fan_slot in range(neighbor_ids.shape[3]):
        adjacency = adjacency + (neighbor_ids[:, :, :, fan_slot, None] == position).astype(
            jnp.bfloat16
        )
    keep_mask = live_rows[:, None, :, None] & live_rows[:, None, None, :]
    adjacency = jnp.where(keep_mask, adjacency, jnp.zeros((), jnp.bfloat16))
    degree = jnp.maximum(jnp.sum(adjacency, axis=3, dtype=jnp.float32), 1.0)
    return (adjacency, degree)


def first_inputs(vertex_embedding_lines, adjacency, degree):
    mixed = (
        jnp.einsum(
            "grds,gsf->grdf", adjacency, vertex_embedding_lines, preferred_element_type=jnp.float32
        )
        / degree[..., None]
    )
    return jnp.concatenate([vertex_embedding_lines[:, None], mixed.astype(jnp.bfloat16)], axis=1)


def slice_matrix(source, start_row):
    return lax.dynamic_slice_in_dim(source, start_row, SEED_VERTICES, 1)


def slice_rows(source, start_row):
    return lax.dynamic_slice_in_dim(source, start_row, SEED_VERTICES, 0)


def place_rows(grad_block, piece, start_row):
    return lax.dynamic_update_slice_in_dim(grad_block, piece, start_row, 0)


def local(
    vertex_embeddings,
    adjacent_vertices,
    node_counts,
    target_offsets,
    weight_one,
    bias_one,
    weight_two,
    score_derivative,
):
    groups = node_counts.shape[0]
    capacity = adjacent_vertices.shape[2]
    adjacency, degree = node_masks(adjacent_vertices, node_counts)
    vertex_embedding_lines = vertex_embeddings.reshape(groups, capacity, vertex_embeddings.shape[1])
    local_in = first_inputs(vertex_embedding_lines, adjacency, degree)
    partial_sums = jnp.einsum(
        "grnf,rfh->gnh", local_in, weight_one, preferred_element_type=jnp.float32
    )
    partial_sums = partial_sums.reshape(groups * capacity, partial_sums.shape[2])
    hidden_sums = lax.psum_scatter(partial_sums, "feat", scatter_dimension=1, tiled=True)
    preact = hidden_sums.reshape(groups, capacity, hidden_sums.shape[1]) + bias_one
    hidden_state = jnp.maximum(preact, 0.0).astype(jnp.bfloat16)
    target_adjacency_list = jax.vmap(slice_matrix)(adjacency, target_offsets)
    target_deg = jax.vmap(slice_matrix)(degree, target_offsets)
    target_hidden = jax.vmap(slice_rows)(hidden_state, target_offsets)
    gathered = (
        jnp.einsum(
            "lpvj,ljd->lpvd",
            target_adjacency_list,
            hidden_state,
            preferred_element_type=jnp.float32,
        )
        / target_deg[..., None]
    )
    second_in = jnp.concatenate([target_hidden[:, None], gathered.astype(jnp.bfloat16)], axis=1)
    partial_scores = jnp.einsum(
        "grth,rhc->gtc", second_in, weight_two, preferred_element_type=jnp.float32
    )
    scores = lax.psum(partial_scores, "feat")
    scores = scores.reshape(groups * SEED_VERTICES, scores.shape[2])
    upstream = score_derivative.reshape(groups, SEED_VERTICES, score_derivative.shape[1])
    grad_second = jnp.einsum(
        "grth,gtc->rhc", second_in, upstream, preferred_element_type=jnp.float32
    )
    returned = jnp.einsum("gtc,rhc->grth", upstream, weight_two, preferred_element_type=jnp.float32)
    self_part = returned[:, 0].astype(jnp.bfloat16)
    neighbor_spread = (returned[:, 1:] / target_deg[..., None]).astype(jnp.bfloat16)
    hidden_grad = jnp.einsum(
        "kifq,kifp->kqp", target_adjacency_list, neighbor_spread, preferred_element_type=jnp.float32
    )
    placed = jax.vmap(place_rows)(
        jnp.zeros_like(hidden_grad), self_part.astype(jnp.float32), target_offsets
    )
    pre_grad = jnp.where(preact > 0, hidden_grad + placed, 0.0).astype(jnp.bfloat16)
    flat_grad = pre_grad.reshape(groups * capacity, pre_grad.shape[2])
    piece = lax.all_gather(flat_grad, "feat", axis=1, tiled=True)
    shaped = piece.reshape(groups, capacity, piece.shape[1])
    grad_first = jnp.einsum("grnf,gnh->rfh", local_in, shaped, preferred_element_type=jnp.float32)
    summed_first, summed_second = lax.psum((grad_first, grad_second), "batch")
    return (scores, summed_first, summed_second)


def solution(mesh):
    placed = (
        P("batch", "feat"),
        P("batch", None, None, None),
        P("batch"),
        P("batch"),
        P(None, "feat", None),
        P("feat"),
        P(None, "feat", None),
        P("batch", None),
    )
    return jax.shard_map(
        local,
        mesh=mesh,
        in_specs=placed,
        out_specs=(P("batch", None), P(None, "feat", None), P(None, "feat", None)),
        check_vma=False,
    )
```

profile of v0, /device:TPU:1, one launch (start us, length us, event | category | flops | bytes accessed | tf_op | source)
XLA Modules:
  0.0 568.5 jit_solution(10809636102586224769)
XLA Ops:
  7.2 1.0 reshape.76
  8.2 0.9 broadcast_in_dim_reshape.3
  9.2 2.2 fusion.46
  11.4 0.3 copy.97
  11.7 0.3 copy.96
  11.9 0.3 copy.95
  12.2 0.3 copy.94
  12.5 0.3 copy.93
  12.7 1.0 copy.92
  13.8 1.1 copy.91
  14.8 1.1 copy.90
  15.9 0.7 iota_compare_fusion.8
  16.6 0.2 copy.38
  16.8 1.7 broadcast_and_fusion
  18.5 26.2 %convert_reduce_fusion = (f32[2,5,512]{1,0,2:T(2,128)S(1)}, bf16[2,5,512,512]{3,1,0,2:T(8,128)(2,1)}) fusion(s32[2,5,512]{1,0,2:T(2,128)S(1)} %bitcast.115, s32[2,5,512]{1,0,2:T(2,128)S(1)} %bitcast.116, s32[2,5,512]{1,0,2:T(2,128)S(1)} %bitcast.117, s32[2,5,512]{1,0,2:T(2,128)S(1)} %bitcast.118, s32[2,5,512]{1,0,2:T(2,128)S(1)} %bitcast.119, ...), kind=kLoop, calls=%fused_computation.7 | loop fusion | flops 91745280 | bytes 5951488 | tf_op jit(solution)/shard_map/reduce_sum | solution.py:20
  44.7 0.2 broadcast_maximum_fusion
  45.0 0.2 copy.57
  45.2 9.2 %divide_convert_fusion = bf16[2,5,512,48]{2,3,1,0:T(8,128)(2,1)S(1)} fusion(bf16[2,5,512,512]{3,1,0,2:T(8,128)(2,1)} %get-tuple-element.30, f32[2,5,512]{2,1,0:T(8,128)S(1)} %copy.57, bf16[2,512,48,1]{1,0,2,3:T(2,128)(2,1)S(1)} %bitcast.131), kind=kOutput, calls=%fused_computation.45 | convolution fusion | flops 252149760 | bytes 5853184 | tf_op jit(solution)/shard_map/grds,gsf->grdf/dot_general | solution.py:26
  54.4 3.2 fusion.25
  57.7 5.5 copy.59
  63.1 0.2 all-gather.2.cloned.1.call-start
  63.4 4.0 gather_fusion.1
  67.4 0.8 gather_fusion.2
  68.2 0.1 copy.64
  68.3 0.1 pad_clamp_fusion
  68.4 0.1 copy.71
  68.5 0.2 reshape.80
  68.7 0.1 copy.82
  68.8 0.2 convolution_bitcast_fusion.2
  69.1 14.4 %while.1 = (s32[]{:T(128)}, f32[2,512,64]{1,2,0:T(8,128)S(1)}, s32[2,3]{1,0:T(2,128)S(1)}, f32[2,64,64]{2,1,0:T(8,128)S(1)}, s32[]{:T(128)}, /*index=5*/s32[3]{0:T(128)S(1)}, s32[]{:T(128)}) while((s32[]{:T(128)}, f32[2,512,64]{1,2,0:T(8,128)S(1)}, s32[2,3]{1,0:T(2,128)S(1)}, f32[2,64,64]{2,1,0:T(8,128)S(1)}, s32[]{:T(128)}, /*index=5*/s32[3]{0:T(128)S(1)}, ...), condition=%wide.while_cond, body=%wide.while_body.sunk | while | flops 4115 | bytes 180403 | solution.py:43
  69.1 0.7 fusion.51
  69.8 1.3 constant_dynamic-slice_fusion.5
  71.1 0.1 copy.129
  71.2 2.7 and_reduce_fusion.2
  73.9 0.6 dynamic-slice_select_fusion.2
  74.5 0.1 copy.130
  74.6 1.7 dynamic-update-slice.3
  76.4 0.7 fusion.51
  77.0 1.3 constant_dynamic-slice_fusion.5
  78.4 0.1 copy.129
  78.4 2.7 and_reduce_fusion.2
  81.1 0.6 dynamic-slice_select_fusion.2
  81.7 0.1 copy.130
  81.8 1.7 dynamic-update-slice.3
  83.6 76.4 %reduce-scatter.2.cloned.1.call-done = f32[1024,64]{0,1:T(8,128)} async-done(((f32[1024,1024]{0,1:T(8,128)}), f32[1024,64]{0,1:T(8,128)}) %reduce-scatter.2.cloned.1.call-update) | async-done | bytes 262160 | tf_op jit(solution)/shard_map/reduce_scatter | solution.py:65
  159.9 1.4 fusion.22
  161.3 0.7 copy.109
  162.0 0.0 all-reduce.6.cloned.1.call-start
  162.1 1.0 maximum_convert_fusion
  163.1 0.2 copy.61
  163.3 0.7 gather_fusion
  164.0 0.4 fusion.18
  164.3 0.2 fusion.31
  164.6 0.7 copy.65
  165.3 1.0 convolution_bitcast_fusion.1
  166.3 0.0 all-reduce.8.cloned.1.call-start
  166.4 58.1 %all-gather.2.cloned.1.call-done = bf16[1024,1024]{0,1:T(8,128)(2,1)} async-done(((bf16[1024,64]{0,1:T(8,128)(2,1)}), bf16[1024,1024]{0,1:T(8,128)(2,1)}) %all-gather.2.cloned.1.call-update) | async-done | bytes 2097168 | tf_op jit(solution)/shard_map/all_gather | solution.py:101
  224.5 2.9 copy.74
  227.4 1.8 convolution_bitcast_fusion
  229.2 109.7 %all-reduce.6.cloned.1.call-done = f32[128,153]{0,1:T(8,128)} async-done(((f32[128,153]{0,1:T(8,128)}), f32[128,153]{0,1:T(8,128)}) %all-reduce.6.cloned.1.call-update) | async-done | bytes 78352 | tf_op jit(solution)/shard_map/psum | solution.py:84
  338.9 217.4 %all-reduce.8.cloned.1.call-done = (f32[6,48,1024]{2,1,0:T(8,128)}, f32[6,64,153]{2,1,0:T(8,128)}) async-done(((f32[6,48,1024]{2,1,0:T(8,128)}, f32[6,64,153]{2,1,0:T(8,128)}), (f32[6,48,1024]{2,1,0:T(8,128)}, f32[6,64,153]{2,1,0:T(8,128)})) %all-reduce.8.cloned.1.call-update) | async-done | bytes 1414672 | tf_op jit(solution)/shard_map/psum | solution.py:104
  556.3 1.5 copy.141
  557.8 2.4 copy.142
  560.2 1.8 copy.143
  (29 shorter events, 0.2 us)
Async XLA Ops:
  7.2 47.2 %copy-start = (bf16[6,48,1024]{2,1,0:T(8,128)(2,1)S(1)}, bf16[6,48,1024]{2,1,0:T(8,128)(2,1)}, u32[]{:S(2)}) copy-start(bf16[6,48,1024]{2,1,0:T(8,128)(2,1)} %param.12) | copy-start | bytes 1769476
  7.2 152.7 %reduce-scatter.2.cloned.1.call-start = ((), (), s32[]{:S(2)}) async-start(), calls=%async_computation.1 | async-start | bytes 4456448 | tf_op jit(solution)/shard_map/reduce_scatter | solution.py:65
  57.6 5.8 %copy-start.6 = (s32[2]{0:T(128)S(1)}, s32[2]{0:T(128)}, u32[]{:S(2)}) copy-start(s32[2]{0:T(128)} %param.11) | copy-start | bytes 28
  57.6 10.7 %copy-start.5 = (s32[2]{0:T(128)S(1)}, s32[2]{0:T(128)}, u32[]{:S(2)}) copy-start(s32[2]{0:T(128)} %constant.2.clone.1) | copy-start | bytes 28
  57.6 10.9 %copy-start.2 = (bf16[128,153]{0,1:T(8,128)(2,1)S(1)}, bf16[128,153]{0,1:T(8,128)(2,1)}, u32[]{:S(2)}) copy-start(bf16[128,153]{0,1:T(8,128)(2,1)} %param.15) | copy-start | bytes 117508
  57.6 11.2 %copy-start.1 = (bf16[6,64,153]{2,1,0:T(8,128)(2,1)S(1)}, bf16[6,64,153]{2,1,0:T(8,128)(2,1)}, u32[]{:S(2)}) copy-start(bf16[6,64,153]{2,1,0:T(8,128)(2,1)} %param.14) | copy-start | bytes 352516
  57.6 11.5 %copy-start.3 = (s32[3]{0:T(128)S(1)}, s32[3]{0:T(128)}, u32[]{:S(2)}) copy-start(s32[3]{0:T(128)} %constant.186) | copy-start | bytes 40
  57.6 102.3 %copy-start.4 = (f32[64]{0:T(128)S(1)}, f32[64]{0:T(128)}, u32[]{:S(2)}) copy-start(f32[64]{0:T(128)} %param.13) | copy-start | bytes 772
  63.1 161.4 %all-gather.2.cloned.1.call-start = ((), (), s32[]{:S(2)}) async-start(), calls=%async_computation.3 | async-start | bytes 2228224 | tf_op jit(solution)/shard_map/all_gather | solution.py:101
  162.0 176.9 %all-reduce.6.cloned.1.call-start = ((), (), s32[]{:S(2)}) async-start(), calls=%async_computation.2 | async-start | bytes 163840 | tf_op jit(solution)/shard_map/psum | solution.py:84
  166.3 389.9 %all-reduce.8.cloned.1.call-start = ((), (), s32[]{:S(2)}) async-start(), calls=%async_computation.4 | async-start | bytes 3145728 | tf_op jit(solution)/shard_map/psum | solution.py:104
Sparse Core Ops, SparseCore 0:
  63.3 96.5 reduce-scatter.1
  163.9 60.5 all-gather.1
  228.7 110.2 all-reduce.5
  341.7 214.4 all-reduce.7
where the time goes:
time: 569 us
  waiting for transfers between devices  462 us (81%)
  local copies, waits for them, and re-layouts  38.4 us (7%)
  other arithmetic  36.6 us (6%)
  matrix products  17.5 us (3%)
  between operations  14 us (2%)
    psum x1, waiting for transfers between devices, local(): summed_first, summed_second = lax.psum((grad_first, grad_second), 'batch')  217 us
    psum x1, waiting for transfers between devices, local(): scores = lax.psum(partial_scores, 'feat')  110 us
    reduce_scatter x1, waiting for transfers between devices, local(): lax.psum_scatter(partial_sums, 'feat', scatter_dimension=1, tiled=True)  76.4 us
    all_gather x1, waiting for transfers between devices, local(): piece = lax.all_gather(flat_grad, 'feat', axis=1, tiled=True)  58.1 us
    reduce_sum x1, other arithmetic, node_masks(): degree = jnp.maximum(jnp.sum(adjacency, axis=3, dtype=jnp.float32), 1.0)  26.2 us
  transfers between devices with their start and end apart: 4, of which 4 were waited for; matrix products, arithmetic and copies ran while one was open for 5% of the time, Pallas kernels for 0%

commit v1 on v0

v1 whole, which is shorter than its diff:
```python
import jax
import jax.numpy as jnp
from jax import lax
from jax.experimental import pallas as pl
from jax.experimental.pallas import tpu as pltpu
from jax.sharding import PartitionSpec as P

BF16 = jnp.bfloat16
F32 = jnp.float32

GROUPS = 2
CAPACITY = 512
RELATIONS = 5
KINDS = RELATIONS + 1
SLOTS = 8
TARGETS = 64
CLASSES = 153
FEAT = 16
COLUMNS = 48
WIDTH = FEAT * COLUMNS
UNITS = 64
HIDDEN = FEAT * UNITS
PAIRS = KINDS // 2
NODES = GROUPS * CAPACITY
MESSAGE = NODES + KINDS * UNITS
Z = 16
CORES = 2
HALF = COLUMNS // CORES
FIRST_ROWS = PAIRS * HALF
SECOND_ROWS = 16
SHARD_ROWS = FIRST_ROWS + SECOND_ROWS
CLASS_ROWS = 160
VMEM_LIMIT = 56 * 1024 * 1024


def dot(a, b, contract):
    return lax.dot_general(a, b, ((contract[:1], contract[1:]), ((), ())), preferred_element_type=F32)


def eye(size):
    row = lax.broadcasted_iota(jnp.int32, (size, size), 0)
    column = lax.broadcasted_iota(jnp.int32, (size, size), 1)
    return (row == column).astype(F32).astype(BF16)


def swap_halves(tile):
    return pltpu.roll(tile, UNITS, 1)


def low_half(rows):
    return lax.broadcasted_iota(jnp.int32, (rows, 2 * UNITS), 1) < UNITS


def pack_kernel(x_ref, w_ref, out_ref):
    columns = dot(eye(COLUMNS), x_ref[...], (1, 1)).astype(BF16)
    for dest in range(FEAT):
        out_ref[dest, :, :NODES] = columns
    low = low_half(COLUMNS)
    for pair in range(PAIRS):
        for tile in range(FEAT // 2):
            lanes = pl.ds(tile * 2 * UNITS, 2 * UNITS)
            even = w_ref[2 * pair, :, lanes].astype(F32)
            odd = w_ref[2 * pair + 1, :, lanes].astype(F32)
            where = pl.ds(NODES + pair * 2 * UNITS, 2 * UNITS)
            out_ref[2 * tile, :, where] = jnp.where(low, even, swap_halves(odd)).astype(BF16)
            out_ref[2 * tile + 1, :, where] = jnp.where(low, swap_halves(even), odd).astype(BF16)


def layer_kernel(
    counts_ref,
    offsets_ref,
    core_ref,
    message_ref,
    slots_ref,
    bias_ref,
    weight_ref,
    upstream_ref,
    keep_ref,
    send_ref,
    score_ref,
    adj_ref,
    rows_ref,
    mixed_ref,
    low_ref,
    high_ref,
    value_ref,
    whole_ref,
    second_ref,
):
    first_weight = dot(eye(KINDS * UNITS), message_ref[:, NODES:], (1, 1)).astype(BF16)
    node = lax.broadcasted_iota(jnp.int32, (SLOTS, CAPACITY), 1)
    tile_row = lax.broadcasted_iota(jnp.int32, (16, CAPACITY), 0).astype(F32).astype(BF16)
    one = jnp.ones((16, CAPACITY), BF16)
    zero = jnp.zeros((16, CAPACITY), BF16)
    target = lax.broadcasted_iota(jnp.int32, (TARGETS, CAPACITY), 0)
    place = lax.broadcasted_iota(jnp.int32, (TARGETS, CAPACITY), 1)
    half = CAPACITY // 2
    for group in range(GROUPS):
        count = counts_ref[group]
        offset = offsets_ref[group]
        lanes = slice(group * CAPACITY, (group + 1) * CAPACITY)
        pick = (place == target + offset).astype(F32).astype(BF16)
        rows_ref[:TARGETS, :] = pick

        def relation_step(relation, carry, group=group, count=count, lanes=lanes, pick=pick):
            ids = slots_ref[group, relation]
            live = (ids >= 0) & (ids < count) & (node < count)
            inverse = 1.0 / jnp.maximum(jnp.sum(live.astype(F32), axis=0, keepdims=True), 1.0)
            for part in range(2):
                inside = live & (ids >= part * half) & (ids < (part + 1) * half)
                value = jnp.where(inside, ids - part * half, -1).astype(F32)
                for slot in range(SLOTS):
                    value_ref[part, slot] = jnp.broadcast_to(
                        value[slot : slot + 1, :], (16, CAPACITY)
                    ).astype(BF16)
            for part in range(2):

                def tile_step(step, carry, part=part):
                    base = step * 32
                    here = tile_row + base.astype(F32).astype(BF16)
                    there = here + jnp.full((), 16, BF16)
                    first = zero
                    second = zero
                    for slot in range(SLOTS):
                        value = value_ref[part, slot]
                        first = first + jnp.where(value == here, one, zero)
                        second = second + jnp.where(value == there, one, zero)
                    start = pl.multiple_of(part * half + base, 32)
                    adj_ref[pl.ds(start, 16), :] = first
                    adj_ref[pl.ds(start + 16, 16), :] = second
                    return carry

                lax.fori_loop(0, half // 32, tile_step, 0)
            adjacency = adj_ref[...]
            for block in range(3):
                size = WIDTH // 3
                mixed = dot(message_ref[block * size : (block + 1) * size, lanes], adjacency, (1, 0))
                start = pl.multiple_of(relation * WIDTH + block * size, size)
                mixed_ref[group, pl.ds(start, size), :] = (mixed * inverse).astype(BF16)
            start = pl.multiple_of((relation + 1) * TARGETS, TARGETS)
            rows_ref[pl.ds(start, TARGETS), :] = dot(pick, adjacency, (1, 1)).astype(BF16)
            return carry

        lax.fori_loop(0, RELATIONS, relation_step, 0)

        preact = bias_ref[...] + dot(first_weight[:UNITS], message_ref[:, lanes], (1, 0))
        for kind in range(1, KINDS):
            preact = preact + dot(
                first_weight[kind * UNITS : (kind + 1) * UNITS],
                mixed_ref[group, (kind - 1) * WIDTH : kind * WIDTH, :],
                (1, 0),
            )
        hidden = jnp.maximum(preact, 0.0).astype(BF16)
        rows = rows_ref[...]
        degree = jnp.maximum(jnp.sum(rows.astype(F32), axis=1, keepdims=True), 1.0)
        second_in = (dot(rows, hidden, (1, 1)) / degree).astype(BF16)
        upstream = upstream_ref[group * TARGETS : (group + 1) * TARGETS, :]
        scores = jnp.zeros((TARGETS, CLASSES), F32)
        returned = []
        for kind in range(KINDS):
            piece = slice(kind * TARGETS, (kind + 1) * TARGETS)
            scores = scores + dot(second_in[piece], weight_ref[kind], (1, 0))
            returned.append(dot(upstream, weight_ref[kind], (1, 1)))
        score_ref[group * TARGETS : (group + 1) * TARGETS, :] = scores
        spread = (jnp.concatenate(returned, axis=0) / degree).astype(BF16)
        wide = jnp.concatenate(
            [second_in[kind * TARGETS : (kind + 1) * TARGETS].astype(F32) for kind in range(KINDS)], axis=1
        ).astype(BF16)
        grad_second = dot(upstream, wide, (0, 0))
        if group == 0:
            second_ref[...] = grad_second
        else:
            second_ref[...] += grad_second
        hidden_grad = dot(spread, rows, (0, 0))
        pre_grad = jnp.where(preact > 0, hidden_grad, 0.0)
        nothing = jnp.zeros_like(pre_grad)
        low_ref[group] = jnp.concatenate([pre_grad, nothing], axis=0).astype(BF16)
        high_ref[group] = jnp.concatenate([nothing, pre_grad], axis=0).astype(BF16)

    for pair in range(PAIRS):
        total = jnp.zeros((WIDTH, 2 * UNITS), F32)
        for group in range(GROUPS):
            lanes = slice(group * CAPACITY, (group + 1) * CAPACITY)
            if pair == 0:
                even = message_ref[:, lanes]
            else:
                even = mixed_ref[group, (2 * pair - 1) * WIDTH : 2 * pair * WIDTH, :]
            odd = mixed_ref[group, 2 * pair * WIDTH : (2 * pair + 1) * WIDTH, :]
            total = total + dot(even, low_ref[group], (1, 1)) + dot(odd, high_ref[group], (1, 1))
        total = total.reshape(FEAT, COLUMNS, 2 * UNITS)
        for part in range(CORES):
            whole_ref[part, :, pair * HALF : (pair + 1) * HALF, :] = total[:, part * HALF : (part + 1) * HALF, :]
    tail = jnp.zeros((CLASS_ROWS - CLASSES, 2 * UNITS), F32)
    packed = []
    for pair in range(PAIRS):
        packed.append(second_ref[:, pair * 2 * UNITS : (pair + 1) * 2 * UNITS])
        packed.append(tail)
    packed.append(jnp.zeros((Z * CORES * SECOND_ROWS - PAIRS * CLASS_ROWS, 2 * UNITS), F32))
    packed = jnp.concatenate(packed, axis=0).reshape(Z, CORES, SECOND_ROWS, 2 * UNITS)
    for part in range(CORES):
        whole_ref[part, :, FIRST_ROWS:, :] = packed[:, part]
    core = core_ref[0]
    keep_ref[...] = whole_ref[core]
    send_ref[...] = whole_ref[1 - core]


def unpack_kernel(shards_ref, first_ref, second_ref):
    low = low_half(HALF)
    for tile in range(FEAT // 2):
        lanes = pl.ds(tile * 2 * UNITS, 2 * UNITS)
        for part in range(CORES):
            left = shards_ref[(2 * tile) * CORES + part].astype(F32)
            right = shards_ref[(2 * tile + 1) * CORES + part].astype(F32)
            rows = pl.ds(part * HALF, HALF)
            for pair in range(PAIRS):
                a = left[pair * HALF : (pair + 1) * HALF]
                b = right[pair * HALF : (pair + 1) * HALF]
                first_ref[2 * pair, rows, lanes] = jnp.where(low, a, swap_halves(b))
                first_ref[2 * pair + 1, rows, lanes] = jnp.where(low, swap_halves(a), b)
    packed = shards_ref[...].astype(F32)[:, FIRST_ROWS:, :].reshape(Z * CORES * SECOND_ROWS, 2 * UNITS)
    identity = eye(2 * UNITS)
    for pair in range(PAIRS):
        block = packed[pair * CLASS_ROWS : (pair + 1) * CLASS_ROWS].astype(BF16)
        turned = dot(identity, block, (1, 1))
        second_ref[2 * pair] = turned[:UNITS, :CLASSES]
        second_ref[2 * pair + 1] = turned[UNITS:, :CLASSES]


VMEM = pl.BlockSpec(memory_space=pltpu.VMEM)
SMEM = pl.BlockSpec(memory_space=pltpu.SMEM)
PARAMS = pltpu.CompilerParams(vmem_limit_bytes=VMEM_LIMIT)


def pack(x, w):
    return pl.pallas_call(
        pack_kernel,
        out_shape=jax.ShapeDtypeStruct((FEAT, COLUMNS, MESSAGE), BF16),
        in_specs=[VMEM, VMEM],
        out_specs=VMEM,
        compiler_params=PARAMS,
    )(x, w)


def layers(counts, offsets, core, message, slots, bias, weight, upstream):
    shard = jax.ShapeDtypeStruct((Z, SHARD_ROWS, 2 * UNITS), F32)
    return pl.pallas_call(
        layer_kernel,
        out_shape=(shard, shard, jax.ShapeDtypeStruct((GROUPS * TARGETS, CLASSES), F32)),
        in_specs=[SMEM, SMEM, SMEM, VMEM, VMEM, VMEM, VMEM, VMEM],
        out_specs=(VMEM, VMEM, VMEM),
        scratch_shapes=[
            pltpu.VMEM((CAPACITY, CAPACITY), BF16),
            pltpu.VMEM((KINDS * TARGETS, CAPACITY), BF16),
            pltpu.VMEM((GROUPS, RELATIONS * WIDTH, CAPACITY), BF16),
            pltpu.VMEM((GROUPS, 2 * UNITS, CAPACITY), BF16),
            pltpu.VMEM((GROUPS, 2 * UNITS, CAPACITY), BF16),
            pltpu.VMEM((2, SLOTS, 16, CAPACITY), BF16),
            pltpu.VMEM((CORES, Z, SHARD_ROWS, 2 * UNITS), F32),
            pltpu.VMEM((CLASSES, KINDS * UNITS), F32),
        ],
        compiler_params=PARAMS,
    )(counts, offsets, core, message, slots, bias, weight, upstream)


def unpack(shards):
    return pl.pallas_call(
        unpack_kernel,
        out_shape=(
            jax.ShapeDtypeStruct((KINDS, COLUMNS, HIDDEN), F32),
            jax.ShapeDtypeStruct((KINDS, UNITS, CLASSES), F32),
        ),
        in_specs=[VMEM],
        out_specs=(VMEM, VMEM),
        compiler_params=PARAMS,
    )(shards)


def local(
    vertex_embeddings,
    adjacent_vertices,
    node_counts,
    target_offsets,
    weight_one,
    bias_one,
    weight_two,
    score_derivative,
):
    batch = lax.axis_index("batch")
    core = (batch % CORES).astype(jnp.int32).reshape(1)
    slots = jnp.swapaxes(adjacent_vertices, 2, 3)
    message = lax.all_to_all(pack(vertex_embeddings, weight_one), "feat", 0, 0)
    message = message.reshape(WIDTH, MESSAGE)
    keep, send, partial_scores = layers(
        node_counts,
        target_offsets,
        core,
        message,
        slots,
        bias_one.reshape(UNITS, 1),
        weight_two,
        score_derivative,
    )
    scores = jnp.sum(lax.all_gather(partial_scores, "feat"), axis=0)
    received = lax.ppermute(send, "batch", [(i, i ^ 1) for i in range(Z * CORES)])
    chip = keep + received
    first = lax.all_to_all(chip[:, :FIRST_ROWS].astype(BF16), "feat", 0, 0)
    shards = jnp.concatenate([first, chip[:, FIRST_ROWS:].astype(BF16)], axis=1)
    same_core = [[z * CORES + c for z in range(Z)] for c in range(CORES)]
    pieces = lax.all_to_all(shards, "batch", 0, 0, axis_index_groups=same_core)
    shard = jnp.sum(pieces.astype(F32), axis=0).astype(BF16)
    first_grad, second_grad = unpack(lax.all_gather(shard, "batch"))
    return (scores, first_grad, second_grad)


def solution(mesh):
    placed = (
        P("batch", "feat"),
        P("batch", None, None, None),
        P("batch"),
        P("batch"),
        P(None, "feat", None),
        P("feat"),
        P(None, "feat", None),
        P("batch", None),
    )
    return jax.shard_map(
        local,
        mesh=mesh,
        in_specs=placed,
        out_specs=(P("batch", None), P(None, "feat", None), P(None, "feat", None)),
        check_vma=False,
    )
```

time: 569 us -> 179 us (0.31)
  waiting for transfers between devices: 462 us -> 35.1 us
  blocking collectives: 0 us -> 73.1 us
  other arithmetic: 36.6 us -> 3.01 us
  local copies, waits for them, and re-layouts: 38.4 us -> 6.02 us
  Pallas kernels: 0 us -> 27.7 us
  starting transfers between devices: 0.34 us -> 19.2 us
  matrix products: 17.5 us -> 0 us
    psum x2 -> x0, waiting for transfers between devices: 327 us -> none  [the longest x1 217 us: local(): summed_first, summed_second = lax.psum((grad_first, grad_second), 'batch')]
    reduce_scatter x1 -> x0, waiting for transfers between devices: 76.4 us -> none  [local(): lax.psum_scatter(partial_sums, 'feat', scatter_dimension=1, tiled=True)]
    all_gather x1, waiting for transfers between devices: 58.1 us -> 0.01 us  [local(): scores = jnp.sum(lax.all_gather(partial_scores, 'feat'), axis=0)]
    all_gather x0 -> x1, blocking collectives: none -> 41.5 us  [local(): first_grad, second_grad = unpack(lax.all_gather(shard, 'batch'))]
    all_to_all x0 -> x2, waiting for transfers between devices: none -> 33.1 us  [the longest x1 24.4 us: local(): message = lax.all_to_all(pack(vertex_embeddings, weight_one), 'feat', 0, 0)]
    all_to_all x0 -> x1, blocking collectives: none -> 31.6 us  [local(): pieces = lax.all_to_all(shards, 'batch', 0, 0, axis_index_groups=same_core)]
    pallas_call x0 -> x3, Pallas kernels: none -> 27.7 us  [the longest x1 22.3 us: layers(): pl.pallas_call(layer_kernel, out_shape=(shard, shard, jax.ShapeDtypeStruc...]
    reduce_sum x1 -> x2, other arithmetic: 26.2 us -> 1.8 us  [the longest x1 1.74 us: local(): scores = jnp.sum(lax.all_gather(partial_scores, 'feat'), axis=0)]
  transfers between devices with their start and end apart: 4 -> 4, of which waited for: 4 -> 3; matrix products, arithmetic and copies ran while one was open for 5% -> 2% of each run, Pallas kernels for 0% -> 1%
where the time goes in v1:
time: 179 us; the launch traced here: 178 us
  blocking collectives  73.1 us (41%)
  waiting for transfers between devices  35.1 us (20%)
  Pallas kernels  27.7 us (15%)
  starting transfers between devices  19.2 us (11%)
  between operations  14.1 us (8%)
  local copies, waits for them, and re-layouts  6.02 us (3%)
  other arithmetic  3.01 us (2%)
    all_gather x1, blocking collectives, local(): first_grad, second_grad = unpack(lax.all_gather(shard, 'batch'))  41.5 us
    all_to_all x1, blocking collectives, local(): pieces = lax.all_to_all(shards, 'batch', 0, 0, axis_index_groups=same_core)  31.6 us
    all_to_all x1, waiting for transfers between devices, local(): message = lax.all_to_all(pack(vertex_embeddings, weight_one), 'feat', 0, 0)  24.4 us
    pallas_call x1, Pallas kernels, layers(): pl.pallas_call(layer_kernel, out_shape=(shard, shard, jax.ShapeDtypeStruc...  22.3 us
    all_to_all x1, waiting for transfers between devices, local(): first = lax.all_to_all(chip[:, :FIRST_ROWS].astype(BF16), 'feat', 0, 0)  8.73 us
    ppermute x1, starting transfers between devices, local(): lax.ppermute(send, 'batch', [(i, i ^ 1) for i in range(Z * CORES)])  7.89 us
    all_to_all x1, starting transfers between devices, local(): message = lax.all_to_all(pack(vertex_embeddings, weight_one), 'feat', 0, 0)  7.72 us
    unnamed x9, local copies, waits for them, and re-layouts  4.57 us
  transfers between devices with their start and end apart: 4, of which 3 were waited for; matrix products, arithmetic and copies ran while one was open for 2% of the time, Pallas kernels for 1%

profile of v1, /device:TPU:1, one launch (start us, length us, event | category | flops | bytes accessed | tf_op | source)
XLA Modules:
  0.0 178.2 jit_solution(4326402777956936861)
XLA Ops:
  7.2 1.7 copy.14.x_ref
  8.9 2.9 %shard_map.103 = bf16[16,48,1408]{2,1,0:T(8,128)(2,1)} custom-call(bf16[1024,48]{1,0:T(8,128)(2,1)} %copy.14.x_ref, bf16[6,48,1024]{2,1,0:T(8,128)(2,1)} %w_ref.1), custom_call_target="tpu_custom_call" | custom-call | tf_op jit(solution)/shard_map/pallas_call | solution.py:235
  11.7 0.0 copy-start.1
  11.8 0.0 copy-start.2
  11.8 7.7 %all-to-all-start = ((bf16[16,48,1408]{2,1,0:T(8,128)(2,1)}), bf16[16,48,1408]{2,1,0:T(8,128)(2,1)S(1)}, u32[]{:S(2)}, u32[]{:S(2)}) async-start(bf16[16,48,1408]{2,1,0:T(8,128)(2,1)} %shard_map.103), calls=%async_computation | async-start | bytes 4325376 | tf_op jit(solution)/shard_map/all_to_all | solution.py:291
  19.5 0.0 all-gather.4.cloned.1.call-start
  19.5 0.0 copy-done.1
  19.5 0.7 copy.16.upstream_ref
  20.3 0.0 copy-done.2
  20.3 0.7 copy.15.bias_ref
  21.0 24.4 %all-to-all-done = bf16[16,48,1408]{2,1,0:T(8,128)(2,1)S(1)} async-done(((bf16[16,48,1408]{2,1,0:T(8,128)(2,1)}), bf16[16,48,1408]{2,1,0:T(8,128)(2,1)S(1)}, u32[]{:S(2)}, u32[]{:S(2)}) %all-to-all-start) | async-done | bytes 2162720 | tf_op jit(solution)/shard_map/all_to_all | solution.py:291
  45.4 0.0 copy-start
  45.4 1.3 copy-done
  46.7 22.3 %shard_map.104 = (f32[16,88,128]{2,1,0:T(8,128)}, f32[16,88,128]{2,1,0:T(8,128)}, f32[128,153]{1,0:T(8,128)}) custom-call(s32[2]{0:T(128)} %counts_ref.1, s32[2]{0:T(128)} %offsets_ref.1, s32[1]{0:T(128)} %bitcast.core_ref, bf16[768,1408]{1,0:T(8,128)(2,1)} %bitcast.6, s32[2,5,8,512]{3,2,1,0:T(8,128)} %bitcast.9, f32[64,1]{1,0:T(8,128)} %copy.15.bias_ref, ...), custom_call_target="tpu_custom_call" | custom-call | tf_op jit(solution)/shard_map/pallas_call | solution.py:246
  69.0 7.9 %collective-permute-start = (f32[16,88,128]{2,1,0:T(8,128)}, f32[16,88,128]{2,1,0:T(8,128)S(1)}, u32[]{:S(2)}, u32[]{:S(2)}) collective-permute-start(f32[16,88,128]{2,1,0:T(8,128)} %get-tuple-element.10), channel_id=1, source_target_pairs={{0,16},{16,0},{32,48},{48,32},{64,80},{80,64},{96,112},{112,96},{1... | collective-permute-start | bytes 2162696 | tf_op jit(solution)/shard_map/ppermute | solution.py:304
  76.9 0.0 all-gather.4.cloned.1.call-update
  76.9 2.0 %collective-permute-done = f32[16,88,128]{2,1,0:T(8,128)S(1)} collective-permute-done((f32[16,88,128]{2,1,0:T(8,128)}, f32[16,88,128]{2,1,0:T(8,128)S(1)}, u32[]{:S(2)}, u32[]{:S(2)}) %collective-permute-start) | collective-permute-done | bytes 720928 | tf_op jit(solution)/shard_map/ppermute | solution.py:304
  78.9 1.2 add_convert_fusion
  80.1 0.7 slice.10
  80.9 3.5 %all-to-all-start.1 = ((bf16[16,72,128]{2,1,0:T(8,128)(2,1)}), bf16[16,72,128]{2,1,0:T(8,128)(2,1)S(1)}, u32[]{:S(2)}, u32[]{:S(2)}) async-start(bf16[16,72,128]{2,1,0:T(8,128)(2,1)} %slice.10), calls=%async_computation.1 | async-start | bytes 589824 | tf_op jit(solution)/shard_map/all_to_all | solution.py:306
  84.4 8.7 %all-to-all-done.1 = bf16[16,72,128]{2,1,0:T(8,128)(2,1)S(1)} async-done(((bf16[16,72,128]{2,1,0:T(8,128)(2,1)}), bf16[16,72,128]{2,1,0:T(8,128)(2,1)S(1)}, u32[]{:S(2)}, u32[]{:S(2)}) %all-to-all-start.1) | async-done | bytes 294944 | tf_op jit(solution)/shard_map/all_to_all | solution.py:306
  93.2 31.6 %all_to_all.15 = bf16[16,88,128]{2,1,0:T(8,128)(2,1)S(1)} all-to-all(bf16[16,88,128]{2,1,0:T(8,128)(2,1)S(1)} %pad_maximum_fusion), channel_id=1, replica_groups={{0,32,64,96,128,160,192,224,256,288,320,352,384,416,448,480},{16,48,80,..., dimensions={0} | all-to-all | bytes 720896 | tf_op jit(solution)/shard_map/all_to_all | solution.py:309
  124.8 0.1 reduce_sum.22
  124.8 41.5 %all-gather.1 = bf16[2816,128]{1,0:T(8,128)(2,1)} all-gather(bf16[88,128]{1,0:T(8,128)(2,1)S(1)} %reduce_sum.22), channel_id=3, replica_groups=mesh['batch'=32,'feat'=16] {'batch'}, dimensions={0}, use_global_device_ids=true | all-gather | bytes 743424 | tf_op jit(solution)/shard_map/all_gather | solution.py:311
  166.3 2.5 %shard_map.105 = (f32[6,48,1024]{2,1,0:T(8,128)}, f32[6,64,153]{2,1,0:T(8,128)}) custom-call(bf16[32,88,128]{2,1,0:T(8,128)(2,1)} %bitcast.7), custom_call_target="tpu_custom_call" | custom-call | tf_op jit(solution)/shard_map/pallas_call | solution.py:266
  168.9 0.0 all-gather.4.cloned.1.call-done
  168.9 1.7 reduce_sum.21
  170.6 0.7 copy.17
  (2 shorter events, 0.0 us)
Async XLA Ops:
  11.7 7.8 %copy-start.1 = (bf16[128,153]{0,1:T(8,128)(2,1)S(1)}, bf16[128,153]{0,1:T(8,128)(2,1)}, u32[]{:S(2)}) copy-start(bf16[128,153]{0,1:T(8,128)(2,1)} %param.15) | copy-start | bytes 117508
  11.8 8.5 %copy-start.2 = (f32[64]{0:T(128)S(1)}, f32[64]{0:T(128)}, u32[]{:S(2)}) copy-start(f32[64]{0:T(128)} %param.13) | copy-start | bytes 772
  11.8 33.6 %all-to-all-start = ((bf16[16,48,1408]{2,1,0:T(8,128)(2,1)}), bf16[16,48,1408]{2,1,0:T(8,128)(2,1)S(1)}, u32[]{:S(2)}, u32[]{:S(2)}) async-start(bf16[16,48,1408]{2,1,0:T(8,128)(2,1)} %shard_map.103), calls=%async_computation | async-start | bytes 4325376 | tf_op jit(solution)/shard_map/all_to_all | solution.py:291
  19.5 149.4 %all-gather.4.cloned.1.call-start = ((), (), s32[]{:S(2)}) async-start(), calls=%async_computation.3 | async-start | bytes 2228224 | tf_op jit(solution)/shard_map/all_gather | solution.py:303
  45.4 1.3 copy-start
  69.0 9.9 %collective-permute-start = (f32[16,88,128]{2,1,0:T(8,128)}, f32[16,88,128]{2,1,0:T(8,128)S(1)}, u32[]{:S(2)}, u32[]{:S(2)}) collective-permute-start(f32[16,88,128]{2,1,0:T(8,128)} %get-tuple-element.10), channel_id=1, source_target_pairs={{0,16},{16,0},{32,48},{48,32},{64,80},{80,64},{96,112},{112,96},{1... | collective-permute-start | bytes 2162696 | tf_op jit(solution)/shard_map/ppermute | solution.py:304
  80.9 12.3 %all-to-all-start.1 = ((bf16[16,72,128]{2,1,0:T(8,128)(2,1)}), bf16[16,72,128]{2,1,0:T(8,128)(2,1)S(1)}, u32[]{:S(2)}, u32[]{:S(2)}) async-start(bf16[16,72,128]{2,1,0:T(8,128)(2,1)} %slice.10), calls=%async_computation.1 | async-start | bytes 589824 | tf_op jit(solution)/shard_map/all_to_all | solution.py:306
Sparse Core Ops, SparseCore 0:
  77.1 61.6 all-gather.3

commit v2 on v1

v2 whole, which is shorter than its diff:
```python
import jax
import jax.numpy as jnp
from jax import lax
from jax.experimental import pallas as pl
from jax.experimental.pallas import tpu as pltpu
from jax.sharding import PartitionSpec as P

BF16 = jnp.bfloat16
F32 = jnp.float32

GROUPS = 2
CAPACITY = 512
RELATIONS = 5
KINDS = RELATIONS + 1
SLOTS = 8
TARGETS = 64
CLASSES = 153
FEAT = 16
COLUMNS = 48
WIDTH = FEAT * COLUMNS
UNITS = 64
HIDDEN = FEAT * UNITS
PAIRS = KINDS // 2
NODES = GROUPS * CAPACITY
WEIGHT_LANES = 256
MESSAGE = NODES + WEIGHT_LANES
Z = 16
CORES = 2
HALF = COLUMNS // CORES
FIRST_ROWS = PAIRS * HALF
SECOND_ROWS = 16
SHARD_ROWS = SECOND_ROWS + FIRST_ROWS
CLASS_ROWS = 160
SIDE = 4
CLASS_PART = CLASS_ROWS // SIDE
SCORE_ROWS = 48
ADJ_ROWS = RELATIONS * CAPACITY
ROWS = KINDS * TARGETS
MIB = 1024 * 1024


def dot(a, b, contract):
    return lax.dot_general(a, b, ((contract[:1], contract[1:]), ((), ())), preferred_element_type=F32)


def eye(size):
    row = lax.broadcasted_iota(jnp.int32, (size, size), 0)
    column = lax.broadcasted_iota(jnp.int32, (size, size), 1)
    return (row == column).astype(F32).astype(BF16)


def swap_halves(tile):
    return pltpu.roll(tile, UNITS, 1)


def low_half(rows):
    return lax.broadcasted_iota(jnp.int32, (rows, 2 * UNITS), 1) < UNITS


def pack_kernel(core_ref, x_ref, w_ref, out_ref):
    columns = x_ref[...]
    for dest in range(FEAT):
        out_ref[dest, :, :NODES] = columns
    low = low_half(COLUMNS)
    core = core_ref[0]
    for tile in range(FEAT // 2):
        lanes = pl.ds(tile * 2 * UNITS, 2 * UNITS)
        first, second, third = [w_ref[2 * pair + core, :, lanes].astype(F32) for pair in range(PAIRS)]
        front = pl.ds(NODES, 2 * UNITS)
        back = pl.ds(NODES + 2 * UNITS, 2 * UNITS)
        out_ref[2 * tile, :, front] = jnp.where(low, first, swap_halves(second)).astype(BF16)
        out_ref[2 * tile, :, back] = third.astype(BF16)
        out_ref[2 * tile + 1, :, front] = jnp.where(low, swap_halves(first), second).astype(BF16)
        out_ref[2 * tile + 1, :, back] = swap_halves(third).astype(BF16)


def live_slots(ids, count):
    node = lax.broadcasted_iota(jnp.int32, (SLOTS, CAPACITY), 1)
    return (ids >= 0) & (ids < count) & (node < count)


def adjacency_kernel(counts_ref, offsets_ref, slots_ref, adj_ref, value_ref):
    tile_row = lax.broadcasted_iota(jnp.int32, (16, CAPACITY), 0).astype(F32).astype(BF16)
    one = jnp.ones((16, CAPACITY), BF16)
    zero = jnp.zeros((16, CAPACITY), BF16)
    target = lax.broadcasted_iota(jnp.int32, (TARGETS, CAPACITY), 0)
    place = lax.broadcasted_iota(jnp.int32, (TARGETS, CAPACITY), 1)
    half = CAPACITY // 2
    for group in range(GROUPS):
        count = counts_ref[group]
        pick = (place == target + offsets_ref[group]).astype(F32).astype(BF16)
        adj_ref[group, ADJ_ROWS : ADJ_ROWS + TARGETS, :] = pick

        def relation_step(relation, carry, group=group, count=count, pick=pick):
            ids = slots_ref[group, relation]
            live = live_slots(ids, count)
            origin = pl.multiple_of(relation * CAPACITY, CAPACITY)
            for part in range(2):
                inside = live & (ids >= part * half) & (ids < (part + 1) * half)
                value = jnp.where(inside, ids - part * half, -1).astype(F32)
                for slot in range(SLOTS):
                    value_ref[part, slot] = jnp.broadcast_to(
                        value[slot : slot + 1, :], (16, CAPACITY)
                    ).astype(BF16)
            for part in range(2):

                def tile_step(step, carry, part=part):
                    base = step * 32
                    here = tile_row + base.astype(F32).astype(BF16)
                    there = here + jnp.full((), 16, BF16)
                    first = zero
                    second = zero
                    for slot in range(SLOTS):
                        value = value_ref[part, slot]
                        first = first + jnp.where(value == here, one, zero)
                        second = second + jnp.where(value == there, one, zero)
                    start = pl.multiple_of(origin + part * half + base, 32)
                    adj_ref[group, pl.ds(start, 16), :] = first
                    adj_ref[group, pl.ds(start + 16, 16), :] = second
                    return carry

                lax.fori_loop(0, half // 32, tile_step, 0)
            start = pl.multiple_of(ADJ_ROWS + (relation + 1) * TARGETS, TARGETS)
            adj_ref[group, pl.ds(start, TARGETS), :] = dot(
                pick, adj_ref[group, pl.ds(origin, CAPACITY), :], (1, 1)
            ).astype(BF16)
            return carry

        lax.fori_loop(0, RELATIONS, relation_step, 0)


def layer_kernel(
    core_ref,
    counts_ref,
    message_ref,
    first_ref,
    slots_ref,
    bias_ref,
    weight_ref,
    upstream_ref,
    adj_from,
    keep_ref,
    send_ref,
    score_ref,
    adj_ref,
    adj_sem,
    mixed_ref,
    low_ref,
    high_ref,
    whole_ref,
    second_ref,
):
    def fetch(group, relation):
        rows = pl.ds(pl.multiple_of(relation * CAPACITY, CAPACITY), CAPACITY)
        return pltpu.make_async_copy(
            adj_from.at[group, rows], adj_ref.at[group, rows], adj_sem.at[group, relation]
        )

    def fetch_rows(group):
        rows = pl.ds(ADJ_ROWS, ROWS)
        return pltpu.make_async_copy(
            adj_from.at[group, rows], adj_ref.at[group, rows], adj_sem.at[group, RELATIONS]
        )

    for group in range(GROUPS):
        for relation in range(RELATIONS):
            fetch(group, relation).start()
        fetch_rows(group).start()
    turn = eye(WEIGHT_LANES)
    first_weight = [dot(turn, first_ref[part], (1, 1)).astype(BF16) for part in range(CORES)]
    size = WIDTH // 3
    score_parts = []
    for group in range(GROUPS):
        lanes = slice(group * CAPACITY, (group + 1) * CAPACITY)

        count = counts_ref[group]

        def relation_step(relation, carry, group=group, lanes=lanes, count=count):
            fetch(group, relation).wait()
            rows = pl.ds(pl.multiple_of(relation * CAPACITY, CAPACITY), CAPACITY)
            adjacency = adj_ref[group, rows, :]
            live = live_slots(slots_ref[group, relation], count)
            inverse = 1.0 / jnp.maximum(jnp.sum(live.astype(F32), axis=0, keepdims=True), 1.0)
            for block in range(3):
                mixed = dot(message_ref[block * size : (block + 1) * size, lanes], adjacency, (1, 0))
                start = pl.multiple_of(relation * WIDTH + block * size, size)
                mixed_ref[group, pl.ds(start, size), :] = (mixed * inverse).astype(BF16)
            return carry

        lax.fori_loop(0, RELATIONS, relation_step, 0)

        preact = bias_ref[...] + dot(first_weight[0][:UNITS], message_ref[:, lanes], (1, 0))
        for kind in range(1, KINDS):
            preact = preact + dot(
                first_weight[kind % CORES][kind // CORES * UNITS : (kind // CORES + 1) * UNITS],
                mixed_ref[group, (kind - 1) * WIDTH : kind * WIDTH, :],
                (1, 0),
            )
        hidden = jnp.maximum(preact, 0.0).astype(BF16)
        fetch_rows(group).wait()
        rows = adj_ref[group, ADJ_ROWS:, :]
        degree = jnp.maximum(jnp.sum(rows.astype(F32), axis=1, keepdims=True), 1.0)
        second_in = (dot(rows, hidden, (1, 1)) / degree).astype(BF16)
        upstream = upstream_ref[group * TARGETS : (group + 1) * TARGETS, :]
        returned = []
        for kind in range(KINDS):
            returned.append(dot(upstream, weight_ref[kind * UNITS : (kind + 1) * UNITS, :], (1, 1)))
        spread = (jnp.concatenate(returned, axis=0) / degree).astype(BF16)
        wide = jnp.concatenate(
            [second_in[kind * TARGETS : (kind + 1) * TARGETS].astype(F32) for kind in range(KINDS)], axis=1
        ).astype(BF16)
        score_parts.append(dot(weight_ref[...], wide, (0, 1)))
        grad_second = dot(upstream, wide, (0, 0))
        if group == 0:
            second_ref[...] = grad_second
        else:
            second_ref[...] += grad_second
        hidden_grad = dot(spread, rows, (0, 0))
        pre_grad = jnp.where(preact > 0, hidden_grad, 0.0)
        nothing = jnp.zeros_like(pre_grad)
        low_ref[group] = jnp.concatenate([pre_grad, nothing], axis=0).astype(BF16)
        high_ref[group] = jnp.concatenate([nothing, pre_grad], axis=0).astype(BF16)

    tail = jnp.zeros((CLASS_ROWS - CLASSES, 2 * UNITS), F32)
    score = jnp.concatenate([jnp.concatenate(score_parts, axis=1), tail], axis=0)
    for part in range(SIDE):
        piece = score[part * CLASS_PART : (part + 1) * CLASS_PART]
        piece = jnp.concatenate([piece, jnp.zeros((SCORE_ROWS - CLASS_PART, 2 * UNITS), F32)], axis=0)
        score_ref[part] = piece.astype(BF16)
    for pair in range(PAIRS):
        total = jnp.zeros((WIDTH, 2 * UNITS), F32)
        for group in range(GROUPS):
            lanes = slice(group * CAPACITY, (group + 1) * CAPACITY)
            if pair == 0:
                even = message_ref[:, lanes]
            else:
                even = mixed_ref[group, (2 * pair - 1) * WIDTH : 2 * pair * WIDTH, :]
            odd = mixed_ref[group, 2 * pair * WIDTH : (2 * pair + 1) * WIDTH, :]
            total = total + dot(even, low_ref[group], (1, 1)) + dot(odd, high_ref[group], (1, 1))
        total = total.reshape(FEAT, COLUMNS, 2 * UNITS)
        start = SECOND_ROWS + pair * HALF
        for part in range(CORES):
            whole_ref[part, :, start : start + HALF, :] = total[:, part * HALF : (part + 1) * HALF, :]
    packed = []
    for pair in range(PAIRS):
        packed.append(second_ref[:, pair * 2 * UNITS : (pair + 1) * 2 * UNITS])
        packed.append(tail)
    packed.append(jnp.zeros((Z * CORES * SECOND_ROWS - PAIRS * CLASS_ROWS, 2 * UNITS), F32))
    packed = jnp.concatenate(packed, axis=0).reshape(Z, CORES, SECOND_ROWS, 2 * UNITS)
    for part in range(CORES):
        whole_ref[part, :, :SECOND_ROWS, :] = packed[:, part]
    core = core_ref[0]
    keep_ref[...] = whole_ref[core]
    send_ref[...] = whole_ref[1 - core]


def merge_kernel(keep_ref, received_ref, score_ref, message_ref, second_ref):
    chip = keep_ref[...] + received_ref[...]
    message_ref[:, SCORE_ROWS:, :] = chip[:, SECOND_ROWS:, :].astype(BF16)
    for part in range(FEAT):
        message_ref[part, :SCORE_ROWS, :] = score_ref[part % SIDE]
    second_ref[...] = chip[:, :SECOND_ROWS, :].astype(BF16)


def relay_kernel(message_ref, second_ref, shards_ref):
    shards_ref[:, SECOND_ROWS:, :] = message_ref[:, SCORE_ROWS:, :]
    shards_ref[:, :SECOND_ROWS, :] = second_ref[...]


def score_kernel(message_ref, score_ref):
    total = message_ref[0, :SCORE_ROWS, :].astype(F32)
    for part in range(1, FEAT):
        total = total + message_ref[part, :SCORE_ROWS, :].astype(F32)
    score_ref[...] = total[:CLASS_PART]


def unpack_kernel(place_ref, shards_ref, s0_ref, s1_ref, s2_ref, s3_ref, first_ref, second_ref, logits_ref, scores_ref):
    low = low_half(HALF)
    for tile in range(FEAT // 2):
        lanes = pl.ds(tile * 2 * UNITS, 2 * UNITS)
        for part in range(CORES):
            left = shards_ref[(2 * tile) * CORES + part].astype(F32)
            right = shards_ref[(2 * tile + 1) * CORES + part].astype(F32)
            rows = pl.ds(part * HALF, HALF)
            for pair in range(PAIRS):
                start = SECOND_ROWS + pair * HALF
                a = left[start : start + HALF]
                b = right[start : start + HALF]
                first_ref[2 * pair, rows, lanes] = jnp.where(low, a, swap_halves(b))
                first_ref[2 * pair + 1, rows, lanes] = jnp.where(low, swap_halves(a), b)
    packed = shards_ref[:, :SECOND_ROWS, :].reshape(Z * CORES * SECOND_ROWS, 2 * UNITS)
    identity = eye(2 * UNITS)
    for pair in range(PAIRS):
        block = packed[pair * CLASS_ROWS : (pair + 1) * CLASS_ROWS]
        turned = dot(identity, block, (1, 1))
        second_ref[2 * pair] = turned[:UNITS, :CLASSES]
        second_ref[2 * pair + 1] = turned[UNITS:, :CLASSES]
    for step, ref in enumerate((s0_ref, s1_ref, s2_ref, s3_ref)):
        part = (place_ref[0] + SIDE - step) % SIDE
        scores_ref[pl.ds(pl.multiple_of(part * CLASS_PART, 8), CLASS_PART), :] = ref[...]
    logits_ref[...] = scores_ref[:CLASSES, :]


VMEM = pl.BlockSpec(memory_space=pltpu.VMEM)
SMEM = pl.BlockSpec(memory_space=pltpu.SMEM)


def params(mib):
    return pltpu.CompilerParams(vmem_limit_bytes=mib * MIB)


def cost(flops, size):
    return pl.CostEstimate(flops=flops, bytes_accessed=size, transcendentals=0)


def shape(*dims, dtype=BF16):
    return jax.ShapeDtypeStruct(dims, dtype)


def pack(core, x, w):
    return pl.pallas_call(
        pack_kernel,
        out_shape=shape(FEAT, COLUMNS, MESSAGE),
        in_specs=[SMEM, VMEM, VMEM],
        out_specs=VMEM,
        compiler_params=params(58),
    )(core, x, w)


def adjacency(counts, offsets, slots):
    return pl.pallas_call(
        adjacency_kernel,
        out_shape=shape(GROUPS, ADJ_ROWS + ROWS, CAPACITY),
        in_specs=[SMEM, SMEM, VMEM],
        out_specs=VMEM,
        scratch_shapes=[pltpu.VMEM((2, SLOTS, 16, CAPACITY), BF16)],
        compiler_params=params(58),
        cost_estimate=cost(8 * 10**9, 8 * MIB),
    )(counts, offsets, slots)


def layers(core, counts, message, first, slots, bias, weight, upstream, adj):
    shard = shape(Z, SHARD_ROWS, 2 * UNITS, dtype=F32)
    return pl.pallas_call(
        layer_kernel,
        out_shape=(shard, shard, shape(SIDE, SCORE_ROWS, 2 * UNITS)),
        in_specs=[SMEM] * 2 + [VMEM] * 6 + [pl.BlockSpec(memory_space=pl.ANY)],
        out_specs=(VMEM, VMEM, VMEM),
        scratch_shapes=[
            pltpu.VMEM(adj.shape, BF16),
            pltpu.SemaphoreType.DMA((GROUPS, KINDS)),
            pltpu.VMEM((GROUPS, RELATIONS * WIDTH, CAPACITY), BF16),
            pltpu.VMEM((GROUPS, 2 * UNITS, CAPACITY), BF16),
            pltpu.VMEM((GROUPS, 2 * UNITS, CAPACITY), BF16),
            pltpu.VMEM((CORES, Z, SHARD_ROWS, 2 * UNITS), F32),
            pltpu.VMEM((CLASSES, KINDS * UNITS), F32),
        ],
        compiler_params=params(44),
        cost_estimate=cost(12 * 10**9, 12 * MIB),
    )(core, counts, message, first, slots, bias, weight, upstream, adj)


def merge(keep, received, score):
    return pl.pallas_call(
        merge_kernel,
        out_shape=(shape(FEAT, SCORE_ROWS + FIRST_ROWS, 2 * UNITS), shape(Z, SECOND_ROWS, 2 * UNITS)),
        in_specs=[VMEM] * 3,
        out_specs=(VMEM, VMEM),
        compiler_params=params(8),
    )(keep, received, score)


def relay(message, second):
    return pl.pallas_call(
        relay_kernel,
        out_shape=shape(Z, SHARD_ROWS, 2 * UNITS),
        in_specs=[VMEM] * 2,
        out_specs=VMEM,
        compiler_params=params(8),
    )(message, second)


def add_scores(message):
    return pl.pallas_call(
        score_kernel,
        out_shape=shape(CLASS_PART, 2 * UNITS, dtype=F32),
        in_specs=[VMEM],
        out_specs=VMEM,
        compiler_params=params(8),
        cost_estimate=cost(2 * 10**9, 2 * MIB),
    )(message)


def gather_scores(score):
    parts = [score]
    for step in range(1, SIDE):
        hops = [(i, i // SIDE * SIDE + (i + step) % SIDE) for i in range(FEAT)]
        parts.append(lax.ppermute(score, "feat", hops))
    return parts


def unpack(place, shards, blocks):
    return pl.pallas_call(
        unpack_kernel,
        out_shape=(
            shape(KINDS, COLUMNS, HIDDEN, dtype=F32),
            shape(KINDS, UNITS, CLASSES, dtype=F32),
            shape(CLASSES, GROUPS * TARGETS, dtype=F32),
        ),
        in_specs=[SMEM] + [VMEM] * 5,
        out_specs=(VMEM, VMEM, VMEM),
        scratch_shapes=[pltpu.VMEM((CLASS_ROWS, 2 * UNITS), F32)],
        compiler_params=params(8),
    )(place, shards, *blocks)


def local(
    vertex_embeddings,
    adjacent_vertices,
    node_counts,
    target_offsets,
    weight_one,
    bias_one,
    weight_two,
    score_derivative,
):
    core = (lax.axis_index("batch") % CORES).astype(jnp.int32).reshape(1)
    place = (lax.axis_index("feat") % SIDE).astype(jnp.int32).reshape(1)
    chips = [[z * CORES + c for c in range(CORES)] for z in range(Z)]
    same_core = [[z * CORES + c for z in range(Z)] for c in range(CORES)]
    message = lax.all_to_all(pack(core, vertex_embeddings.T, weight_one), "feat", 0, 0)
    message = message.reshape(WIDTH, MESSAGE)
    first = lax.all_gather(message[:, NODES:], "batch", axis_index_groups=chips)
    slots = jnp.swapaxes(adjacent_vertices, 2, 3)
    adj = adjacency(node_counts, target_offsets, slots)
    keep, send, score = layers(
        core,
        node_counts,
        message,
        first,
        slots,
        bias_one.reshape(UNITS, 1),
        weight_two.reshape(KINDS * UNITS, CLASSES),
        score_derivative,
        adj,
    )
    received = lax.ppermute(send, "batch", [(i, i ^ 1) for i in range(Z * CORES)])
    first, second = merge(keep, received, score)
    first = lax.all_to_all(first, "feat", 0, 0)
    shards = relay(first, second)
    pieces = lax.all_to_all(shards, "batch", 0, 0, axis_index_groups=same_core)
    blocks = gather_scores(add_scores(first))
    shard = jnp.sum(pieces.astype(F32), axis=0).astype(BF16)
    first_grad, second_grad, logits = unpack(place, lax.all_gather(shard, "batch"), blocks)
    return (logits.T, first_grad, second_grad)


def solution(mesh):
    placed = (
        P("batch", "feat"),
        P("batch", None, None, None),
        P("batch"),
        P("batch"),
        P(None, "feat", None),
        P("feat"),
        P(None, "feat", None),
        P("batch", None),
    )
    return jax.shard_map(
        local,
        mesh=mesh,
        in_specs=placed,
        out_specs=(P("batch", None), P(None, "feat", None), P(None, "feat", None)),
        check_vma=False,
    )
```

time: 179 us -> 147 us (0.82)
  starting transfers between devices: 19.2 us -> 34.4 us
  waiting for transfers between devices: 35.1 us -> 20.2 us
  blocking collectives: 73.1 us -> 59.5 us
  between operations: 14.1 us -> 0.75 us
  local copies, waits for them, and re-layouts: 6.02 us -> 0.25 us
  Pallas kernels: 27.7 us -> 31.2 us
  other arithmetic: 3.01 us -> 0.06 us
    all_to_all x1, blocking collectives: 31.6 us -> 13.1 us  [local(): first = lax.all_to_all(first, 'feat', 0, 0)]
    all_to_all x2, waiting for transfers between devices: 33.1 us -> 18.4 us  [the longest x1 10.9 us: local(): lax.all_to_all(pack(core, vertex_embeddings.T, weight_one), 'feat', 0, 0)]
    all_to_all x2, starting transfers between devices: 11.3 us -> 24.3 us  [the longest x1 16.5 us: local(): pieces = lax.all_to_all(shards, 'batch', 0, 0, axis_index_groups=same_core)]
    ppermute x0 -> x3, starting transfers between devices: none -> 7.82 us  [gather_scores(): parts.append(lax.ppermute(score, 'feat', hops))]
    ppermute x1, starting transfers between devices: 7.89 us -> 2.29 us  [local(): lax.ppermute(send, 'batch', [(i, i ^ 1) for i in range(Z * CORES)])]
    all_gather x1 -> x2, blocking collectives: 41.5 us -> 46.4 us  [the longest x1 39.1 us: local(): lax.all_gather(shard, 'batch')]
    unnamed x9 -> x11, local copies, waits for them, and re-layouts: 4.57 us -> 0.12 us
    pallas_call x3 -> x7, Pallas kernels: 27.7 us -> 31.2 us  [the longest x1 13.6 us: layers(): pl.pallas_call(layer_kernel, out_shape=(shard, shard, shape(SIDE, SCORE_R...]
  transfers between devices with their start and end apart: 4 -> 6, of which waited for: 3 -> 3; matrix products, arithmetic and copies ran while one was open for 2% -> 0% of each run, Pallas kernels for 1% -> 9%
where the time goes in v2:
time: 147 us; the launch traced here: 146 us
  blocking collectives  59.5 us (40%)
  starting transfers between devices  34.4 us (23%)
  Pallas kernels  31.2 us (21%)
  waiting for transfers between devices  20.2 us (14%)
    all_gather x1, blocking collectives, local(): lax.all_gather(shard, 'batch')  39.1 us
    all_to_all x1, starting transfers between devices, local(): pieces = lax.all_to_all(shards, 'batch', 0, 0, axis_index_groups=same_core)  16.5 us
    pallas_call x1, Pallas kernels, layers(): pl.pallas_call(layer_kernel, out_shape=(shard, shard, shape(SIDE, SCORE_R...  13.6 us
    all_to_all x1, blocking collectives, local(): first = lax.all_to_all(first, 'feat', 0, 0)  13.1 us
    pallas_call x1, Pallas kernels, adjacency(): pl.pallas_call(adjacency_kernel, out_shape=shape(GROUPS, ADJ_ROWS + ROWS,...  12.6 us
    all_to_all x1, waiting for transfers between devices, local(): lax.all_to_all(pack(core, vertex_embeddings.T, weight_one), 'feat', 0, 0)  10.9 us
    ppermute x3, starting transfers between devices, gather_scores(): parts.append(lax.ppermute(score, 'feat', hops))  7.82 us
    all_to_all x1, starting transfers between devices, local(): lax.all_to_all(pack(core, vertex_embeddings.T, weight_one), 'feat', 0, 0)  7.72 us
  transfers between devices with their start and end apart: 6, of which 3 were waited for; matrix products, arithmetic and copies ran while one was open for 0% of the time, Pallas kernels for 9%

profile of v2, /device:TPU:1, one launch (start us, length us, event | category | flops | bytes accessed | tf_op | source)
XLA Modules:
  0.0 146.3 jit_solution(11929189455388031206)
XLA Ops:
  0.6 2.6 %shard_map.103 = bf16[16,48,1280]{2,1,0:T(8,128)(2,1)} custom-call(s32[1]{0:T(128)} %bitcast.1.core_ref, bf16[48,1024]{1,0:T(8,128)(2,1)} %bitcast.17, bf16[6,48,1024]{2,1,0:T(8,128)(2,1)} %w_ref.1), custom_call_target="tpu_custom_call" | custom-call | tf_op jit(solution)/shard_map/pallas_call | solution.py:321
  3.3 0.0 copy-start.4
  3.3 0.0 copy-start.3
  3.3 7.7 %all-to-all-start = ((bf16[16,48,1280]{2,1,0:T(8,128)(2,1)}), bf16[16,48,1280]{2,1,0:T(8,128)(2,1)S(1)}, u32[]{:S(2)}, u32[]{:S(2)}) async-start(bf16[16,48,1280]{2,1,0:T(8,128)(2,1)} %shard_map.103), calls=%async_computation | async-start | bytes 3932160 | tf_op jit(solution)/shard_map/all_to_all | solution.py:431
  11.0 0.0 copy-done.4
  11.0 0.1 copy.11.bias_ref
  11.1 0.0 copy-done.3
  11.1 0.1 copy.12.upstream_ref
  11.2 12.6 %shard_map.104.adj_from = bf16[2,2944,512]{2,1,0:T(8,128)(2,1)} custom-call(s32[2]{0:T(128)} %counts_ref.3, s32[2]{0:T(128)} %offsets_ref.1, s32[2,5,8,512]{3,2,1,0:T(8,128)} %bitcast.15), custom_call_target="tpu_custom_call" | custom-call | flops 8000000000 | bytes 8388608 | tf_op jit(solution)/shard_map/pallas_call | solution.py:331
  23.9 0.0 copy-start
  23.9 0.0 copy-start.1
  23.9 0.0 copy-start.2
  23.9 10.9 %all-to-all-done = bf16[16,48,1280]{2,1,0:T(8,128)(2,1)S(1)} async-done(((bf16[16,48,1280]{2,1,0:T(8,128)(2,1)}), bf16[16,48,1280]{2,1,0:T(8,128)(2,1)S(1)}, u32[]{:S(2)}, u32[]{:S(2)}) %all-to-all-start) | async-done | bytes 1966112 | tf_op jit(solution)/shard_map/all_to_all | solution.py:431
  34.8 7.3 %all-gather = bf16[1536,256]{1,0:T(8,128)(2,1)S(1)} all-gather(bf16[768,256]{1,0:T(8,128)(2,1)S(1)} %slice.4), channel_id=2, replica_groups={{0,16},{32,48},{64,80},{96,112},{128,144},{160,176},{192,208},{224,240}..., dimensions={0}, use_global_device_ids=true | all-gather | bytes 1179648 | tf_op jit(solution)/shard_map/all_gather | solution.py:433
  42.1 0.0 copy-done
  42.1 0.0 copy-done.1
  42.1 0.0 copy-done.2
  42.1 13.6 %shard_map.105 = (f32[16,88,128]{2,1,0:T(8,128)S(1)}, f32[16,88,128]{2,1,0:T(8,128)S(1)}, bf16[4,48,128]{2,1,0:T(8,128)(2,1)S(1)}) custom-call(s32[1]{0:T(128)} %bitcast.1.core_ref, s32[2]{0:T(128)S(1)} %copy-done.2, bf16[768,1280]{1,0:T(8,128)(2,1)S(1)} %bitcast.12, bf16[2,768,256]{2,1,0:T(8,128)(2,1)S(1)} %bitcast.13, s32[2,5,8,512]{3,2,1,0:T(8,128)S(1)} %bitcast.16, ...), custom_call_target="tpu_custom_call" | custom-call | flops 12000000000 | bytes 12582912 | tf_op jit(solution)/shard_map/pallas_call | solution.py:344
  55.7 2.3 %collective-permute-start = (f32[16,88,128]{2,1,0:T(8,128)S(1)}, f32[16,88,128]{2,1,0:T(8,128)S(1)}, u32[]{:S(2)}, u32[]{:S(2)}) collective-permute-start(f32[16,88,128]{2,1,0:T(8,128)S(1)} %get-tuple-element.12), channel_id=1, source_target_pairs={{0,16},{16,0},{32,48},{48,32},{64,80},{80,64},{96,112},{112,96},{1... | collective-permute-start | bytes 2162696 | tf_op jit(solution)/shard_map/ppermute | solution.py:447
  58.0 1.8 %collective-permute-done.received_ref = f32[16,88,128]{2,1,0:T(8,128)S(1)} collective-permute-done((f32[16,88,128]{2,1,0:T(8,128)S(1)}, f32[16,88,128]{2,1,0:T(8,128)S(1)}, u32[]{:S(2)}, u32[]{:S(2)}) %collective-permute-start) | collective-permute-done | bytes 720928 | tf_op jit(solution)/shard_map/ppermute | solution.py:447
  59.8 0.1 shard_map.106
  59.9 13.1 %all_to_all.15.message_ref = bf16[16,120,128]{2,1,0:T(8,128)(2,1)S(1)} all-to-all(bf16[16,120,128]{2,1,0:T(8,128)(2,1)S(1)} %get-tuple-element.14), channel_id=1, replica_groups=mesh['batch'=32,'feat'=16] {'feat'}, dimensions={0} | all-to-all | bytes 983040 | tf_op jit(solution)/shard_map/all_to_all | solution.py:449
  73.0 0.8 shard_map.107
  73.8 16.5 %all-to-all-start.2 = ((bf16[16,88,128]{2,1,0:T(8,128)(2,1)}), bf16[16,88,128]{2,1,0:T(8,128)(2,1)S(1)}, u32[]{:S(2)}, u32[]{:S(2)}) async-start(bf16[16,88,128]{2,1,0:T(8,128)(2,1)} %shard_map.107), calls=%async_computation.2 | async-start | bytes 720896 | tf_op jit(solution)/shard_map/all_to_all | solution.py:451
  90.4 2.0 %collective-permute-start.3 = (f32[40,128]{1,0:T(8,128)S(1)}, f32[40,128]{1,0:T(8,128)S(1)}, u32[]{:S(2)}, u32[]{:S(2)}) collective-permute-start(f32[40,128]{1,0:T(8,128)S(1)} %shard_map.108.s0_ref), channel_id=1, source_target_pairs={{0,3},{1,0},{2,1},{3,2},{4,7},{5,4},{6,5},{7,6},{8,11},{9,8},{10,9... | collective-permute-start | bytes 61448 | tf_op jit(solution)/shard_map/ppermute | solution.py:398
  92.3 3.9 %collective-permute-start.2 = (f32[40,128]{1,0:T(8,128)S(1)}, f32[40,128]{1,0:T(8,128)S(1)}, u32[]{:S(2)}, u32[]{:S(2)}) collective-permute-start(f32[40,128]{1,0:T(8,128)S(1)} %shard_map.108.s0_ref), channel_id=1, source_target_pairs={{0,2},{1,3},{2,0},{3,1},{4,6},{5,7},{6,4},{7,5},{8,10},{9,11},{10,... | collective-permute-start | bytes 61448 | tf_op jit(solution)/shard_map/ppermute | solution.py:398
  96.3 1.9 %collective-permute-start.1 = (f32[40,128]{1,0:T(8,128)S(1)}, f32[40,128]{1,0:T(8,128)S(1)}, u32[]{:S(2)}, u32[]{:S(2)}) collective-permute-start(f32[40,128]{1,0:T(8,128)S(1)} %shard_map.108.s0_ref), channel_id=1, source_target_pairs={{0,1},{1,2},{2,3},{3,0},{4,5},{5,6},{6,7},{7,4},{8,9},{9,10},{10,1... | collective-permute-start | bytes 61448 | tf_op jit(solution)/shard_map/ppermute | solution.py:398
  98.2 7.5 %all-to-all-done.2 = bf16[16,88,128]{2,1,0:T(8,128)(2,1)S(1)} async-done(((bf16[16,88,128]{2,1,0:T(8,128)(2,1)}), bf16[16,88,128]{2,1,0:T(8,128)(2,1)S(1)}, u32[]{:S(2)}, u32[]{:S(2)}) %all-to-all-start.2) | async-done | bytes 360480 | tf_op jit(solution)/shard_map/all_to_all | solution.py:451
  105.7 0.1 reduce_sum.12
  105.7 39.1 %all-gather.1 = bf16[2816,128]{1,0:T(8,128)(2,1)S(1)} all-gather(bf16[88,128]{1,0:T(8,128)(2,1)S(1)} %reduce_sum.12), channel_id=3, replica_groups=mesh['batch'=32,'feat'=16] {'batch'}, dimensions={0}, use_global_device_ids=true | all-gather | bytes 743424 | tf_op jit(solution)/shard_map/all_gather | solution.py:454
  144.8 0.0 collective-permute-done.3.s3_ref
  144.9 0.0 collective-permute-done.2.s2_ref
  144.9 0.0 collective-permute-done.1.s1_ref
  144.9 1.5 %shard_map.109 = (f32[6,48,1024]{2,1,0:T(8,128)}, f32[6,64,153]{2,1,0:T(8,128)}, f32[153,128]{1,0:T(8,128)}) custom-call(s32[1]{0:T(128)} %bitcast.place_ref, bf16[32,88,128]{2,1,0:T(8,128)(2,1)S(1)} %bitcast.10, f32[40,128]{1,0:T(8,128)S(1)} %shard_map.108.s0_ref, f32[40,128]{1,0:T(8,128)S(1)} %collective-permute-done.1.s1_ref, ...), custom_call_target="tpu_custom_call" | custom-call | tf_op jit(solution)/shard_map/pallas_call | solution.py:403
  (2 shorter events, 0.1 us)
Async XLA Ops:
  3.3 7.7 %copy-start.4 = (f32[64]{0:T(128)S(1)}, f32[64]{0:T(128)}, u32[]{:S(2)}) copy-start(f32[64]{0:T(128)} %param.13) | copy-start | bytes 772
  3.3 7.8 %copy-start.3 = (bf16[128,153]{0,1:T(8,128)(2,1)S(1)}, bf16[128,153]{0,1:T(8,128)(2,1)}, u32[]{:S(2)}) copy-start(bf16[128,153]{0,1:T(8,128)(2,1)} %param.15) | copy-start | bytes 117508
  3.3 31.5 %all-to-all-start = ((bf16[16,48,1280]{2,1,0:T(8,128)(2,1)}), bf16[16,48,1280]{2,1,0:T(8,128)(2,1)S(1)}, u32[]{:S(2)}, u32[]{:S(2)}) async-start(bf16[16,48,1280]{2,1,0:T(8,128)(2,1)} %shard_map.103), calls=%async_computation | async-start | bytes 3932160 | tf_op jit(solution)/shard_map/all_to_all | solution.py:431
  23.9 18.2 %copy-start = (bf16[6,64,153]{2,1,0:T(8,128)(2,1)S(1)}, bf16[6,64,153]{2,1,0:T(8,128)(2,1)}, u32[]{:S(2)}) copy-start(bf16[6,64,153]{2,1,0:T(8,128)(2,1)} %param.14) | copy-start | bytes 352516
  23.9 18.2 %copy-start.1 = (s32[2,5,512,8]{2,3,1,0:T(8,128)S(1)}, s32[2,5,512,8]{2,3,1,0:T(8,128)}, u32[]{:S(2)}) copy-start(s32[2,5,512,8]{2,3,1,0:T(8,128)} %param.9) | copy-start | bytes 491524
  23.9 18.2 %copy-start.2 = (s32[2]{0:T(128)S(1)}, s32[2]{0:T(128)}, u32[]{:S(2)}) copy-start(s32[2]{0:T(128)} %counts_ref.3) | copy-start | bytes 28
  55.7 4.1 %collective-permute-start = (f32[16,88,128]{2,1,0:T(8,128)S(1)}, f32[16,88,128]{2,1,0:T(8,128)S(1)}, u32[]{:S(2)}, u32[]{:S(2)}) collective-permute-start(f32[16,88,128]{2,1,0:T(8,128)S(1)} %get-tuple-element.12), channel_id=1, source_target_pairs={{0,16},{16,0},{32,48},{48,32},{64,80},{80,64},{96,112},{112,96},{1... | collective-permute-start | bytes 2162696 | tf_op jit(solution)/shard_map/ppermute | solution.py:447
  73.8 31.9 %all-to-all-start.2 = ((bf16[16,88,128]{2,1,0:T(8,128)(2,1)}), bf16[16,88,128]{2,1,0:T(8,128)(2,1)S(1)}, u32[]{:S(2)}, u32[]{:S(2)}) async-start(bf16[16,88,128]{2,1,0:T(8,128)(2,1)} %shard_map.107), calls=%async_computation.2 | async-start | bytes 720896 | tf_op jit(solution)/shard_map/all_to_all | solution.py:451
  90.4 54.5 %collective-permute-start.3 = (f32[40,128]{1,0:T(8,128)S(1)}, f32[40,128]{1,0:T(8,128)S(1)}, u32[]{:S(2)}, u32[]{:S(2)}) collective-permute-start(f32[40,128]{1,0:T(8,128)S(1)} %shard_map.108.s0_ref), channel_id=1, source_target_pairs={{0,3},{1,0},{2,1},{3,2},{4,7},{5,4},{6,5},{7,6},{8,11},{9,8},{10,9... | collective-permute-start | bytes 61448 | tf_op jit(solution)/shard_map/ppermute | solution.py:398
  92.3 52.5 %collective-permute-start.2 = (f32[40,128]{1,0:T(8,128)S(1)}, f32[40,128]{1,0:T(8,128)S(1)}, u32[]{:S(2)}, u32[]{:S(2)}) collective-permute-start(f32[40,128]{1,0:T(8,128)S(1)} %shard_map.108.s0_ref), channel_id=1, source_target_pairs={{0,2},{1,3},{2,0},{3,1},{4,6},{5,7},{6,4},{7,5},{8,10},{9,11},{10,... | collective-permute-start | bytes 61448 | tf_op jit(solution)/shard_map/ppermute | solution.py:398
  96.3 48.6 %collective-permute-start.1 = (f32[40,128]{1,0:T(8,128)S(1)}, f32[40,128]{1,0:T(8,128)S(1)}, u32[]{:S(2)}, u32[]{:S(2)}) collective-permute-start(f32[40,128]{1,0:T(8,128)S(1)} %shard_map.108.s0_ref), channel_id=1, source_target_pairs={{0,1},{1,2},{2,3},{3,0},{4,5},{5,6},{6,7},{7,4},{8,9},{9,10},{10,1... | collective-permute-start | bytes 61448 | tf_op jit(solution)/shard_map/ppermute | solution.py:398

commit v3 on v2

v3 whole, which is shorter than its diff:
```python
import jax
import jax.numpy as jnp
from jax import lax
from jax.experimental import pallas as pl
from jax.experimental.pallas import tpu as pltpu
from jax.sharding import PartitionSpec as P

BF16 = jnp.bfloat16
F32 = jnp.float32

GROUPS = 2
CAPACITY = 512
RELATIONS = 5
KINDS = RELATIONS + 1
SLOTS = 8
TARGETS = 64
CLASSES = 153
FEAT = 16
COLUMNS = 48
WIDTH = FEAT * COLUMNS
UNITS = 64
HIDDEN = FEAT * UNITS
PAIRS = KINDS // 2
NODES = GROUPS * CAPACITY
WEIGHT_LANES = 256
MESSAGE = NODES + WEIGHT_LANES
Z = 16
CORES = 2
HALF = COLUMNS // CORES
FIRST_ROWS = PAIRS * HALF
SECOND_ROWS = 16
SHARD_ROWS = SECOND_ROWS + FIRST_ROWS
CLASS_ROWS = 160
SIDE = 4
ADJ_ROWS = RELATIONS * CAPACITY
ROWS = KINDS * TARGETS
MIB = 1024 * 1024


def dot(a, b, contract):
    return lax.dot_general(a, b, ((contract[:1], contract[1:]), ((), ())), preferred_element_type=F32)


def eye(size):
    row = lax.broadcasted_iota(jnp.int32, (size, size), 0)
    column = lax.broadcasted_iota(jnp.int32, (size, size), 1)
    return (row == column).astype(F32).astype(BF16)


def swap_halves(tile):
    return pltpu.roll(tile, UNITS, 1)


def low_half(rows):
    return lax.broadcasted_iota(jnp.int32, (rows, 2 * UNITS), 1) < UNITS


def pack_kernel(core_ref, x_ref, w_ref, out_ref):
    columns = x_ref[...]
    for dest in range(FEAT):
        out_ref[dest, :, :NODES] = columns
    low = low_half(COLUMNS)
    core = core_ref[0]
    for tile in range(FEAT // 2):
        lanes = pl.ds(tile * 2 * UNITS, 2 * UNITS)
        first, second, third = [w_ref[2 * pair + core, :, lanes].astype(F32) for pair in range(PAIRS)]
        front = pl.ds(NODES, 2 * UNITS)
        back = pl.ds(NODES + 2 * UNITS, 2 * UNITS)
        out_ref[2 * tile, :, front] = jnp.where(low, first, swap_halves(second)).astype(BF16)
        out_ref[2 * tile, :, back] = third.astype(BF16)
        out_ref[2 * tile + 1, :, front] = jnp.where(low, swap_halves(first), second).astype(BF16)
        out_ref[2 * tile + 1, :, back] = swap_halves(third).astype(BF16)


def live_slots(ids, count):
    node = lax.broadcasted_iota(jnp.int32, (SLOTS, CAPACITY), 1)
    return (ids >= 0) & (ids < count) & (node < count)


def adjacency_kernel(
    counts_ref,
    offsets_ref,
    slots_ref,
    weight_ref,
    upstream_ref,
    adj_ref,
    grad_ref,
    degree_ref,
    value_ref,
):
    tile_row = lax.broadcasted_iota(jnp.int32, (16, CAPACITY), 0).astype(F32).astype(BF16)
    one = jnp.ones((16, CAPACITY), BF16)
    zero = jnp.zeros((16, CAPACITY), BF16)
    target = lax.broadcasted_iota(jnp.int32, (TARGETS, CAPACITY), 0)
    place = lax.broadcasted_iota(jnp.int32, (TARGETS, CAPACITY), 1)
    half = CAPACITY // 2
    for group in range(GROUPS):
        count = counts_ref[group]
        pick = (place == target + offsets_ref[group]).astype(F32).astype(BF16)
        adj_ref[group, ADJ_ROWS : ADJ_ROWS + TARGETS, :] = pick

        def relation_step(relation, carry, group=group, count=count, pick=pick):
            ids = slots_ref[group, relation]
            live = live_slots(ids, count)
            origin = pl.multiple_of(relation * CAPACITY, CAPACITY)
            for part in range(2):
                inside = live & (ids >= part * half) & (ids < (part + 1) * half)
                value = jnp.where(inside, ids - part * half, -1).astype(F32)
                for slot in range(SLOTS):
                    value_ref[part, slot] = jnp.broadcast_to(
                        value[slot : slot + 1, :], (16, CAPACITY)
                    ).astype(BF16)
            for part in range(2):

                def tile_step(step, carry, part=part):
                    base = step * 32
                    here = tile_row + base.astype(F32).astype(BF16)
                    there = here + jnp.full((), 16, BF16)
                    first = zero
                    second = zero
                    for slot in range(SLOTS):
                        value = value_ref[part, slot]
                        first = first + jnp.where(value == here, one, zero)
                        second = second + jnp.where(value == there, one, zero)
                    start = pl.multiple_of(origin + part * half + base, 32)
                    adj_ref[group, pl.ds(start, 16), :] = first
                    adj_ref[group, pl.ds(start + 16, 16), :] = second
                    return carry

                lax.fori_loop(0, half // 32, tile_step, 0)
            start = pl.multiple_of(ADJ_ROWS + (relation + 1) * TARGETS, TARGETS)
            adj_ref[group, pl.ds(start, TARGETS), :] = dot(
                pick, adj_ref[group, pl.ds(origin, CAPACITY), :], (1, 1)
            ).astype(BF16)
            return carry

        lax.fori_loop(0, RELATIONS, relation_step, 0)
        rows = adj_ref[group, ADJ_ROWS:, :]
        degree = jnp.maximum(jnp.sum(rows.astype(F32), axis=1, keepdims=True), 1.0)
        degree_ref[group] = jnp.broadcast_to(degree, (ROWS, 2 * UNITS))
        upstream = upstream_ref[group * TARGETS : (group + 1) * TARGETS, :]
        returned = []
        for kind in range(KINDS):
            returned.append(dot(upstream, weight_ref[kind * UNITS : (kind + 1) * UNITS, :], (1, 1)))
        spread = (jnp.concatenate(returned, axis=0) / degree).astype(BF16)
        grad_ref[group] = dot(spread, rows, (0, 0))


def layer_kernel(
    core_ref,
    counts_ref,
    message_ref,
    first_ref,
    slots_ref,
    bias_ref,
    weight_ref,
    upstream_ref,
    adj_from,
    grad_from,
    degree_from,
    keep_ref,
    send_ref,
    score_ref,
    adj_ref,
    grad_ref,
    degree_ref,
    adj_sem,
    other_sem,
    mixed_ref,
    low_ref,
    high_ref,
    whole_ref,
):
    def fetch(group, relation):
        size = CAPACITY if relation < RELATIONS else ROWS
        rows = pl.ds(relation * CAPACITY, size)
        return pltpu.make_async_copy(
            adj_from.at[group, rows], adj_ref.at[group, rows], adj_sem.at[group, relation]
        )

    others = [
        pltpu.make_async_copy(grad_from, grad_ref, other_sem.at[0]),
        pltpu.make_async_copy(degree_from, degree_ref, other_sem.at[1]),
    ]
    for group in range(GROUPS):
        for relation in range(KINDS):
            fetch(group, relation).start()
        if group == 0:
            others[0].start()
            others[1].start()
    turn = eye(WEIGHT_LANES)
    first_weight = [dot(turn, first_ref[part], (1, 1)).astype(BF16) for part in range(CORES)]
    size = WIDTH // 3
    preacts = []
    for group in range(GROUPS):
        lanes = slice(group * CAPACITY, (group + 1) * CAPACITY)
        count = counts_ref[group]
        for relation in range(RELATIONS):
            fetch(group, relation).wait()
            adjacency = adj_ref[group, relation * CAPACITY : (relation + 1) * CAPACITY, :]
            live = live_slots(slots_ref[group, relation], count)
            inverse = 1.0 / jnp.maximum(jnp.sum(live.astype(F32), axis=0, keepdims=True), 1.0)
            for block in range(3):
                mixed = dot(message_ref[block * size : (block + 1) * size, lanes], adjacency, (1, 0))
                start = relation * WIDTH + block * size
                mixed_ref[group, start : start + size, :] = (mixed * inverse).astype(BF16)
        preact = bias_ref[...] + dot(first_weight[0][:UNITS], message_ref[:, lanes], (1, 0))
        for kind in range(1, KINDS):
            preact = preact + dot(
                first_weight[kind % CORES][kind // CORES * UNITS : (kind // CORES + 1) * UNITS],
                mixed_ref[group, (kind - 1) * WIDTH : kind * WIDTH, :],
                (1, 0),
            )
        preacts.append(preact)
    others[0].wait()
    others[1].wait()
    hiddens = []
    for group, preact in enumerate(preacts):
        hiddens.append(jnp.maximum(preact, 0.0).astype(BF16))
        pre_grad = jnp.where(preact > 0, grad_ref[group], 0.0)
        nothing = jnp.zeros_like(pre_grad)
        low_ref[group] = jnp.concatenate([pre_grad, nothing], axis=0).astype(BF16)
        high_ref[group] = jnp.concatenate([nothing, pre_grad], axis=0).astype(BF16)
    score_parts = []
    grad_second = jnp.zeros((CLASSES, KINDS * UNITS), F32)
    for group, hidden in enumerate(hiddens):
        fetch(group, RELATIONS).wait()
        rows = adj_ref[group, ADJ_ROWS:, :]
        second_in = dot(rows, hidden, (1, 1)) / degree_ref[group][:, :UNITS]
        wide = jnp.concatenate(
            [second_in[kind * TARGETS : (kind + 1) * TARGETS] for kind in range(KINDS)], axis=1
        ).astype(BF16)
        score_parts.append(dot(weight_ref[...], wide, (0, 1)))
        upstream = upstream_ref[group * TARGETS : (group + 1) * TARGETS, :]
        grad_second = grad_second + dot(upstream, wide, (0, 0))
    tail = jnp.zeros((CLASS_ROWS - CLASSES, 2 * UNITS), F32)
    score = jnp.concatenate([jnp.concatenate(score_parts, axis=1), tail], axis=0)
    score_ref[...] = score
    for pair in range(PAIRS):
        total = jnp.zeros((WIDTH, 2 * UNITS), F32)
        for group in range(GROUPS):
            lanes = slice(group * CAPACITY, (group + 1) * CAPACITY)
            if pair == 0:
                even = message_ref[:, lanes]
            else:
                even = mixed_ref[group, (2 * pair - 1) * WIDTH : 2 * pair * WIDTH, :]
            odd = mixed_ref[group, 2 * pair * WIDTH : (2 * pair + 1) * WIDTH, :]
            total = total + dot(even, low_ref[group], (1, 1)) + dot(odd, high_ref[group], (1, 1))
        total = total.reshape(FEAT, COLUMNS, 2 * UNITS)
        start = SECOND_ROWS + pair * HALF
        for part in range(CORES):
            whole_ref[part, :, start : start + HALF, :] = total[:, part * HALF : (part + 1) * HALF, :]
    packed = []
    for pair in range(PAIRS):
        packed.append(grad_second[:, pair * 2 * UNITS : (pair + 1) * 2 * UNITS])
        packed.append(tail)
    packed.append(jnp.zeros((Z * CORES * SECOND_ROWS - PAIRS * CLASS_ROWS, 2 * UNITS), F32))
    packed = jnp.concatenate(packed, axis=0).reshape(Z, CORES, SECOND_ROWS, 2 * UNITS)
    for part in range(CORES):
        whole_ref[part, :, :SECOND_ROWS, :] = packed[:, part]
    core = core_ref[0]
    keep_ref[...] = whole_ref[core]
    send_ref[...] = whole_ref[1 - core]


def merge_kernel(keep_ref, received_ref, message_ref, second_ref):
    chip = keep_ref[...] + received_ref[...]
    message_ref[...] = chip[:, SECOND_ROWS:, :].astype(BF16)
    second_ref[...] = chip[:, :SECOND_ROWS, :].astype(BF16)


def relay_kernel(message_ref, second_ref, score_ref, shards_ref, passed_ref):
    shards_ref[:, SECOND_ROWS:, :] = message_ref[...]
    shards_ref[:, :SECOND_ROWS, :] = second_ref[...]
    passed_ref[...] = score_ref[...]


def fold_kernel(pieces_ref, s0_ref, s1_ref, s2_ref, s3_ref, copies_ref, score_ref):
    total = pieces_ref[0].astype(F32)
    for part in range(1, Z):
        total = total + pieces_ref[part].astype(F32)
    total = total.astype(BF16)
    for part in range(Z):
        copies_ref[part] = total
    score_ref[...] = s0_ref[...] + s1_ref[...] + s2_ref[...] + s3_ref[...]


def unpack_kernel(shards_ref, s0_ref, s1_ref, s2_ref, s3_ref, first_ref, second_ref, logits_ref):
    low = low_half(HALF)
    for tile in range(FEAT // 2):
        lanes = pl.ds(tile * 2 * UNITS, 2 * UNITS)
        for part in range(CORES):
            left = shards_ref[part, 2 * tile].astype(F32)
            right = shards_ref[part, 2 * tile + 1].astype(F32)
            rows = pl.ds(part * HALF, HALF)
            for pair in range(PAIRS):
                start = SECOND_ROWS + pair * HALF
                a = left[start : start + HALF]
                b = right[start : start + HALF]
                first_ref[2 * pair, rows, lanes] = jnp.where(low, a, swap_halves(b))
                first_ref[2 * pair + 1, rows, lanes] = jnp.where(low, swap_halves(a), b)
    packed = jnp.stack([shards_ref[part, :, :SECOND_ROWS, :] for part in range(CORES)], axis=1)
    packed = packed.reshape(Z * CORES * SECOND_ROWS, 2 * UNITS)
    identity = eye(2 * UNITS)
    for pair in range(PAIRS):
        block = packed[pair * CLASS_ROWS : (pair + 1) * CLASS_ROWS]
        turned = dot(identity, block, (1, 1))
        second_ref[2 * pair] = turned[:UNITS, :CLASSES]
        second_ref[2 * pair + 1] = turned[UNITS:, :CLASSES]
    logits_ref[...] = (s0_ref[...] + s1_ref[...] + s2_ref[...] + s3_ref[...])[:CLASSES]


VMEM = pl.BlockSpec(memory_space=pltpu.VMEM)
SMEM = pl.BlockSpec(memory_space=pltpu.SMEM)


def params(mib):
    return pltpu.CompilerParams(vmem_limit_bytes=mib * MIB)


def cost(flops, size):
    return pl.CostEstimate(flops=flops, bytes_accessed=size, transcendentals=0)


def shape(*dims, dtype=BF16):
    return jax.ShapeDtypeStruct(dims, dtype)


def pack(core, x, w):
    return pl.pallas_call(
        pack_kernel,
        out_shape=shape(FEAT, COLUMNS, MESSAGE),
        in_specs=[SMEM, VMEM, VMEM],
        out_specs=VMEM,
        compiler_params=params(58),
    )(core, x, w)


def adjacency(counts, offsets, slots, weight, upstream):
    return pl.pallas_call(
        adjacency_kernel,
        out_shape=(
            shape(GROUPS, ADJ_ROWS + ROWS, CAPACITY),
            shape(GROUPS, UNITS, CAPACITY, dtype=F32),
            shape(GROUPS, ROWS, 2 * UNITS, dtype=F32),
        ),
        in_specs=[SMEM] * 2 + [VMEM] * 3,
        out_specs=(VMEM,) * 3,
        scratch_shapes=[pltpu.VMEM((2, SLOTS, 16, CAPACITY), BF16)],
        compiler_params=params(58),
        cost_estimate=cost(8 * 10**9, 8 * MIB),
    )(counts, offsets, slots, weight, upstream)


def layers(core, counts, message, first, slots, bias, weight, upstream, adj, grad, degree):
    shard = shape(Z, SHARD_ROWS, 2 * UNITS, dtype=F32)
    return pl.pallas_call(
        layer_kernel,
        out_shape=(shard, shard, shape(CLASS_ROWS, GROUPS * TARGETS, dtype=F32)),
        in_specs=[SMEM] * 2 + [VMEM] * 6 + [pl.BlockSpec(memory_space=pl.ANY)] * 3,
        out_specs=(VMEM, VMEM, VMEM),
        scratch_shapes=[
            pltpu.VMEM(adj.shape, BF16),
            pltpu.VMEM(grad.shape, F32),
            pltpu.VMEM(degree.shape, F32),
            pltpu.SemaphoreType.DMA((GROUPS, KINDS)),
            pltpu.SemaphoreType.DMA((2,)),
            pltpu.VMEM((GROUPS, RELATIONS * WIDTH, CAPACITY), BF16),
            pltpu.VMEM((GROUPS, 2 * UNITS, CAPACITY), BF16),
            pltpu.VMEM((GROUPS, 2 * UNITS, CAPACITY), BF16),
            pltpu.VMEM((CORES, Z, SHARD_ROWS, 2 * UNITS), F32),
        ],
        compiler_params=params(44),
        cost_estimate=cost(12 * 10**9, 12 * MIB),
    )(core, counts, message, first, slots, bias, weight, upstream, adj, grad, degree)


def merge(keep, received):
    return pl.pallas_call(
        merge_kernel,
        out_shape=(shape(FEAT, FIRST_ROWS, 2 * UNITS), shape(Z, SECOND_ROWS, 2 * UNITS)),
        in_specs=[VMEM] * 2,
        out_specs=(VMEM,) * 2,
        compiler_params=params(8),
    )(keep, received)


def relay(message, second, score):
    return pl.pallas_call(
        relay_kernel,
        out_shape=(shape(Z, SHARD_ROWS, 2 * UNITS), shape(*score.shape, dtype=F32)),
        in_specs=[VMEM] * 3,
        out_specs=(VMEM,) * 2,
        compiler_params=params(8),
    )(message, second, score)


def fold(pieces, scores):
    return pl.pallas_call(
        fold_kernel,
        out_shape=(shape(Z, SHARD_ROWS, 2 * UNITS), shape(*scores[0].shape, dtype=F32)),
        in_specs=[VMEM] * 5,
        out_specs=(VMEM,) * 2,
        compiler_params=params(8),
    )(pieces, *scores)


def row_hops(step):
    return [(i, i // SIDE * SIDE + (i + step) % SIDE) for i in range(FEAT)]


def column_hops(step):
    return [(i, (i + step * SIDE) % FEAT) for i in range(FEAT)]


def spread_out(score, hops):
    return [score] + [lax.ppermute(score, "feat", hops(step)) for step in range(1, SIDE)]


def unpack(shards, scores):
    return pl.pallas_call(
        unpack_kernel,
        out_shape=(
            shape(KINDS, COLUMNS, HIDDEN, dtype=F32),
            shape(KINDS, UNITS, CLASSES, dtype=F32),
            shape(CLASSES, GROUPS * TARGETS, dtype=F32),
        ),
        in_specs=[VMEM] * 5,
        out_specs=(VMEM, VMEM, VMEM),
        compiler_params=params(8),
    )(shards, *scores)


def local(
    vertex_embeddings,
    adjacent_vertices,
    node_counts,
    target_offsets,
    weight_one,
    bias_one,
    weight_two,
    score_derivative,
):
    core = (lax.axis_index("batch") % CORES).astype(jnp.int32).reshape(1)
    chips = [[z * CORES + c for c in range(CORES)] for z in range(Z)]
    same_core = [[z * CORES + c for z in range(Z)] for c in range(CORES)]
    message = lax.all_to_all(pack(core, vertex_embeddings.T, weight_one), "feat", 0, 0)
    message = message.reshape(WIDTH, MESSAGE)
    first = lax.all_gather(message[:, NODES:], "batch", axis_index_groups=chips)
    slots = jnp.swapaxes(adjacent_vertices, 2, 3)
    weight = weight_two.reshape(KINDS * UNITS, CLASSES)
    adj, grad, degree = adjacency(node_counts, target_offsets, slots, weight, score_derivative)
    keep, send, score = layers(
        core,
        node_counts,
        message,
        first,
        slots,
        bias_one.reshape(UNITS, 1),
        weight,
        score_derivative,
        adj,
        grad,
        degree,
    )
    received = lax.ppermute(send, "batch", [(i, i ^ 1) for i in range(Z * CORES)])
    message, second = merge(keep, received)
    message = lax.all_to_all(message, "feat", 0, 0)
    shards, score = relay(message, second, score)
    pieces = lax.all_to_all(shards, "batch", 0, 0, axis_index_groups=same_core)
    copies, score = fold(pieces, spread_out(score, row_hops))
    shards = lax.all_to_all(copies, "batch", 0, 0, axis_index_groups=same_core)
    scores = spread_out(score, column_hops)
    shards = lax.all_gather(shards, "batch", axis_index_groups=chips)
    first_grad, second_grad, logits = unpack(shards, scores)
    return (logits.T, first_grad, second_grad)


def solution(mesh):
    placed = (
        P("batch", "feat"),
        P("batch", None, None, None),
        P("batch"),
        P("batch"),
        P(None, "feat", None),
        P("feat"),
        P(None, "feat", None),
        P("batch", None),
    )
    return jax.shard_map(
        local,
        mesh=mesh,
        in_specs=placed,
        out_specs=(P("batch", None), P(None, "feat", None), P(None, "feat", None)),
        check_vma=False,
    )
```

time: 147 us -> 143 us (0.973)
  blocking collectives: 59.5 us -> 27.6 us
  starting transfers between devices: 34.4 us -> 54.3 us
  waiting for transfers between devices: 20.2 us -> 27.1 us
    all_gather x1, blocking collectives: 39.1 us -> 9.15 us  [local(): shards = lax.all_gather(shards, 'batch', axis_index_groups=chips)]
    all_to_all x0 -> x1, starting transfers between devices: none -> 12.9 us  [local(): shards = lax.all_to_all(copies, 'batch', 0, 0, axis_index_groups=same_core)]
    all_to_all x0 -> x1, waiting for transfers between devices: none -> 8.42 us  [local(): shards = lax.all_to_all(copies, 'batch', 0, 0, axis_index_groups=same_core)]
    ppermute x3 -> x6, starting transfers between devices: 7.82 us -> 14.9 us  [spread_out(): lax.ppermute(score, 'feat', hops(step))]
    all_to_all x1, waiting for transfers between devices: 7.46 us -> 2.39 us  [local(): pieces = lax.all_to_all(shards, 'batch', 0, 0, axis_index_groups=same_core)]
    ppermute x3 -> x6, waiting for transfers between devices: 0.01 us -> 4.95 us  [spread_out(): lax.ppermute(score, 'feat', hops(step))]
    all_to_all x1, blocking collectives: 13.1 us -> 11.2 us  [local(): message = lax.all_to_all(message, 'feat', 0, 0)]
  transfers between devices with their start and end apart: 6 -> 10, of which waited for: 3 -> 6; matrix products, arithmetic and copies ran while one was open for 0% -> 1% of each run, Pallas kernels for 9% -> 9%
where the time goes in v3:
time: 143 us
  starting transfers between devices  54.3 us (38%)
  Pallas kernels  31.9 us (22%)
  blocking collectives  27.6 us (19%)
  waiting for transfers between devices  27.1 us (19%)
    all_to_all x1, starting transfers between devices, local(): pieces = lax.all_to_all(shards, 'batch', 0, 0, axis_index_groups=same_core)  16.5 us
    ppermute x6, starting transfers between devices, spread_out(): lax.ppermute(score, 'feat', hops(step))  14.9 us
    pallas_call x1, Pallas kernels, adjacency(): pl.pallas_call(adjacency_kernel, out_shape=(shape(GROUPS, ADJ_ROWS + ROWS...  13.3 us
    all_to_all x1, starting transfers between devices, local(): shards = lax.all_to_all(copies, 'batch', 0, 0, axis_index_groups=same_core)  12.9 us
    pallas_call x1, Pallas kernels, layers(): pl.pallas_call(layer_kernel, out_shape=(shard, shard, shape(CLASS_ROWS, G...  12.8 us
    all_to_all x1, blocking collectives, local(): message = lax.all_to_all(message, 'feat', 0, 0)  11.2 us
    all_to_all x1, waiting for transfers between devices, local(): lax.all_to_all(pack(core, vertex_embeddings.T, weight_one), 'feat', 0, 0)  9.57 us
    all_gather x1, blocking collectives, local(): shards = lax.all_gather(shards, 'batch', axis_index_groups=chips)  9.15 us
  transfers between devices with their start and end apart: 10, of which 6 were waited for; matrix products, arithmetic and copies ran while one was open for 1% of the time, Pallas kernels for 9%

profile of v3, /device:TPU:1, one launch (start us, length us, event | category | flops | bytes accessed | tf_op | source)
XLA Modules:
  0.0 142.7 jit_solution(8213017275930234790)
XLA Ops:
  0.6 2.7 %shard_map.103 = bf16[16,48,1280]{2,1,0:T(8,128)(2,1)} custom-call(s32[1]{0:T(128)} %bitcast.core_ref, bf16[48,1024]{1,0:T(8,128)(2,1)} %bitcast.17, bf16[6,48,1024]{2,1,0:T(8,128)(2,1)} %w_ref.1), custom_call_target="tpu_custom_call" | custom-call | tf_op jit(solution)/shard_map/pallas_call | solution.py:330
  3.3 0.0 copy-start.7
  3.3 0.0 copy-start.6
  3.3 7.7 %all-to-all-start = ((bf16[16,48,1280]{2,1,0:T(8,128)(2,1)}), bf16[16,48,1280]{2,1,0:T(8,128)(2,1)S(1)}, u32[]{:S(2)}, u32[]{:S(2)}) async-start(bf16[16,48,1280]{2,1,0:T(8,128)(2,1)} %shard_map.103), calls=%async_computation | async-start | bytes 3932160 | tf_op jit(solution)/shard_map/all_to_all | solution.py:447
  11.0 0.0 copy-done.7
  11.1 0.1 copy.15.bias_ref
  11.2 0.0 copy-done.6
  11.2 0.7 copy.16.upstream_ref
  11.9 13.3 %shard_map.104 = (bf16[2,2944,512]{2,1,0:T(8,128)(2,1)}, f32[2,64,512]{2,1,0:T(8,128)}, f32[2,384,128]{2,1,0:T(8,128)}) custom-call(s32[2]{0:T(128)} %counts_ref.3, s32[2]{0:T(128)} %offsets_ref.1, s32[2,5,8,512]{3,2,1,0:T(8,128)} %bitcast.15, bf16[384,153]{1,0:T(8,128)(2,1)} %bitcast.13, bf16[128,153]{1,0:T(8,128)(2,1)} %copy.16.upstream_ref), custom_call_target="tpu_custom_call" | custom-call | flops 8000000000 | bytes 8388608 | tf_op jit(solution)/shard_map/pallas_call | solution.py:340
  25.2 0.0 copy-start
  25.2 0.0 copy-start.1
  25.2 0.0 copy-start.2
  25.2 0.0 copy-start.3
  25.2 0.0 copy-start.4
  25.3 0.0 copy-start.5
  25.3 9.6 %all-to-all-done = bf16[16,48,1280]{2,1,0:T(8,128)(2,1)S(1)} async-done(((bf16[16,48,1280]{2,1,0:T(8,128)(2,1)}), bf16[16,48,1280]{2,1,0:T(8,128)(2,1)S(1)}, u32[]{:S(2)}, u32[]{:S(2)}) %all-to-all-start) | async-done | bytes 1966112 | tf_op jit(solution)/shard_map/all_to_all | solution.py:447
  34.9 7.3 %all-gather = bf16[1536,256]{1,0:T(8,128)(2,1)S(1)} all-gather(bf16[768,256]{1,0:T(8,128)(2,1)S(1)} %slice.4), channel_id=2, replica_groups={{0,16},{32,48},{64,80},{96,112},{128,144},{160,176},{192,208},{224,240}..., dimensions={0}, use_global_device_ids=true | all-gather | bytes 1179648 | tf_op jit(solution)/shard_map/all_gather | solution.py:449
  42.1 0.0 copy-done
  42.1 0.0 copy-done.1
  42.1 0.0 copy-done.2
  42.1 0.0 copy-done.3
  42.1 0.0 copy-done.4
  42.1 0.0 copy-done.5
  42.2 12.8 %shard_map.105 = (f32[16,88,128]{2,1,0:T(8,128)S(1)}, f32[16,88,128]{2,1,0:T(8,128)S(1)}, f32[160,128]{1,0:T(8,128)S(1)}) custom-call(s32[1]{0:T(128)} %bitcast.core_ref, s32[2]{0:T(128)S(1)} %copy-done.3, bf16[768,1280]{1,0:T(8,128)(2,1)S(1)} %bitcast.11, bf16[2,768,256]{2,1,0:T(8,128)(2,1)S(1)} %bitcast.12, s32[2,5,8,512]{3,2,1,0:T(8,128)S(1)} %bitcast.16, ...), custom_call_target="tpu_custom_call" | custom-call | flops 12000000000 | bytes 12582912 | tf_op jit(solution)/shard_map/pallas_call | solution.py:357
  55.0 2.3 %collective-permute-start = (f32[16,88,128]{2,1,0:T(8,128)S(1)}, f32[16,88,128]{2,1,0:T(8,128)S(1)}, u32[]{:S(2)}, u32[]{:S(2)}) collective-permute-start(f32[16,88,128]{2,1,0:T(8,128)S(1)} %get-tuple-element.22), channel_id=1, source_target_pairs={{0,16},{16,0},{32,48},{48,32},{64,80},{80,64},{96,112},{112,96},{1... | collective-permute-start | bytes 2162696 | tf_op jit(solution)/shard_map/ppermute | solution.py:466
  57.3 1.8 %collective-permute-done.received_ref = f32[16,88,128]{2,1,0:T(8,128)S(1)} collective-permute-done((f32[16,88,128]{2,1,0:T(8,128)S(1)}, f32[16,88,128]{2,1,0:T(8,128)S(1)}, u32[]{:S(2)}, u32[]{:S(2)}) %collective-permute-start) | collective-permute-done | bytes 720928 | tf_op jit(solution)/shard_map/ppermute | solution.py:466
  59.1 0.1 shard_map.106
  59.2 11.2 %all_to_all.20.message_ref = bf16[16,72,128]{2,1,0:T(8,128)(2,1)S(1)} all-to-all(bf16[16,72,128]{2,1,0:T(8,128)(2,1)S(1)} %get-tuple-element.23), channel_id=1, replica_groups=mesh['batch'=32,'feat'=16] {'feat'}, dimensions={0} | all-to-all | bytes 589824 | tf_op jit(solution)/shard_map/all_to_all | solution.py:468
  70.3 0.8 shard_map.107
  71.1 16.5 %all-to-all-start.2 = ((bf16[16,88,128]{2,1,0:T(8,128)(2,1)}), bf16[16,88,128]{2,1,0:T(8,128)(2,1)S(1)}, u32[]{:S(2)}, u32[]{:S(2)}) async-start(bf16[16,88,128]{2,1,0:T(8,128)(2,1)} %get-tuple-element.26), calls=%async_computation.2 | async-start | bytes 720896 | tf_op jit(solution)/shard_map/all_to_all | solution.py:470
  87.6 1.9 %collective-permute-start.3 = (f32[160,128]{1,0:T(8,128)S(1)}, f32[160,128]{1,0:T(8,128)S(1)}, u32[]{:S(2)}, u32[]{:S(2)}) collective-permute-start(f32[160,128]{1,0:T(8,128)S(1)} %get-tuple-element.27.s0_ref), channel_id=1, source_target_pairs={{0,3},{1,0},{2,1},{3,2},{4,7},{5,4},{6,5},{7,6},{8,11},{9,8},{10,9... | collective-permute-start | bytes 245768 | tf_op jit(solution)/shard_map/ppermute | solution.py:417
  89.6 3.9 %collective-permute-start.2 = (f32[160,128]{1,0:T(8,128)S(1)}, f32[160,128]{1,0:T(8,128)S(1)}, u32[]{:S(2)}, u32[]{:S(2)}) collective-permute-start(f32[160,128]{1,0:T(8,128)S(1)} %get-tuple-element.27.s0_ref), channel_id=1, source_target_pairs={{0,2},{1,3},{2,0},{3,1},{4,6},{5,7},{6,4},{7,5},{8,10},{9,11},{10,... | collective-permute-start | bytes 245768 | tf_op jit(solution)/shard_map/ppermute | solution.py:417
  93.5 1.9 %collective-permute-start.1 = (f32[160,128]{1,0:T(8,128)S(1)}, f32[160,128]{1,0:T(8,128)S(1)}, u32[]{:S(2)}, u32[]{:S(2)}) collective-permute-start(f32[160,128]{1,0:T(8,128)S(1)} %get-tuple-element.27.s0_ref), channel_id=1, source_target_pairs={{0,1},{1,2},{2,3},{3,0},{4,5},{5,6},{6,7},{7,4},{8,9},{9,10},{10,1... | collective-permute-start | bytes 245768 | tf_op jit(solution)/shard_map/ppermute | solution.py:417
  95.4 0.0 collective-permute-done.3.s3_ref
  95.4 1.1 collective-permute-done.2.s2_ref
  96.5 3.8 %collective-permute-done.1.s1_ref = f32[160,128]{1,0:T(8,128)S(1)} collective-permute-done((f32[160,128]{1,0:T(8,128)S(1)}, f32[160,128]{1,0:T(8,128)S(1)}, u32[]{:S(2)}, u32[]{:S(2)}) %collective-permute-start.1) | collective-permute-done | bytes 81952 | tf_op jit(solution)/shard_map/ppermute | solution.py:417
  100.3 2.4 %all-to-all-done.2.pieces_ref = bf16[16,88,128]{2,1,0:T(8,128)(2,1)S(1)} async-done(((bf16[16,88,128]{2,1,0:T(8,128)(2,1)}), bf16[16,88,128]{2,1,0:T(8,128)(2,1)S(1)}, u32[]{:S(2)}, u32[]{:S(2)}) %all-to-all-start.2) | async-done | bytes 360480 | tf_op jit(solution)/shard_map/all_to_all | solution.py:470
  102.7 0.8 shard_map.108
  103.5 12.9 %all-to-all-start.3 = ((bf16[16,88,128]{2,1,0:T(8,128)(2,1)}), bf16[16,88,128]{2,1,0:T(8,128)(2,1)S(1)}, u32[]{:S(2)}, u32[]{:S(2)}) async-start(bf16[16,88,128]{2,1,0:T(8,128)(2,1)} %get-tuple-element.28), calls=%async_computation.3 | async-start | bytes 720896 | tf_op jit(solution)/shard_map/all_to_all | solution.py:472
  116.4 2.5 %collective-permute-start.6 = (f32[160,128]{1,0:T(8,128)S(1)}, f32[160,128]{1,0:T(8,128)S(1)}, u32[]{:S(2)}, u32[]{:S(2)}) collective-permute-start(f32[160,128]{1,0:T(8,128)S(1)} %get-tuple-element.29.s0_ref), channel_id=1, source_target_pairs={{0,12},{1,13},{2,14},{3,15},{4,0},{5,1},{6,2},{7,3},{8,4},{9,5},{1... | collective-permute-start | bytes 245768 | tf_op jit(solution)/shard_map/ppermute | solution.py:417
  118.9 1.9 %collective-permute-start.5 = (f32[160,128]{1,0:T(8,128)S(1)}, f32[160,128]{1,0:T(8,128)S(1)}, u32[]{:S(2)}, u32[]{:S(2)}) collective-permute-start(f32[160,128]{1,0:T(8,128)S(1)} %get-tuple-element.29.s0_ref), channel_id=1, source_target_pairs={{0,8},{1,9},{2,10},{3,11},{4,12},{5,13},{6,14},{7,15},{8,0},{9,1},... | collective-permute-start | bytes 245768 | tf_op jit(solution)/shard_map/ppermute | solution.py:417
  120.8 2.8 %collective-permute-start.4 = (f32[160,128]{1,0:T(8,128)S(1)}, f32[160,128]{1,0:T(8,128)S(1)}, u32[]{:S(2)}, u32[]{:S(2)}) collective-permute-start(f32[160,128]{1,0:T(8,128)S(1)} %get-tuple-element.29.s0_ref), channel_id=1, source_target_pairs={{0,4},{1,5},{2,6},{3,7},{4,8},{5,9},{6,10},{7,11},{8,12},{9,13},{1... | collective-permute-start | bytes 245768 | tf_op jit(solution)/shard_map/ppermute | solution.py:417
  123.6 8.4 %all-to-all-done.3 = bf16[16,88,128]{2,1,0:T(8,128)(2,1)S(1)} async-done(((bf16[16,88,128]{2,1,0:T(8,128)(2,1)}), bf16[16,88,128]{2,1,0:T(8,128)(2,1)S(1)}, u32[]{:S(2)}, u32[]{:S(2)}) %all-to-all-start.3) | async-done | bytes 360480 | tf_op jit(solution)/shard_map/all_to_all | solution.py:472
  132.1 9.1 %all-gather.1 = bf16[32,88,128]{2,1,0:T(8,128)(2,1)S(1)} all-gather(bf16[16,88,128]{2,1,0:T(8,128)(2,1)S(1)} %all-to-all-done.3), channel_id=3, replica_groups={{0,16},{32,48},{64,80},{96,112},{128,144},{160,176},{192,208},{224,240}..., dimensions={0}, use_global_device_ids=true | all-gather | bytes 1081344 | tf_op jit(solution)/shard_map/all_gather | solution.py:474
  141.2 0.0 collective-permute-done.6.s3_ref
  141.2 0.0 collective-permute-done.5.s2_ref
  141.2 0.0 collective-permute-done.4.s1_ref
  141.2 1.5 %shard_map.109 = (f32[6,48,1024]{2,1,0:T(8,128)}, f32[6,64,153]{2,1,0:T(8,128)}, f32[153,128]{1,0:T(8,128)}) custom-call(bf16[2,16,88,128]{3,2,1,0:T(8,128)(2,1)S(1)} %bitcast.9, f32[160,128]{1,0:T(8,128)S(1)} %get-tuple-element.29.s0_ref, f32[160,128]{1,0:T(8,128)S(1)} %collective-permute-done.4.s1_ref, f32[160,128]{1,0:T(8,128)S(1)} %collective-permute-done.5.s2_ref, ...), custom_call_target="tpu_custom_call" | custom-call | tf_op jit(solution)/shard_map/pallas_call | solution.py:421
  (1 shorter events, 0.0 us)
Async XLA Ops:
  3.3 7.7 %copy-start.7 = (f32[64]{0:T(128)S(1)}, f32[64]{0:T(128)}, u32[]{:S(2)}) copy-start(f32[64]{0:T(128)} %param.13) | copy-start | bytes 772
  3.3 7.8 %copy-start.6 = (bf16[128,153]{0,1:T(8,128)(2,1)S(1)}, bf16[128,153]{0,1:T(8,128)(2,1)}, u32[]{:S(2)}) copy-start(bf16[128,153]{0,1:T(8,128)(2,1)} %param.15) | copy-start | bytes 117508
  3.3 31.5 %all-to-all-start = ((bf16[16,48,1280]{2,1,0:T(8,128)(2,1)}), bf16[16,48,1280]{2,1,0:T(8,128)(2,1)S(1)}, u32[]{:S(2)}, u32[]{:S(2)}) async-start(bf16[16,48,1280]{2,1,0:T(8,128)(2,1)} %shard_map.103), calls=%async_computation | async-start | bytes 3932160 | tf_op jit(solution)/shard_map/all_to_all | solution.py:447
  25.2 16.9 %copy-start = (bf16[128,153]{1,0:T(8,128)(2,1)S(1)}, bf16[128,153]{1,0:T(8,128)(2,1)}, u32[]{:S(2)}) copy-start(bf16[128,153]{1,0:T(8,128)(2,1)} %copy.16.upstream_ref) | copy-start | bytes 117508
  25.2 16.9 %copy-start.1 = (bf16[6,64,153]{2,1,0:T(8,128)(2,1)S(1)}, bf16[6,64,153]{2,1,0:T(8,128)(2,1)}, u32[]{:S(2)}) copy-start(bf16[6,64,153]{2,1,0:T(8,128)(2,1)} %param.14) | copy-start | bytes 352516
  25.2 16.9 %copy-start.2 = (s32[2,5,512,8]{2,3,1,0:T(8,128)S(1)}, s32[2,5,512,8]{2,3,1,0:T(8,128)}, u32[]{:S(2)}) copy-start(s32[2,5,512,8]{2,3,1,0:T(8,128)} %param.9) | copy-start | bytes 491524
  25.2 16.9 %copy-start.3 = (s32[2]{0:T(128)S(1)}, s32[2]{0:T(128)}, u32[]{:S(2)}) copy-start(s32[2]{0:T(128)} %counts_ref.3) | copy-start | bytes 28
  25.2 16.9 %copy-start.4 = (f32[2,384,128]{2,1,0:T(8,128)S(1)}, f32[2,384,128]{2,1,0:T(8,128)}, u32[]{:S(2)}) copy-start(f32[2,384,128]{2,1,0:T(8,128)} %get-tuple-element.20.degree_from) | copy-start | bytes 1179652
  25.3 16.9 %copy-start.5 = (f32[2,64,512]{2,1,0:T(8,128)S(1)}, f32[2,64,512]{2,1,0:T(8,128)}, u32[]{:S(2)}) copy-start(f32[2,64,512]{2,1,0:T(8,128)} %get-tuple-element.19.grad_from) | copy-start | bytes 786436
  55.0 4.1 %collective-permute-start = (f32[16,88,128]{2,1,0:T(8,128)S(1)}, f32[16,88,128]{2,1,0:T(8,128)S(1)}, u32[]{:S(2)}, u32[]{:S(2)}) collective-permute-start(f32[16,88,128]{2,1,0:T(8,128)S(1)} %get-tuple-element.22), channel_id=1, source_target_pairs={{0,16},{16,0},{32,48},{48,32},{64,80},{80,64},{96,112},{112,96},{1... | collective-permute-start | bytes 2162696 | tf_op jit(solution)/shard_map/ppermute | solution.py:466
  71.1 31.6 %all-to-all-start.2 = ((bf16[16,88,128]{2,1,0:T(8,128)(2,1)}), bf16[16,88,128]{2,1,0:T(8,128)(2,1)S(1)}, u32[]{:S(2)}, u32[]{:S(2)}) async-start(bf16[16,88,128]{2,1,0:T(8,128)(2,1)} %get-tuple-element.26), calls=%async_computation.2 | async-start | bytes 720896 | tf_op jit(solution)/shard_map/all_to_all | solution.py:470
  87.6 7.8 %collective-permute-start.3 = (f32[160,128]{1,0:T(8,128)S(1)}, f32[160,128]{1,0:T(8,128)S(1)}, u32[]{:S(2)}, u32[]{:S(2)}) collective-permute-start(f32[160,128]{1,0:T(8,128)S(1)} %get-tuple-element.27.s0_ref), channel_id=1, source_target_pairs={{0,3},{1,0},{2,1},{3,2},{4,7},{5,4},{6,5},{7,6},{8,11},{9,8},{10,9... | collective-permute-start | bytes 245768 | tf_op jit(solution)/shard_map/ppermute | solution.py:417
  89.6 7.0 %collective-permute-start.2 = (f32[160,128]{1,0:T(8,128)S(1)}, f32[160,128]{1,0:T(8,128)S(1)}, u32[]{:S(2)}, u32[]{:S(2)}) collective-permute-start(f32[160,128]{1,0:T(8,128)S(1)} %get-tuple-element.27.s0_ref), channel_id=1, source_target_pairs={{0,2},{1,3},{2,0},{3,1},{4,6},{5,7},{6,4},{7,5},{8,10},{9,11},{10,... | collective-permute-start | bytes 245768 | tf_op jit(solution)/shard_map/ppermute | solution.py:417
  93.5 6.9 %collective-permute-start.1 = (f32[160,128]{1,0:T(8,128)S(1)}, f32[160,128]{1,0:T(8,128)S(1)}, u32[]{:S(2)}, u32[]{:S(2)}) collective-permute-start(f32[160,128]{1,0:T(8,128)S(1)} %get-tuple-element.27.s0_ref), channel_id=1, source_target_pairs={{0,1},{1,2},{2,3},{3,0},{4,5},{5,6},{6,7},{7,4},{8,9},{9,10},{10,1... | collective-permute-start | bytes 245768 | tf_op jit(solution)/shard_map/ppermute | solution.py:417
  103.5 28.5 %all-to-all-start.3 = ((bf16[16,88,128]{2,1,0:T(8,128)(2,1)}), bf16[16,88,128]{2,1,0:T(8,128)(2,1)S(1)}, u32[]{:S(2)}, u32[]{:S(2)}) async-start(bf16[16,88,128]{2,1,0:T(8,128)(2,1)} %get-tuple-element.28), calls=%async_computation.3 | async-start | bytes 720896 | tf_op jit(solution)/shard_map/all_to_all | solution.py:472
  116.4 24.8 %collective-permute-start.6 = (f32[160,128]{1,0:T(8,128)S(1)}, f32[160,128]{1,0:T(8,128)S(1)}, u32[]{:S(2)}, u32[]{:S(2)}) collective-permute-start(f32[160,128]{1,0:T(8,128)S(1)} %get-tuple-element.29.s0_ref), channel_id=1, source_target_pairs={{0,12},{1,13},{2,14},{3,15},{4,0},{5,1},{6,2},{7,3},{8,4},{9,5},{1... | collective-permute-start | bytes 245768 | tf_op jit(solution)/shard_map/ppermute | solution.py:417
  118.9 22.3 %collective-permute-start.5 = (f32[160,128]{1,0:T(8,128)S(1)}, f32[160,128]{1,0:T(8,128)S(1)}, u32[]{:S(2)}, u32[]{:S(2)}) collective-permute-start(f32[160,128]{1,0:T(8,128)S(1)} %get-tuple-element.29.s0_ref), channel_id=1, source_target_pairs={{0,8},{1,9},{2,10},{3,11},{4,12},{5,13},{6,14},{7,15},{8,0},{9,1},... | collective-permute-start | bytes 245768 | tf_op jit(solution)/shard_map/ppermute | solution.py:417
  120.8 20.4 %collective-permute-start.4 = (f32[160,128]{1,0:T(8,128)S(1)}, f32[160,128]{1,0:T(8,128)S(1)}, u32[]{:S(2)}, u32[]{:S(2)}) collective-permute-start(f32[160,128]{1,0:T(8,128)S(1)} %get-tuple-element.29.s0_ref), channel_id=1, source_target_pairs={{0,4},{1,5},{2,6},{3,7},{4,8},{5,9},{6,10},{7,11},{8,12},{9,13},{1... | collective-permute-start | bytes 245768 | tf_op jit(solution)/shard_map/ppermute | solution.py:417

commit v4 on v3

--- a/solution.py
+++ b/solution.py
@@ -26,6 +26,8 @@
 MESSAGE = NODES + WEIGHT_LANES
 Z = 16
 CORES = 2
+BLOCK = 2 * CORES
+BLOCKS = Z * CORES // BLOCK
 HALF = COLUMNS // CORES
 FIRST_ROWS = PAIRS * HALF
 SECOND_ROWS = 16
@@ -34,6 +36,10 @@
 SIDE = 4
 ADJ_ROWS = RELATIONS * CAPACITY
 ROWS = KINDS * TARGETS
+GRAD_START = ADJ_ROWS + ROWS
+DEGREE_START = GRAD_START + UNITS
+DEGREE_ROWS = ROWS // 4
+GRAPH_ROWS = DEGREE_START + DEGREE_ROWS
 MIB = 1024 * 1024
 
 
@@ -55,21 +61,34 @@
     return lax.broadcasted_iota(jnp.int32, (rows, 2 * UNITS), 1) < UNITS
 
 
-def pack_kernel(core_ref, x_ref, w_ref, out_ref):
-    columns = x_ref[...]
+def pack_kernel(core_ref, x_ref, w_ref, out_ref, x_tile, w_tiles, packed_ref, w_sem, x_sem, out_sem):
+    load_x = pltpu.make_async_copy(x_ref, x_tile, w_sem.at[PAIRS])
+    load_x.start()
+    loads = []
+    for pair in range(PAIRS):
+        loads.append(pltpu.make_async_copy(w_ref.at[2 * pair + core_ref[0]], w_tiles.at[pair], w_sem.at[pair]))
+        loads[-1].start()
+    load_x.wait()
+    stores = []
     for dest in range(FEAT):
-        out_ref[dest, :, :NODES] = columns
+        stores.append(pltpu.make_async_copy(x_tile, out_ref.at[dest, :, pl.ds(0, NODES)], x_sem.at[dest]))
+        stores[-1].start()
+    for load in loads:
+        load.wait()
     low = low_half(COLUMNS)
-    core = core_ref[0]
     for tile in range(FEAT // 2):
         lanes = pl.ds(tile * 2 * UNITS, 2 * UNITS)
-        first, second, third = [w_ref[2 * pair + core, :, lanes].astype(F32) for pair in range(PAIRS)]
-        front = pl.ds(NODES, 2 * UNITS)
-        back = pl.ds(NODES + 2 * UNITS, 2 * UNITS)
-        out_ref[2 * tile, :, front] = jnp.where(low, first, swap_halves(second)).astype(BF16)
-        out_ref[2 * tile, :, back] = third.astype(BF16)
-        out_ref[2 * tile + 1, :, front] = jnp.where(low, swap_halves(first), second).astype(BF16)
-        out_ref[2 * tile + 1, :, back] = swap_halves(third).astype(BF16)
+        first, second, third = [w_tiles[pair, :, lanes].astype(F32) for pair in range(PAIRS)]
+        front = pl.ds(0, 2 * UNITS)
+        back = pl.ds(2 * UNITS, 2 * UNITS)
+        packed_ref[2 * tile, :, front] = jnp.where(low, first, swap_halves(second)).astype(BF16)
+        packed_ref[2 * tile, :, back] = third.astype(BF16)
+        packed_ref[2 * tile + 1, :, front] = jnp.where(low, swap_halves(first), second).astype(BF16)
+        packed_ref[2 * tile + 1, :, back] = swap_halves(third).astype(BF16)
+    stores.append(pltpu.make_async_copy(packed_ref, out_ref.at[:, :, pl.ds(NODES, WEIGHT_LANES)], out_sem))
+    stores[-1].start()
+    for store in stores:
+        store.wait()
 
 
 def live_slots(ids, count):
@@ -84,8 +103,6 @@
     weight_ref,
     upstream_ref,
     adj_ref,
-    grad_ref,
-    degree_ref,
     value_ref,
 ):
     tile_row = lax.broadcasted_iota(jnp.int32, (16, CAPACITY), 0).astype(F32).astype(BF16)
@@ -135,15 +152,19 @@
             return carry
 
         lax.fori_loop(0, RELATIONS, relation_step, 0)
-        rows = adj_ref[group, ADJ_ROWS:, :]
+        rows = adj_ref[group, ADJ_ROWS:GRAD_START, :]
         degree = jnp.maximum(jnp.sum(rows.astype(F32), axis=1, keepdims=True), 1.0)
-        degree_ref[group] = jnp.broadcast_to(degree, (ROWS, 2 * UNITS))
+        for part in range(4):
+            piece = degree[part * DEGREE_ROWS : (part + 1) * DEGREE_ROWS]
+            adj_ref[group, DEGREE_START:, part * 2 * UNITS : (part + 1) * 2 * UNITS] = jnp.broadcast_to(
+                piece, (DEGREE_ROWS, 2 * UNITS)
+            ).astype(BF16)
         upstream = upstream_ref[group * TARGETS : (group + 1) * TARGETS, :]
         returned = []
         for kind in range(KINDS):
             returned.append(dot(upstream, weight_ref[kind * UNITS : (kind + 1) * UNITS, :], (1, 1)))
         spread = (jnp.concatenate(returned, axis=0) / degree).astype(BF16)
-        grad_ref[group] = dot(spread, rows, (0, 0))
+        adj_ref[group, GRAD_START:DEGREE_START, :] = dot(spread, rows, (0, 0)).astype(BF16)
 
 
 def layer_kernel(
@@ -156,38 +177,26 @@
     weight_ref,
     upstream_ref,
     adj_from,
-    grad_from,
-    degree_from,
     keep_ref,
     send_ref,
     score_ref,
     adj_ref,
-    grad_ref,
-    degree_ref,
     adj_sem,
-    other_sem,
     mixed_ref,
     low_ref,
     high_ref,
     whole_ref,
 ):
     def fetch(group, relation):
-        size = CAPACITY if relation < RELATIONS else ROWS
+        size = CAPACITY if relation < RELATIONS else GRAPH_ROWS - ADJ_ROWS
         rows = pl.ds(relation * CAPACITY, size)
         return pltpu.make_async_copy(
             adj_from.at[group, rows], adj_ref.at[group, rows], adj_sem.at[group, relation]
         )
 
-    others = [
-        pltpu.make_async_copy(grad_from, grad_ref, other_sem.at[0]),
-        pltpu.make_async_copy(degree_from, degree_ref, other_sem.at[1]),
-    ]
     for group in range(GROUPS):
         for relation in range(KINDS):
             fetch(group, relation).start()
-        if group == 0:
-            others[0].start()
-            others[1].start()
     turn = eye(WEIGHT_LANES)
     first_weight = [dot(turn, first_ref[part], (1, 1)).astype(BF16) for part in range(CORES)]
     size = WIDTH // 3
@@ -212,21 +221,21 @@
                 (1, 0),
             )
         preacts.append(preact)
-    others[0].wait()
-    others[1].wait()
     hiddens = []
     for group, preact in enumerate(preacts):
+        fetch(group, RELATIONS).wait()
         hiddens.append(jnp.maximum(preact, 0.0).astype(BF16))
-        pre_grad = jnp.where(preact > 0, grad_ref[group], 0.0)
+        pre_grad = jnp.where(preact > 0, adj_ref[group, GRAD_START:DEGREE_START, :].astype(F32), 0.0)
         nothing = jnp.zeros_like(pre_grad)
         low_ref[group] = jnp.concatenate([pre_grad, nothing], axis=0).astype(BF16)
         high_ref[group] = jnp.concatenate([nothing, pre_grad], axis=0).astype(BF16)
     score_parts = []
     grad_second = jnp.zeros((CLASSES, KINDS * UNITS), F32)
     for group, hidden in enumerate(hiddens):
-        fetch(group, RELATIONS).wait()
-        rows = adj_ref[group, ADJ_ROWS:, :]
-        second_in = dot(rows, hidden, (1, 1)) / degree_ref[group][:, :UNITS]
+        rows = adj_ref[group, ADJ_ROWS:GRAD_START, :]
+        degree = adj_ref[group, DEGREE_START:, :].astype(F32)
+        degree = jnp.concatenate([degree[:, part * 2 * UNITS : part * 2 * UNITS + UNITS] for part in range(4)], axis=0)
+        second_in = dot(rows, hidden, (1, 1)) / degree
         wide = jnp.concatenate(
             [second_in[kind * TARGETS : (kind + 1) * TARGETS] for kind in range(KINDS)], axis=1
         ).astype(BF16)
@@ -260,11 +269,11 @@
         whole_ref[part, :, :SECOND_ROWS, :] = packed[:, part]
     core = core_ref[0]
     keep_ref[...] = whole_ref[core]
-    send_ref[...] = whole_ref[1 - core]
-
-
-def merge_kernel(keep_ref, received_ref, message_ref, second_ref):
-    chip = keep_ref[...] + received_ref[...]
+    send_ref[...] = whole_ref[1 - core].astype(BF16)
+
+
+def merge_kernel(core_ref, keep_ref, both_ref, message_ref, second_ref):
+    chip = keep_ref[...] + both_ref[1 - core_ref[0]].astype(F32)
     message_ref[...] = chip[:, SECOND_ROWS:, :].astype(BF16)
     second_ref[...] = chip[:, :SECOND_ROWS, :].astype(BF16)
 
@@ -280,7 +289,7 @@
     for part in range(1, Z):
         total = total + pieces_ref[part].astype(F32)
     total = total.astype(BF16)
-    for part in range(Z):
+    for part in range(BLOCKS):
         copies_ref[part] = total
     score_ref[...] = s0_ref[...] + s1_ref[...] + s2_ref[...] + s3_ref[...]
 
@@ -290,8 +299,8 @@
     for tile in range(FEAT // 2):
         lanes = pl.ds(tile * 2 * UNITS, 2 * UNITS)
         for part in range(CORES):
-            left = shards_ref[part, 2 * tile].astype(F32)
-            right = shards_ref[part, 2 * tile + 1].astype(F32)
+            left = shards_ref[part, tile].astype(F32)
+            right = shards_ref[CORES + part, tile].astype(F32)
             rows = pl.ds(part * HALF, HALF)
             for pair in range(PAIRS):
                 start = SECOND_ROWS + pair * HALF
@@ -299,7 +308,7 @@
                 b = right[start : start + HALF]
                 first_ref[2 * pair, rows, lanes] = jnp.where(low, a, swap_halves(b))
                 first_ref[2 * pair + 1, rows, lanes] = jnp.where(low, swap_halves(a), b)
-    packed = jnp.stack([shards_ref[part, :, :SECOND_ROWS, :] for part in range(CORES)], axis=1)
+    packed = jnp.stack([shards_ref[part, :, :SECOND_ROWS, :] for part in range(BLOCK)], axis=1)
     packed = packed.reshape(Z * CORES * SECOND_ROWS, 2 * UNITS)
     identity = eye(2 * UNITS)
     for pair in range(PAIRS):
@@ -327,11 +336,20 @@
 
 
 def pack(core, x, w):
+    anywhere = pl.BlockSpec(memory_space=pl.ANY)
     return pl.pallas_call(
         pack_kernel,
         out_shape=shape(FEAT, COLUMNS, MESSAGE),
-        in_specs=[SMEM, VMEM, VMEM],
-        out_specs=VMEM,
+        in_specs=[SMEM, anywhere, anywhere],
+        out_specs=anywhere,
+        scratch_shapes=[
+            pltpu.VMEM((COLUMNS, NODES), BF16),
+            pltpu.VMEM((PAIRS, COLUMNS, HIDDEN), BF16),
+            pltpu.VMEM((FEAT, COLUMNS, WEIGHT_LANES), BF16),
+            pltpu.SemaphoreType.DMA((PAIRS + 1,)),
+            pltpu.SemaphoreType.DMA((FEAT,)),
+            pltpu.SemaphoreType.DMA,
+        ],
         compiler_params=params(58),
     )(core, x, w)
 
@@ -339,32 +357,25 @@
 def adjacency(counts, offsets, slots, weight, upstream):
     return pl.pallas_call(
         adjacency_kernel,
-        out_shape=(
-            shape(GROUPS, ADJ_ROWS + ROWS, CAPACITY),
-            shape(GROUPS, UNITS, CAPACITY, dtype=F32),
-            shape(GROUPS, ROWS, 2 * UNITS, dtype=F32),
-        ),
+        out_shape=shape(GROUPS, GRAPH_ROWS, CAPACITY),
         in_specs=[SMEM] * 2 + [VMEM] * 3,
-        out_specs=(VMEM,) * 3,
+        out_specs=VMEM,
         scratch_shapes=[pltpu.VMEM((2, SLOTS, 16, CAPACITY), BF16)],
         compiler_params=params(58),
         cost_estimate=cost(8 * 10**9, 8 * MIB),
     )(counts, offsets, slots, weight, upstream)
 
 
-def layers(core, counts, message, first, slots, bias, weight, upstream, adj, grad, degree):
+def layers(core, counts, message, first, slots, bias, weight, upstream, adj):
     shard = shape(Z, SHARD_ROWS, 2 * UNITS, dtype=F32)
     return pl.pallas_call(
         layer_kernel,
-        out_shape=(shard, shard, shape(CLASS_ROWS, GROUPS * TARGETS, dtype=F32)),
-        in_specs=[SMEM] * 2 + [VMEM] * 6 + [pl.BlockSpec(memory_space=pl.ANY)] * 3,
+        out_shape=(shard, shape(Z, SHARD_ROWS, 2 * UNITS), shape(CLASS_ROWS, GROUPS * TARGETS, dtype=F32)),
+        in_specs=[SMEM] * 2 + [VMEM] * 6 + [pl.BlockSpec(memory_space=pl.ANY)],
         out_specs=(VMEM, VMEM, VMEM),
         scratch_shapes=[
             pltpu.VMEM(adj.shape, BF16),
-            pltpu.VMEM(grad.shape, F32),
-            pltpu.VMEM(degree.shape, F32),
             pltpu.SemaphoreType.DMA((GROUPS, KINDS)),
-            pltpu.SemaphoreType.DMA((2,)),
             pltpu.VMEM((GROUPS, RELATIONS * WIDTH, CAPACITY), BF16),
             pltpu.VMEM((GROUPS, 2 * UNITS, CAPACITY), BF16),
             pltpu.VMEM((GROUPS, 2 * UNITS, CAPACITY), BF16),
@@ -372,17 +383,17 @@
         ],
         compiler_params=params(44),
         cost_estimate=cost(12 * 10**9, 12 * MIB),
-    )(core, counts, message, first, slots, bias, weight, upstream, adj, grad, degree)
-
-
-def merge(keep, received):
+    )(core, counts, message, first, slots, bias, weight, upstream, adj)
+
+
+def merge(core, keep, both):
     return pl.pallas_call(
         merge_kernel,
         out_shape=(shape(FEAT, FIRST_ROWS, 2 * UNITS), shape(Z, SECOND_ROWS, 2 * UNITS)),
-        in_specs=[VMEM] * 2,
+        in_specs=[SMEM] + [VMEM] * 2,
         out_specs=(VMEM,) * 2,
         compiler_params=params(8),
-    )(keep, received)
+    )(core, keep, both)
 
 
 def relay(message, second, score):
@@ -398,7 +409,7 @@
 def fold(pieces, scores):
     return pl.pallas_call(
         fold_kernel,
-        out_shape=(shape(Z, SHARD_ROWS, 2 * UNITS), shape(*scores[0].shape, dtype=F32)),
+        out_shape=(shape(BLOCKS, SHARD_ROWS, 2 * UNITS), shape(*scores[0].shape, dtype=F32)),
         in_specs=[VMEM] * 5,
         out_specs=(VMEM,) * 2,
         compiler_params=params(8),
@@ -449,7 +460,7 @@
     first = lax.all_gather(message[:, NODES:], "batch", axis_index_groups=chips)
     slots = jnp.swapaxes(adjacent_vertices, 2, 3)
     weight = weight_two.reshape(KINDS * UNITS, CLASSES)
-    adj, grad, degree = adjacency(node_counts, target_offsets, slots, weight, score_derivative)
+    adj = adjacency(node_counts, target_offsets, slots, weight, score_derivative)
     keep, send, score = layers(
         core,
         node_counts,
@@ -460,18 +471,18 @@
         weight,
         score_derivative,
         adj,
-        grad,
-        degree,
     )
-    received = lax.ppermute(send, "batch", [(i, i ^ 1) for i in range(Z * CORES)])
-    message, second = merge(keep, received)
+    both = lax.all_gather(send, "batch", axis_index_groups=chips)
+    message, second = merge(core, keep, both)
     message = lax.all_to_all(message, "feat", 0, 0)
     shards, score = relay(message, second, score)
     pieces = lax.all_to_all(shards, "batch", 0, 0, axis_index_groups=same_core)
     copies, score = fold(pieces, spread_out(score, row_hops))
-    shards = lax.all_to_all(copies, "batch", 0, 0, axis_index_groups=same_core)
+    blocks = [[block * BLOCK + i for i in range(BLOCK)] for block in range(BLOCKS)]
+    same_place = [[block * BLOCK + i for block in range(BLOCKS)] for i in range(BLOCK)]
+    shards = lax.all_to_all(copies, "batch", 0, 0, axis_index_groups=same_place)
     scores = spread_out(score, column_hops)
-    shards = lax.all_gather(shards, "batch", axis_index_groups=chips)
+    shards = lax.all_gather(shards, "batch", axis_index_groups=blocks)
     first_grad, second_grad, logits = unpack(shards, scores)
     return (logits.T, first_grad, second_grad)
 

time: 143 us -> 142 us (level)
  blocking collectives: 27.6 us -> 32.9 us
  waiting for transfers between devices: 27.1 us -> 23.3 us
  starting transfers between devices: 54.3 us -> 51.9 us
    all_gather x1 -> x2, blocking collectives: 9.15 us -> 14.5 us  [the longest x1 12.2 us: local(): shards = lax.all_gather(shards, 'batch', axis_index_groups=blocks)]
    ppermute x1 -> x0, starting transfers between devices: 2.29 us -> none  [local(): lax.ppermute(send, 'batch', [(i, i ^ 1) for i in range(Z * CORES)])]
    all_to_all x1, waiting for transfers between devices: 8.42 us -> 6.59 us  [local(): shards = lax.all_to_all(copies, 'batch', 0, 0, axis_index_groups=same_place)]
    ppermute x1 -> x0, waiting for transfers between devices: 1.8 us -> none  [local(): lax.ppermute(send, 'batch', [(i, i ^ 1) for i in range(Z * CORES)])]
  transfers between devices with their start and end apart: 10 -> 9, of which waited for: 6 -> 5; matrix products, arithmetic and copies ran while one was open for 1% -> 1% of each run, Pallas kernels for 9% -> 10%
where the time goes in v4:
time: 142 us
  starting transfers between devices  51.9 us (37%)
  blocking collectives  32.9 us (23%)
  Pallas kernels  31.8 us (22%)
  waiting for transfers between devices  23.3 us (16%)
    all_to_all x1, starting transfers between devices, local(): pieces = lax.all_to_all(shards, 'batch', 0, 0, axis_index_groups=same_core)  16.5 us
    ppermute x6, starting transfers between devices, spread_out(): lax.ppermute(score, 'feat', hops(step))  14.9 us
    pallas_call x1, Pallas kernels, adjacency(): pl.pallas_call(adjacency_kernel, out_shape=shape(GROUPS, GRAPH_ROWS, CAPA...  13.6 us
    pallas_call x1, Pallas kernels, layers(): pl.pallas_call(layer_kernel, out_shape=(shard, shape(Z, SHARD_ROWS, 2 * U...  12.8 us
    all_to_all x1, starting transfers between devices, local(): shards = lax.all_to_all(copies, 'batch', 0, 0, axis_index_groups=same_place)  12.8 us
    all_gather x1, blocking collectives, local(): shards = lax.all_gather(shards, 'batch', axis_index_groups=blocks)  12.2 us
    all_to_all x1, blocking collectives, local(): message = lax.all_to_all(message, 'feat', 0, 0)  11.2 us
    all_to_all x1, waiting for transfers between devices, local(): lax.all_to_all(pack(core, vertex_embeddings.T, weight_one), 'feat', 0, 0)  9.35 us
  transfers between devices with their start and end apart: 9, of which 5 were waited for; matrix products, arithmetic and copies ran while one was open for 1% of the time, Pallas kernels for 10%

profile of v4, /device:TPU:1, one launch (start us, length us, event | category | flops | bytes accessed | tf_op | source)
XLA Modules:
  0.0 141.6 jit_solution(14817472095028872876)
XLA Ops:
  0.6 2.4 %shard_map.103 = bf16[16,48,1280]{2,1,0:T(8,128)(2,1)} custom-call(s32[1]{0:T(128)} %bitcast.core_ref, bf16[48,1024]{1,0:T(8,128)(2,1)} %bitcast.19, bf16[6,48,1024]{2,1,0:T(8,128)(2,1)} %w_ref.1), custom_call_target="tpu_custom_call" | custom-call | tf_op jit(solution)/shard_map/pallas_call | solution.py:340
  3.0 0.0 copy-start.5
  3.0 0.0 copy-start.4
  3.1 7.7 %all-to-all-start = ((bf16[16,48,1280]{2,1,0:T(8,128)(2,1)}), bf16[16,48,1280]{2,1,0:T(8,128)(2,1)S(1)}, u32[]{:S(2)}, u32[]{:S(2)}) async-start(bf16[16,48,1280]{2,1,0:T(8,128)(2,1)} %shard_map.103), calls=%async_computation | async-start | bytes 3932160 | tf_op jit(solution)/shard_map/all_to_all | solution.py:458
  10.8 0.0 copy-done.5
  10.8 0.1 copy.15.bias_ref
  10.9 0.0 copy-done.4
  10.9 0.7 copy.16.upstream_ref
  11.6 13.6 %shard_map.104.adj_from = bf16[2,3104,512]{2,1,0:T(8,128)(2,1)} custom-call(s32[2]{0:T(128)} %counts_ref.3, s32[2]{0:T(128)} %offsets_ref.1, s32[2,5,8,512]{3,2,1,0:T(8,128)} %bitcast.17, bf16[384,153]{1,0:T(8,128)(2,1)} %bitcast.15, bf16[128,153]{1,0:T(8,128)(2,1)} %copy.16.upstream_ref), custom_call_target="tpu_custom_call" | custom-call | flops 8000000000 | bytes 8388608 | tf_op jit(solution)/shard_map/pallas_call | solution.py:358
  25.2 0.0 copy-start
  25.2 0.0 copy-start.1
  25.2 0.0 copy-start.2
  25.2 0.0 copy-start.3
  25.2 9.4 %all-to-all-done = bf16[16,48,1280]{2,1,0:T(8,128)(2,1)S(1)} async-done(((bf16[16,48,1280]{2,1,0:T(8,128)(2,1)}), bf16[16,48,1280]{2,1,0:T(8,128)(2,1)S(1)}, u32[]{:S(2)}, u32[]{:S(2)}) %all-to-all-start) | async-done | bytes 1966112 | tf_op jit(solution)/shard_map/all_to_all | solution.py:458
  34.6 7.3 %all-gather = bf16[1536,256]{1,0:T(8,128)(2,1)S(1)} all-gather(bf16[768,256]{1,0:T(8,128)(2,1)S(1)} %slice.4), channel_id=2, replica_groups={{0,16},{32,48},{64,80},{96,112},{128,144},{160,176},{192,208},{224,240}..., dimensions={0}, use_global_device_ids=true | all-gather | bytes 1179648 | tf_op jit(solution)/shard_map/all_gather | solution.py:460
  41.9 0.0 copy-done
  41.9 0.0 copy-done.1
  41.9 0.0 copy-done.2
  41.9 0.0 copy-done.3
  41.9 12.8 %shard_map.105 = (f32[16,88,128]{2,1,0:T(8,128)S(1)}, bf16[16,88,128]{2,1,0:T(8,128)(2,1)S(1)}, f32[160,128]{1,0:T(8,128)S(1)}) custom-call(s32[1]{0:T(128)} %bitcast.core_ref, s32[2]{0:T(128)S(1)} %copy-done.3, bf16[768,1280]{1,0:T(8,128)(2,1)S(1)} %bitcast.13, bf16[2,768,256]{2,1,0:T(8,128)(2,1)S(1)} %bitcast.14, s32[2,5,8,512]{3,2,1,0:T(8,128)S(1)} %bitcast.18, ...), custom_call_target="tpu_custom_call" | custom-call | flops 12000000000 | bytes 12582912 | tf_op jit(solution)/shard_map/pallas_call | solution.py:371
  54.7 2.3 %all-gather.1 = bf16[32,88,128]{2,1,0:T(8,128)(2,1)S(1)} all-gather(bf16[16,88,128]{2,1,0:T(8,128)(2,1)S(1)} %get-tuple-element.16), channel_id=3, replica_groups={{0,16},{32,48},{64,80},{96,112},{128,144},{160,176},{192,208},{224,240}..., dimensions={0}, use_global_device_ids=true | all-gather | bytes 1081344 | tf_op jit(solution)/shard_map/all_gather | solution.py:475
  57.1 0.1 shard_map.106
  57.1 11.2 %all_to_all.20.message_ref = bf16[16,72,128]{2,1,0:T(8,128)(2,1)S(1)} all-to-all(bf16[16,72,128]{2,1,0:T(8,128)(2,1)S(1)} %get-tuple-element.17), channel_id=1, replica_groups=mesh['batch'=32,'feat'=16] {'feat'}, dimensions={0} | all-to-all | bytes 589824 | tf_op jit(solution)/shard_map/all_to_all | solution.py:477
  68.3 0.8 shard_map.107
  69.1 16.5 %all-to-all-start.2 = ((bf16[16,88,128]{2,1,0:T(8,128)(2,1)}), bf16[16,88,128]{2,1,0:T(8,128)(2,1)S(1)}, u32[]{:S(2)}, u32[]{:S(2)}) async-start(bf16[16,88,128]{2,1,0:T(8,128)(2,1)} %get-tuple-element.20), calls=%async_computation.2 | async-start | bytes 720896 | tf_op jit(solution)/shard_map/all_to_all | solution.py:479
  85.6 1.9 %collective-permute-start.2 = (f32[160,128]{1,0:T(8,128)S(1)}, f32[160,128]{1,0:T(8,128)S(1)}, u32[]{:S(2)}, u32[]{:S(2)}) collective-permute-start(f32[160,128]{1,0:T(8,128)S(1)} %get-tuple-element.21.s0_ref), channel_id=1, source_target_pairs={{0,3},{1,0},{2,1},{3,2},{4,7},{5,4},{6,5},{7,6},{8,11},{9,8},{10,9... | collective-permute-start | bytes 245768 | tf_op jit(solution)/shard_map/ppermute | solution.py:428
  87.5 3.9 %collective-permute-start.1 = (f32[160,128]{1,0:T(8,128)S(1)}, f32[160,128]{1,0:T(8,128)S(1)}, u32[]{:S(2)}, u32[]{:S(2)}) collective-permute-start(f32[160,128]{1,0:T(8,128)S(1)} %get-tuple-element.21.s0_ref), channel_id=1, source_target_pairs={{0,2},{1,3},{2,0},{3,1},{4,6},{5,7},{6,4},{7,5},{8,10},{9,11},{10,... | collective-permute-start | bytes 245768 | tf_op jit(solution)/shard_map/ppermute | solution.py:428
  91.4 1.9 %collective-permute-start = (f32[160,128]{1,0:T(8,128)S(1)}, f32[160,128]{1,0:T(8,128)S(1)}, u32[]{:S(2)}, u32[]{:S(2)}) collective-permute-start(f32[160,128]{1,0:T(8,128)S(1)} %get-tuple-element.21.s0_ref), channel_id=1, source_target_pairs={{0,1},{1,2},{2,3},{3,0},{4,5},{5,6},{6,7},{7,4},{8,9},{9,10},{10,1... | collective-permute-start | bytes 245768 | tf_op jit(solution)/shard_map/ppermute | solution.py:428
  93.4 0.0 collective-permute-done.2.s3_ref
  93.4 1.1 collective-permute-done.1.s2_ref
  94.5 3.8 %collective-permute-done.s1_ref = f32[160,128]{1,0:T(8,128)S(1)} collective-permute-done((f32[160,128]{1,0:T(8,128)S(1)}, f32[160,128]{1,0:T(8,128)S(1)}, u32[]{:S(2)}, u32[]{:S(2)}) %collective-permute-start) | collective-permute-done | bytes 81952 | tf_op jit(solution)/shard_map/ppermute | solution.py:428
  98.3 2.4 %all-to-all-done.2.pieces_ref = bf16[16,88,128]{2,1,0:T(8,128)(2,1)S(1)} async-done(((bf16[16,88,128]{2,1,0:T(8,128)(2,1)}), bf16[16,88,128]{2,1,0:T(8,128)(2,1)S(1)}, u32[]{:S(2)}, u32[]{:S(2)}) %all-to-all-start.2) | async-done | bytes 360480 | tf_op jit(solution)/shard_map/all_to_all | solution.py:479
  100.7 0.7 shard_map.108
  101.4 12.8 %all-to-all-start.3 = ((bf16[8,88,128]{2,1,0:T(8,128)(2,1)}), bf16[8,88,128]{2,1,0:T(8,128)(2,1)S(1)}, u32[]{:S(2)}, u32[]{:S(2)}) async-start(bf16[8,88,128]{2,1,0:T(8,128)(2,1)} %get-tuple-element.22), calls=%async_computation.3 | async-start | bytes 360448 | tf_op jit(solution)/shard_map/all_to_all | solution.py:483
  114.2 2.5 %collective-permute-start.5 = (f32[160,128]{1,0:T(8,128)S(1)}, f32[160,128]{1,0:T(8,128)S(1)}, u32[]{:S(2)}, u32[]{:S(2)}) collective-permute-start(f32[160,128]{1,0:T(8,128)S(1)} %get-tuple-element.23.s0_ref), channel_id=1, source_target_pairs={{0,12},{1,13},{2,14},{3,15},{4,0},{5,1},{6,2},{7,3},{8,4},{9,5},{1... | collective-permute-start | bytes 245768 | tf_op jit(solution)/shard_map/ppermute | solution.py:428
  116.7 1.9 %collective-permute-start.4 = (f32[160,128]{1,0:T(8,128)S(1)}, f32[160,128]{1,0:T(8,128)S(1)}, u32[]{:S(2)}, u32[]{:S(2)}) collective-permute-start(f32[160,128]{1,0:T(8,128)S(1)} %get-tuple-element.23.s0_ref), channel_id=1, source_target_pairs={{0,8},{1,9},{2,10},{3,11},{4,12},{5,13},{6,14},{7,15},{8,0},{9,1},... | collective-permute-start | bytes 245768 | tf_op jit(solution)/shard_map/ppermute | solution.py:428
  118.6 2.8 %collective-permute-start.3 = (f32[160,128]{1,0:T(8,128)S(1)}, f32[160,128]{1,0:T(8,128)S(1)}, u32[]{:S(2)}, u32[]{:S(2)}) collective-permute-start(f32[160,128]{1,0:T(8,128)S(1)} %get-tuple-element.23.s0_ref), channel_id=1, source_target_pairs={{0,4},{1,5},{2,6},{3,7},{4,8},{5,9},{6,10},{7,11},{8,12},{9,13},{1... | collective-permute-start | bytes 245768 | tf_op jit(solution)/shard_map/ppermute | solution.py:428
  121.4 6.6 %all-to-all-done.3 = bf16[8,88,128]{2,1,0:T(8,128)(2,1)S(1)} async-done(((bf16[8,88,128]{2,1,0:T(8,128)(2,1)}), bf16[8,88,128]{2,1,0:T(8,128)(2,1)S(1)}, u32[]{:S(2)}, u32[]{:S(2)}) %all-to-all-start.3) | async-done | bytes 180256 | tf_op jit(solution)/shard_map/all_to_all | solution.py:483
  128.0 12.2 %all-gather.2 = bf16[32,88,128]{2,1,0:T(8,128)(2,1)S(1)} all-gather(bf16[8,88,128]{2,1,0:T(8,128)(2,1)S(1)} %all-to-all-done.3), channel_id=4, replica_groups={{0,16,32,48},{64,80,96,112},{128,144,160,176},{192,208,224,240},{256,27..., dimensions={0}, use_global_device_ids=true | all-gather | bytes 901120 | tf_op jit(solution)/shard_map/all_gather | solution.py:485
  140.2 0.0 collective-permute-done.5.s3_ref
  140.2 0.0 collective-permute-done.4.s2_ref
  140.2 0.0 collective-permute-done.3.s1_ref
  140.2 1.5 %shard_map.109 = (f32[6,48,1024]{2,1,0:T(8,128)}, f32[6,64,153]{2,1,0:T(8,128)}, f32[153,128]{1,0:T(8,128)}) custom-call(bf16[4,8,88,128]{3,2,1,0:T(8,128)(2,1)S(1)} %bitcast.10, f32[160,128]{1,0:T(8,128)S(1)} %get-tuple-element.23.s0_ref, f32[160,128]{1,0:T(8,128)S(1)} %collective-permute-done.3.s1_ref, f32[160,128]{1,0:T(8,128)S(1)} %collective-permute-done.4.s2_ref, ...), custom_call_target="tpu_custom_call" | custom-call | tf_op jit(solution)/shard_map/pallas_call | solution.py:432
  (1 shorter events, 0.0 us)
Async XLA Ops:
  3.0 7.8 %copy-start.5 = (f32[64]{0:T(128)S(1)}, f32[64]{0:T(128)}, u32[]{:S(2)}) copy-start(f32[64]{0:T(128)} %param.13) | copy-start | bytes 772
  3.0 7.9 %copy-start.4 = (bf16[128,153]{0,1:T(8,128)(2,1)S(1)}, bf16[128,153]{0,1:T(8,128)(2,1)}, u32[]{:S(2)}) copy-start(bf16[128,153]{0,1:T(8,128)(2,1)} %param.15) | copy-start | bytes 117508
  3.1 31.5 %all-to-all-start = ((bf16[16,48,1280]{2,1,0:T(8,128)(2,1)}), bf16[16,48,1280]{2,1,0:T(8,128)(2,1)S(1)}, u32[]{:S(2)}, u32[]{:S(2)}) async-start(bf16[16,48,1280]{2,1,0:T(8,128)(2,1)} %shard_map.103), calls=%async_computation | async-start | bytes 3932160 | tf_op jit(solution)/shard_map/all_to_all | solution.py:458
  25.2 16.7 %copy-start = (bf16[128,153]{1,0:T(8,128)(2,1)S(1)}, bf16[128,153]{1,0:T(8,128)(2,1)}, u32[]{:S(2)}) copy-start(bf16[128,153]{1,0:T(8,128)(2,1)} %copy.16.upstream_ref) | copy-start | bytes 117508
  25.2 16.7 %copy-start.1 = (bf16[6,64,153]{2,1,0:T(8,128)(2,1)S(1)}, bf16[6,64,153]{2,1,0:T(8,128)(2,1)}, u32[]{:S(2)}) copy-start(bf16[6,64,153]{2,1,0:T(8,128)(2,1)} %param.14) | copy-start | bytes 352516
  25.2 16.7 %copy-start.2 = (s32[2,5,512,8]{2,3,1,0:T(8,128)S(1)}, s32[2,5,512,8]{2,3,1,0:T(8,128)}, u32[]{:S(2)}) copy-start(s32[2,5,512,8]{2,3,1,0:T(8,128)} %param.9) | copy-start | bytes 491524
  25.2 16.7 %copy-start.3 = (s32[2]{0:T(128)S(1)}, s32[2]{0:T(128)}, u32[]{:S(2)}) copy-start(s32[2]{0:T(128)} %counts_ref.3) | copy-start | bytes 28
  69.1 31.6 %all-to-all-start.2 = ((bf16[16,88,128]{2,1,0:T(8,128)(2,1)}), bf16[16,88,128]{2,1,0:T(8,128)(2,1)S(1)}, u32[]{:S(2)}, u32[]{:S(2)}) async-start(bf16[16,88,128]{2,1,0:T(8,128)(2,1)} %get-tuple-element.20), calls=%async_computation.2 | async-start | bytes 720896 | tf_op jit(solution)/shard_map/all_to_all | solution.py:479
  85.6 7.8 %collective-permute-start.2 = (f32[160,128]{1,0:T(8,128)S(1)}, f32[160,128]{1,0:T(8,128)S(1)}, u32[]{:S(2)}, u32[]{:S(2)}) collective-permute-start(f32[160,128]{1,0:T(8,128)S(1)} %get-tuple-element.21.s0_ref), channel_id=1, source_target_pairs={{0,3},{1,0},{2,1},{3,2},{4,7},{5,4},{6,5},{7,6},{8,11},{9,8},{10,9... | collective-permute-start | bytes 245768 | tf_op jit(solution)/shard_map/ppermute | solution.py:428
  87.5 7.0 %collective-permute-start.1 = (f32[160,128]{1,0:T(8,128)S(1)}, f32[160,128]{1,0:T(8,128)S(1)}, u32[]{:S(2)}, u32[]{:S(2)}) collective-permute-start(f32[160,128]{1,0:T(8,128)S(1)} %get-tuple-element.21.s0_ref), channel_id=1, source_target_pairs={{0,2},{1,3},{2,0},{3,1},{4,6},{5,7},{6,4},{7,5},{8,10},{9,11},{10,... | collective-permute-start | bytes 245768 | tf_op jit(solution)/shard_map/ppermute | solution.py:428
  91.4 6.9 %collective-permute-start = (f32[160,128]{1,0:T(8,128)S(1)}, f32[160,128]{1,0:T(8,128)S(1)}, u32[]{:S(2)}, u32[]{:S(2)}) collective-permute-start(f32[160,128]{1,0:T(8,128)S(1)} %get-tuple-element.21.s0_ref), channel_id=1, source_target_pairs={{0,1},{1,2},{2,3},{3,0},{4,5},{5,6},{6,7},{7,4},{8,9},{9,10},{10,1... | collective-permute-start | bytes 245768 | tf_op jit(solution)/shard_map/ppermute | solution.py:428
  101.4 26.6 %all-to-all-start.3 = ((bf16[8,88,128]{2,1,0:T(8,128)(2,1)}), bf16[8,88,128]{2,1,0:T(8,128)(2,1)S(1)}, u32[]{:S(2)}, u32[]{:S(2)}) async-start(bf16[8,88,128]{2,1,0:T(8,128)(2,1)} %get-tuple-element.22), calls=%async_computation.3 | async-start | bytes 360448 | tf_op jit(solution)/shard_map/all_to_all | solution.py:483
  114.2 26.0 %collective-permute-start.5 = (f32[160,128]{1,0:T(8,128)S(1)}, f32[160,128]{1,0:T(8,128)S(1)}, u32[]{:S(2)}, u32[]{:S(2)}) collective-permute-start(f32[160,128]{1,0:T(8,128)S(1)} %get-tuple-element.23.s0_ref), channel_id=1, source_target_pairs={{0,12},{1,13},{2,14},{3,15},{4,0},{5,1},{6,2},{7,3},{8,4},{9,5},{1... | collective-permute-start | bytes 245768 | tf_op jit(solution)/shard_map/ppermute | solution.py:428
  116.7 23.5 %collective-permute-start.4 = (f32[160,128]{1,0:T(8,128)S(1)}, f32[160,128]{1,0:T(8,128)S(1)}, u32[]{:S(2)}, u32[]{:S(2)}) collective-permute-start(f32[160,128]{1,0:T(8,128)S(1)} %get-tuple-element.23.s0_ref), channel_id=1, source_target_pairs={{0,8},{1,9},{2,10},{3,11},{4,12},{5,13},{6,14},{7,15},{8,0},{9,1},... | collective-permute-start | bytes 245768 | tf_op jit(solution)/shard_map/ppermute | solution.py:428
  118.6 21.6 %collective-permute-start.3 = (f32[160,128]{1,0:T(8,128)S(1)}, f32[160,128]{1,0:T(8,128)S(1)}, u32[]{:S(2)}, u32[]{:S(2)}) collective-permute-start(f32[160,128]{1,0:T(8,128)S(1)} %get-tuple-element.23.s0_ref), channel_id=1, source_target_pairs={{0,4},{1,5},{2,6},{3,7},{4,8},{5,9},{6,10},{7,11},{8,12},{9,13},{1... | collective-permute-start | bytes 245768 | tf_op jit(solution)/shard_map/ppermute | solution.py:428

commit v5 on v4

--- a/solution.py
+++ b/solution.py
@@ -294,20 +294,37 @@
     score_ref[...] = s0_ref[...] + s1_ref[...] + s2_ref[...] + s3_ref[...]
 
 
-def unpack_kernel(shards_ref, s0_ref, s1_ref, s2_ref, s3_ref, first_ref, second_ref, logits_ref):
+def unpack_kernel(
+    shards_ref,
+    s0_ref,
+    s1_ref,
+    s2_ref,
+    s3_ref,
+    first_to,
+    second_to,
+    logits_ref,
+    first_ref,
+    second_ref,
+    first_sem,
+    second_sem,
+):
     low = low_half(HALF)
-    for tile in range(FEAT // 2):
-        lanes = pl.ds(tile * 2 * UNITS, 2 * UNITS)
-        for part in range(CORES):
-            left = shards_ref[part, tile].astype(F32)
-            right = shards_ref[CORES + part, tile].astype(F32)
-            rows = pl.ds(part * HALF, HALF)
-            for pair in range(PAIRS):
+    stores = []
+    for pair in range(PAIRS):
+        for tile in range(FEAT // 2):
+            lanes = pl.ds(tile * 2 * UNITS, 2 * UNITS)
+            for part in range(CORES):
+                left = shards_ref[part, tile].astype(F32)
+                right = shards_ref[CORES + part, tile].astype(F32)
+                rows = pl.ds(part * HALF, HALF)
                 start = SECOND_ROWS + pair * HALF
                 a = left[start : start + HALF]
                 b = right[start : start + HALF]
                 first_ref[2 * pair, rows, lanes] = jnp.where(low, a, swap_halves(b))
                 first_ref[2 * pair + 1, rows, lanes] = jnp.where(low, swap_halves(a), b)
+        both = pl.ds(2 * pair, 2)
+        stores.append(pltpu.make_async_copy(first_ref.at[both], first_to.at[both], first_sem.at[pair]))
+        stores[-1].start()
     packed = jnp.stack([shards_ref[part, :, :SECOND_ROWS, :] for part in range(BLOCK)], axis=1)
     packed = packed.reshape(Z * CORES * SECOND_ROWS, 2 * UNITS)
     identity = eye(2 * UNITS)
@@ -316,7 +333,11 @@
         turned = dot(identity, block, (1, 1))
         second_ref[2 * pair] = turned[:UNITS, :CLASSES]
         second_ref[2 * pair + 1] = turned[UNITS:, :CLASSES]
+    stores.append(pltpu.make_async_copy(second_ref, second_to, second_sem))
+    stores[-1].start()
     logits_ref[...] = (s0_ref[...] + s1_ref[...] + s2_ref[...] + s3_ref[...])[:CLASSES]
+    for store in stores:
+        store.wait()
 
 
 VMEM = pl.BlockSpec(memory_space=pltpu.VMEM)
@@ -437,7 +458,13 @@
             shape(CLASSES, GROUPS * TARGETS, dtype=F32),
         ),
         in_specs=[VMEM] * 5,
-        out_specs=(VMEM, VMEM, VMEM),
+        out_specs=(pl.BlockSpec(memory_space=pl.ANY), pl.BlockSpec(memory_space=pl.ANY), VMEM),
+        scratch_shapes=[
+            pltpu.VMEM((KINDS, COLUMNS, HIDDEN), F32),
+            pltpu.VMEM((KINDS, UNITS, CLASSES), F32),
+            pltpu.SemaphoreType.DMA((PAIRS,)),
+            pltpu.SemaphoreType.DMA,
+        ],
         compiler_params=params(8),
     )(shards, *scores)
 

time: 142 us -> 143 us (level)
  no operation moved by 1% of the time
where the time goes in v5:
time: 143 us; the launch traced here: 142 us
  starting transfers between devices  51.9 us (36%)
  blocking collectives  32.9 us (23%)
  Pallas kernels  32.3 us (23%)
  waiting for transfers between devices  23.3 us (16%)
    all_to_all x1, starting transfers between devices, local(): pieces = lax.all_to_all(shards, 'batch', 0, 0, axis_index_groups=same_core)  16.5 us
    ppermute x6, starting transfers between devices, spread_out(): lax.ppermute(score, 'feat', hops(step))  14.9 us
    pallas_call x1, Pallas kernels, adjacency(): pl.pallas_call(adjacency_kernel, out_shape=shape(GROUPS, GRAPH_ROWS, CAPA...  13.6 us
    pallas_call x1, Pallas kernels, layers(): pl.pallas_call(layer_kernel, out_shape=(shard, shape(Z, SHARD_ROWS, 2 * U...  12.8 us
    all_to_all x1, starting transfers between devices, local(): shards = lax.all_to_all(copies, 'batch', 0, 0, axis_index_groups=same_place)  12.8 us
    all_gather x1, blocking collectives, local(): shards = lax.all_gather(shards, 'batch', axis_index_groups=blocks)  12.2 us
    all_to_all x1, blocking collectives, local(): message = lax.all_to_all(message, 'feat', 0, 0)  11.2 us
    all_to_all x1, waiting for transfers between devices, local(): lax.all_to_all(pack(core, vertex_embeddings.T, weight_one), 'feat', 0, 0)  9.35 us
  transfers between devices with their start and end apart: 9, of which 5 were waited for; matrix products, arithmetic and copies ran while one was open for 1% of the time, Pallas kernels for 10%

profile of v5, /device:TPU:1, one launch (start us, length us, event | category | flops | bytes accessed | tf_op | source)
XLA Modules:
  0.0 142.1 jit_solution(128785770798119260)
XLA Ops:
  0.6 2.4 %shard_map.103 = bf16[16,48,1280]{2,1,0:T(8,128)(2,1)} custom-call(s32[1]{0:T(128)} %bitcast.core_ref, bf16[48,1024]{1,0:T(8,128)(2,1)} %bitcast.19, bf16[6,48,1024]{2,1,0:T(8,128)(2,1)} %w_ref.1), custom_call_target="tpu_custom_call" | custom-call | tf_op jit(solution)/shard_map/pallas_call | solution.py:361
  3.0 0.0 copy-start.5
  3.0 0.0 copy-start.4
  3.1 7.7 %all-to-all-start = ((bf16[16,48,1280]{2,1,0:T(8,128)(2,1)}), bf16[16,48,1280]{2,1,0:T(8,128)(2,1)S(1)}, u32[]{:S(2)}, u32[]{:S(2)}) async-start(bf16[16,48,1280]{2,1,0:T(8,128)(2,1)} %shard_map.103), calls=%async_computation | async-start | bytes 3932160 | tf_op jit(solution)/shard_map/all_to_all | solution.py:485
  10.8 0.0 copy-done.5
  10.8 0.1 copy.15.bias_ref
  10.9 0.0 copy-done.4
  10.9 0.7 copy.16.upstream_ref
  11.6 13.6 %shard_map.104.adj_from = bf16[2,3104,512]{2,1,0:T(8,128)(2,1)} custom-call(s32[2]{0:T(128)} %counts_ref.3, s32[2]{0:T(128)} %offsets_ref.1, s32[2,5,8,512]{3,2,1,0:T(8,128)} %bitcast.17, bf16[384,153]{1,0:T(8,128)(2,1)} %bitcast.15, bf16[128,153]{1,0:T(8,128)(2,1)} %copy.16.upstream_ref), custom_call_target="tpu_custom_call" | custom-call | flops 8000000000 | bytes 8388608 | tf_op jit(solution)/shard_map/pallas_call | solution.py:379
  25.2 0.0 copy-start
  25.2 0.0 copy-start.1
  25.2 0.0 copy-start.2
  25.2 0.0 copy-start.3
  25.2 9.4 %all-to-all-done = bf16[16,48,1280]{2,1,0:T(8,128)(2,1)S(1)} async-done(((bf16[16,48,1280]{2,1,0:T(8,128)(2,1)}), bf16[16,48,1280]{2,1,0:T(8,128)(2,1)S(1)}, u32[]{:S(2)}, u32[]{:S(2)}) %all-to-all-start) | async-done | bytes 1966112 | tf_op jit(solution)/shard_map/all_to_all | solution.py:485
  34.6 7.3 %all-gather = bf16[1536,256]{1,0:T(8,128)(2,1)S(1)} all-gather(bf16[768,256]{1,0:T(8,128)(2,1)S(1)} %slice.4), channel_id=2, replica_groups={{0,16},{32,48},{64,80},{96,112},{128,144},{160,176},{192,208},{224,240}..., dimensions={0}, use_global_device_ids=true | all-gather | bytes 1179648 | tf_op jit(solution)/shard_map/all_gather | solution.py:487
  41.9 0.0 copy-done
  41.9 0.0 copy-done.1
  41.9 0.0 copy-done.2
  41.9 0.0 copy-done.3
  41.9 12.8 %shard_map.105 = (f32[16,88,128]{2,1,0:T(8,128)S(1)}, bf16[16,88,128]{2,1,0:T(8,128)(2,1)S(1)}, f32[160,128]{1,0:T(8,128)S(1)}) custom-call(s32[1]{0:T(128)} %bitcast.core_ref, s32[2]{0:T(128)S(1)} %copy-done.3, bf16[768,1280]{1,0:T(8,128)(2,1)S(1)} %bitcast.13, bf16[2,768,256]{2,1,0:T(8,128)(2,1)S(1)} %bitcast.14, s32[2,5,8,512]{3,2,1,0:T(8,128)S(1)} %bitcast.18, ...), custom_call_target="tpu_custom_call" | custom-call | flops 12000000000 | bytes 12582912 | tf_op jit(solution)/shard_map/pallas_call | solution.py:392
  54.7 2.3 %all-gather.1 = bf16[32,88,128]{2,1,0:T(8,128)(2,1)S(1)} all-gather(bf16[16,88,128]{2,1,0:T(8,128)(2,1)S(1)} %get-tuple-element.16), channel_id=3, replica_groups={{0,16},{32,48},{64,80},{96,112},{128,144},{160,176},{192,208},{224,240}..., dimensions={0}, use_global_device_ids=true | all-gather | bytes 1081344 | tf_op jit(solution)/shard_map/all_gather | solution.py:502
  57.1 0.1 shard_map.106
  57.1 11.2 %all_to_all.20.message_ref = bf16[16,72,128]{2,1,0:T(8,128)(2,1)S(1)} all-to-all(bf16[16,72,128]{2,1,0:T(8,128)(2,1)S(1)} %get-tuple-element.17), channel_id=1, replica_groups=mesh['batch'=32,'feat'=16] {'feat'}, dimensions={0} | all-to-all | bytes 589824 | tf_op jit(solution)/shard_map/all_to_all | solution.py:504
  68.3 0.8 shard_map.107
  69.1 16.5 %all-to-all-start.2 = ((bf16[16,88,128]{2,1,0:T(8,128)(2,1)}), bf16[16,88,128]{2,1,0:T(8,128)(2,1)S(1)}, u32[]{:S(2)}, u32[]{:S(2)}) async-start(bf16[16,88,128]{2,1,0:T(8,128)(2,1)} %get-tuple-element.20), calls=%async_computation.2 | async-start | bytes 720896 | tf_op jit(solution)/shard_map/all_to_all | solution.py:506
  85.6 1.9 %collective-permute-start.2 = (f32[160,128]{1,0:T(8,128)S(1)}, f32[160,128]{1,0:T(8,128)S(1)}, u32[]{:S(2)}, u32[]{:S(2)}) collective-permute-start(f32[160,128]{1,0:T(8,128)S(1)} %get-tuple-element.21.s0_ref), channel_id=1, source_target_pairs={{0,3},{1,0},{2,1},{3,2},{4,7},{5,4},{6,5},{7,6},{8,11},{9,8},{10,9... | collective-permute-start | bytes 245768 | tf_op jit(solution)/shard_map/ppermute | solution.py:449
  87.5 3.9 %collective-permute-start.1 = (f32[160,128]{1,0:T(8,128)S(1)}, f32[160,128]{1,0:T(8,128)S(1)}, u32[]{:S(2)}, u32[]{:S(2)}) collective-permute-start(f32[160,128]{1,0:T(8,128)S(1)} %get-tuple-element.21.s0_ref), channel_id=1, source_target_pairs={{0,2},{1,3},{2,0},{3,1},{4,6},{5,7},{6,4},{7,5},{8,10},{9,11},{10,... | collective-permute-start | bytes 245768 | tf_op jit(solution)/shard_map/ppermute | solution.py:449
  91.4 1.9 %collective-permute-start = (f32[160,128]{1,0:T(8,128)S(1)}, f32[160,128]{1,0:T(8,128)S(1)}, u32[]{:S(2)}, u32[]{:S(2)}) collective-permute-start(f32[160,128]{1,0:T(8,128)S(1)} %get-tuple-element.21.s0_ref), channel_id=1, source_target_pairs={{0,1},{1,2},{2,3},{3,0},{4,5},{5,6},{6,7},{7,4},{8,9},{9,10},{10,1... | collective-permute-start | bytes 245768 | tf_op jit(solution)/shard_map/ppermute | solution.py:449
  93.4 0.0 collective-permute-done.2.s3_ref
  93.4 1.1 collective-permute-done.1.s2_ref
  94.5 3.8 %collective-permute-done.s1_ref = f32[160,128]{1,0:T(8,128)S(1)} collective-permute-done((f32[160,128]{1,0:T(8,128)S(1)}, f32[160,128]{1,0:T(8,128)S(1)}, u32[]{:S(2)}, u32[]{:S(2)}) %collective-permute-start) | collective-permute-done | bytes 81952 | tf_op jit(solution)/shard_map/ppermute | solution.py:449
  98.3 2.4 %all-to-all-done.2.pieces_ref = bf16[16,88,128]{2,1,0:T(8,128)(2,1)S(1)} async-done(((bf16[16,88,128]{2,1,0:T(8,128)(2,1)}), bf16[16,88,128]{2,1,0:T(8,128)(2,1)S(1)}, u32[]{:S(2)}, u32[]{:S(2)}) %all-to-all-start.2) | async-done | bytes 360480 | tf_op jit(solution)/shard_map/all_to_all | solution.py:506
  100.7 0.7 shard_map.108
  101.4 12.8 %all-to-all-start.3 = ((bf16[8,88,128]{2,1,0:T(8,128)(2,1)}), bf16[8,88,128]{2,1,0:T(8,128)(2,1)S(1)}, u32[]{:S(2)}, u32[]{:S(2)}) async-start(bf16[8,88,128]{2,1,0:T(8,128)(2,1)} %get-tuple-element.22), calls=%async_computation.3 | async-start | bytes 360448 | tf_op jit(solution)/shard_map/all_to_all | solution.py:510
  114.2 2.5 %collective-permute-start.5 = (f32[160,128]{1,0:T(8,128)S(1)}, f32[160,128]{1,0:T(8,128)S(1)}, u32[]{:S(2)}, u32[]{:S(2)}) collective-permute-start(f32[160,128]{1,0:T(8,128)S(1)} %get-tuple-element.23.s0_ref), channel_id=1, source_target_pairs={{0,12},{1,13},{2,14},{3,15},{4,0},{5,1},{6,2},{7,3},{8,4},{9,5},{1... | collective-permute-start | bytes 245768 | tf_op jit(solution)/shard_map/ppermute | solution.py:449
  116.7 1.9 %collective-permute-start.4 = (f32[160,128]{1,0:T(8,128)S(1)}, f32[160,128]{1,0:T(8,128)S(1)}, u32[]{:S(2)}, u32[]{:S(2)}) collective-permute-start(f32[160,128]{1,0:T(8,128)S(1)} %get-tuple-element.23.s0_ref), channel_id=1, source_target_pairs={{0,8},{1,9},{2,10},{3,11},{4,12},{5,13},{6,14},{7,15},{8,0},{9,1},... | collective-permute-start | bytes 245768 | tf_op jit(solution)/shard_map/ppermute | solution.py:449
  118.6 2.8 %collective-permute-start.3 = (f32[160,128]{1,0:T(8,128)S(1)}, f32[160,128]{1,0:T(8,128)S(1)}, u32[]{:S(2)}, u32[]{:S(2)}) collective-permute-start(f32[160,128]{1,0:T(8,128)S(1)} %get-tuple-element.23.s0_ref), channel_id=1, source_target_pairs={{0,4},{1,5},{2,6},{3,7},{4,8},{5,9},{6,10},{7,11},{8,12},{9,13},{1... | collective-permute-start | bytes 245768 | tf_op jit(solution)/shard_map/ppermute | solution.py:449
  121.4 6.6 %all-to-all-done.3 = bf16[8,88,128]{2,1,0:T(8,128)(2,1)S(1)} async-done(((bf16[8,88,128]{2,1,0:T(8,128)(2,1)}), bf16[8,88,128]{2,1,0:T(8,128)(2,1)S(1)}, u32[]{:S(2)}, u32[]{:S(2)}) %all-to-all-start.3) | async-done | bytes 180256 | tf_op jit(solution)/shard_map/all_to_all | solution.py:510
  128.0 12.2 %all-gather.2 = bf16[32,88,128]{2,1,0:T(8,128)(2,1)S(1)} all-gather(bf16[8,88,128]{2,1,0:T(8,128)(2,1)S(1)} %all-to-all-done.3), channel_id=4, replica_groups={{0,16,32,48},{64,80,96,112},{128,144,160,176},{192,208,224,240},{256,27..., dimensions={0}, use_global_device_ids=true | all-gather | bytes 901120 | tf_op jit(solution)/shard_map/all_gather | solution.py:512
  140.2 0.0 collective-permute-done.5.s3_ref
  140.2 0.0 collective-permute-done.4.s2_ref
  140.2 0.0 collective-permute-done.3.s1_ref
  140.2 2.0 %shard_map.109 = (f32[6,48,1024]{2,1,0:T(8,128)}, f32[6,64,153]{2,1,0:T(8,128)}, f32[153,128]{1,0:T(8,128)}) custom-call(bf16[4,8,88,128]{3,2,1,0:T(8,128)(2,1)S(1)} %bitcast.10, f32[160,128]{1,0:T(8,128)S(1)} %get-tuple-element.23.s0_ref, f32[160,128]{1,0:T(8,128)S(1)} %collective-permute-done.3.s1_ref, f32[160,128]{1,0:T(8,128)S(1)} %collective-permute-done.4.s2_ref, ...), custom_call_target="tpu_custom_call" | custom-call | tf_op jit(solution)/shard_map/pallas_call | solution.py:453
  (1 shorter events, 0.0 us)
Async XLA Ops:
  3.0 7.8 %copy-start.5 = (f32[64]{0:T(128)S(1)}, f32[64]{0:T(128)}, u32[]{:S(2)}) copy-start(f32[64]{0:T(128)} %param.13) | copy-start | bytes 772
  3.0 7.9 %copy-start.4 = (bf16[128,153]{0,1:T(8,128)(2,1)S(1)}, bf16[128,153]{0,1:T(8,128)(2,1)}, u32[]{:S(2)}) copy-start(bf16[128,153]{0,1:T(8,128)(2,1)} %param.15) | copy-start | bytes 117508
  3.1 31.5 %all-to-all-start = ((bf16[16,48,1280]{2,1,0:T(8,128)(2,1)}), bf16[16,48,1280]{2,1,0:T(8,128)(2,1)S(1)}, u32[]{:S(2)}, u32[]{:S(2)}) async-start(bf16[16,48,1280]{2,1,0:T(8,128)(2,1)} %shard_map.103), calls=%async_computation | async-start | bytes 3932160 | tf_op jit(solution)/shard_map/all_to_all | solution.py:485
  25.2 16.7 %copy-start = (bf16[128,153]{1,0:T(8,128)(2,1)S(1)}, bf16[128,153]{1,0:T(8,128)(2,1)}, u32[]{:S(2)}) copy-start(bf16[128,153]{1,0:T(8,128)(2,1)} %copy.16.upstream_ref) | copy-start | bytes 117508
  25.2 16.7 %copy-start.1 = (bf16[6,64,153]{2,1,0:T(8,128)(2,1)S(1)}, bf16[6,64,153]{2,1,0:T(8,128)(2,1)}, u32[]{:S(2)}) copy-start(bf16[6,64,153]{2,1,0:T(8,128)(2,1)} %param.14) | copy-start | bytes 352516
  25.2 16.7 %copy-start.2 = (s32[2,5,512,8]{2,3,1,0:T(8,128)S(1)}, s32[2,5,512,8]{2,3,1,0:T(8,128)}, u32[]{:S(2)}) copy-start(s32[2,5,512,8]{2,3,1,0:T(8,128)} %param.9) | copy-start | bytes 491524
  25.2 16.7 %copy-start.3 = (s32[2]{0:T(128)S(1)}, s32[2]{0:T(128)}, u32[]{:S(2)}) copy-start(s32[2]{0:T(128)} %counts_ref.3) | copy-start | bytes 28
  69.1 31.6 %all-to-all-start.2 = ((bf16[16,88,128]{2,1,0:T(8,128)(2,1)}), bf16[16,88,128]{2,1,0:T(8,128)(2,1)S(1)}, u32[]{:S(2)}, u32[]{:S(2)}) async-start(bf16[16,88,128]{2,1,0:T(8,128)(2,1)} %get-tuple-element.20), calls=%async_computation.2 | async-start | bytes 720896 | tf_op jit(solution)/shard_map/all_to_all | solution.py:506
  85.6 7.8 %collective-permute-start.2 = (f32[160,128]{1,0:T(8,128)S(1)}, f32[160,128]{1,0:T(8,128)S(1)}, u32[]{:S(2)}, u32[]{:S(2)}) collective-permute-start(f32[160,128]{1,0:T(8,128)S(1)} %get-tuple-element.21.s0_ref), channel_id=1, source_target_pairs={{0,3},{1,0},{2,1},{3,2},{4,7},{5,4},{6,5},{7,6},{8,11},{9,8},{10,9... | collective-permute-start | bytes 245768 | tf_op jit(solution)/shard_map/ppermute | solution.py:449
  87.5 7.0 %collective-permute-start.1 = (f32[160,128]{1,0:T(8,128)S(1)}, f32[160,128]{1,0:T(8,128)S(1)}, u32[]{:S(2)}, u32[]{:S(2)}) collective-permute-start(f32[160,128]{1,0:T(8,128)S(1)} %get-tuple-element.21.s0_ref), channel_id=1, source_target_pairs={{0,2},{1,3},{2,0},{3,1},{4,6},{5,7},{6,4},{7,5},{8,10},{9,11},{10,... | collective-permute-start | bytes 245768 | tf_op jit(solution)/shard_map/ppermute | solution.py:449
  91.4 6.9 %collective-permute-start = (f32[160,128]{1,0:T(8,128)S(1)}, f32[160,128]{1,0:T(8,128)S(1)}, u32[]{:S(2)}, u32[]{:S(2)}) collective-permute-start(f32[160,128]{1,0:T(8,128)S(1)} %get-tuple-element.21.s0_ref), channel_id=1, source_target_pairs={{0,1},{1,2},{2,3},{3,0},{4,5},{5,6},{6,7},{7,4},{8,9},{9,10},{10,1... | collective-permute-start | bytes 245768 | tf_op jit(solution)/shard_map/ppermute | solution.py:449
  101.4 26.6 %all-to-all-start.3 = ((bf16[8,88,128]{2,1,0:T(8,128)(2,1)}), bf16[8,88,128]{2,1,0:T(8,128)(2,1)S(1)}, u32[]{:S(2)}, u32[]{:S(2)}) async-start(bf16[8,88,128]{2,1,0:T(8,128)(2,1)} %get-tuple-element.22), calls=%async_computation.3 | async-start | bytes 360448 | tf_op jit(solution)/shard_map/all_to_all | solution.py:510
  114.2 26.0 %collective-permute-start.5 = (f32[160,128]{1,0:T(8,128)S(1)}, f32[160,128]{1,0:T(8,128)S(1)}, u32[]{:S(2)}, u32[]{:S(2)}) collective-permute-start(f32[160,128]{1,0:T(8,128)S(1)} %get-tuple-element.23.s0_ref), channel_id=1, source_target_pairs={{0,12},{1,13},{2,14},{3,15},{4,0},{5,1},{6,2},{7,3},{8,4},{9,5},{1... | collective-permute-start | bytes 245768 | tf_op jit(solution)/shard_map/ppermute | solution.py:449
  116.7 23.5 %collective-permute-start.4 = (f32[160,128]{1,0:T(8,128)S(1)}, f32[160,128]{1,0:T(8,128)S(1)}, u32[]{:S(2)}, u32[]{:S(2)}) collective-permute-start(f32[160,128]{1,0:T(8,128)S(1)} %get-tuple-element.23.s0_ref), channel_id=1, source_target_pairs={{0,8},{1,9},{2,10},{3,11},{4,12},{5,13},{6,14},{7,15},{8,0},{9,1},... | collective-permute-start | bytes 245768 | tf_op jit(solution)/shard_map/ppermute | solution.py:449
  118.6 21.6 %collective-permute-start.3 = (f32[160,128]{1,0:T(8,128)S(1)}, f32[160,128]{1,0:T(8,128)S(1)}, u32[]{:S(2)}, u32[]{:S(2)}) collective-permute-start(f32[160,128]{1,0:T(8,128)S(1)} %get-tuple-element.23.s0_ref), channel_id=1, source_target_pairs={{0,4},{1,5},{2,6},{3,7},{4,8},{5,9},{6,10},{7,11},{8,12},{9,13},{1... | collective-permute-start | bytes 245768 | tf_op jit(solution)/shard_map/ppermute | solution.py:449

commit v6 on v4

--- a/solution.py
+++ b/solution.py
@@ -85,8 +85,16 @@
         packed_ref[2 * tile, :, back] = third.astype(BF16)
         packed_ref[2 * tile + 1, :, front] = jnp.where(low, swap_halves(first), second).astype(BF16)
         packed_ref[2 * tile + 1, :, back] = swap_halves(third).astype(BF16)
-    stores.append(pltpu.make_async_copy(packed_ref, out_ref.at[:, :, pl.ds(NODES, WEIGHT_LANES)], out_sem))
-    stores[-1].start()
+        if tile % 2:
+            dests = pl.ds(2 * tile - 2, 4)
+            stores.append(
+                pltpu.make_async_copy(
+                    packed_ref.at[dests],
+                    out_ref.at[dests, :, pl.ds(NODES, WEIGHT_LANES)],
+                    out_sem.at[tile // 2],
+                )
+            )
+            stores[-1].start()
     for store in stores:
         store.wait()
 
@@ -348,7 +356,7 @@
             pltpu.VMEM((FEAT, COLUMNS, WEIGHT_LANES), BF16),
             pltpu.SemaphoreType.DMA((PAIRS + 1,)),
             pltpu.SemaphoreType.DMA((FEAT,)),
-            pltpu.SemaphoreType.DMA,
+            pltpu.SemaphoreType.DMA((FEAT // 4,)),
         ],
         compiler_params=params(58),
     )(core, x, w)

time: 142 us -> 142 us (level)
  no operation moved by 1% of the time
where the time goes in v6:
time: 142 us
  starting transfers between devices  52 us (37%)
  blocking collectives  32.9 us (23%)
  Pallas kernels  31.9 us (22%)
  waiting for transfers between devices  23.3 us (16%)
    all_to_all x1, starting transfers between devices, local(): pieces = lax.all_to_all(shards, 'batch', 0, 0, axis_index_groups=same_core)  16.5 us
    ppermute x6, starting transfers between devices, spread_out(): lax.ppermute(score, 'feat', hops(step))  14.9 us
    pallas_call x1, Pallas kernels, adjacency(): pl.pallas_call(adjacency_kernel, out_shape=shape(GROUPS, GRAPH_ROWS, CAPA...  13.6 us
    pallas_call x1, Pallas kernels, layers(): pl.pallas_call(layer_kernel, out_shape=(shard, shape(Z, SHARD_ROWS, 2 * U...  12.8 us
    all_to_all x1, starting transfers between devices, local(): shards = lax.all_to_all(copies, 'batch', 0, 0, axis_index_groups=same_place)  12.8 us
    all_gather x1, blocking collectives, local(): shards = lax.all_gather(shards, 'batch', axis_index_groups=blocks)  12.2 us
    all_to_all x1, blocking collectives, local(): message = lax.all_to_all(message, 'feat', 0, 0)  11.2 us
    all_to_all x1, waiting for transfers between devices, local(): lax.all_to_all(pack(core, vertex_embeddings.T, weight_one), 'feat', 0, 0)  9.35 us
  transfers between devices with their start and end apart: 9, of which 5 were waited for; matrix products, arithmetic and copies ran while one was open for 1% of the time, Pallas kernels for 10%

profile of v6, /device:TPU:1, one launch (start us, length us, event | category | flops | bytes accessed | tf_op | source)
XLA Modules:
  0.0 141.7 jit_solution(5664750704787193554)
XLA Ops:
  0.6 2.4 %shard_map.103 = bf16[16,48,1280]{2,1,0:T(8,128)(2,1)} custom-call(s32[1]{0:T(128)} %bitcast.core_ref, bf16[48,1024]{1,0:T(8,128)(2,1)} %bitcast.19, bf16[6,48,1024]{2,1,0:T(8,128)(2,1)} %w_ref.1), custom_call_target="tpu_custom_call" | custom-call | tf_op jit(solution)/shard_map/pallas_call | solution.py:348
  3.1 0.0 copy-start.5
  3.1 0.0 copy-start.4
  3.1 7.7 %all-to-all-start = ((bf16[16,48,1280]{2,1,0:T(8,128)(2,1)}), bf16[16,48,1280]{2,1,0:T(8,128)(2,1)S(1)}, u32[]{:S(2)}, u32[]{:S(2)}) async-start(bf16[16,48,1280]{2,1,0:T(8,128)(2,1)} %shard_map.103), calls=%async_computation | async-start | bytes 3932160 | tf_op jit(solution)/shard_map/all_to_all | solution.py:466
  10.8 0.0 copy-done.5
  10.8 0.1 copy.15.bias_ref
  10.9 0.0 copy-done.4
  10.9 0.7 copy.16.upstream_ref
  11.7 13.6 %shard_map.104.adj_from = bf16[2,3104,512]{2,1,0:T(8,128)(2,1)} custom-call(s32[2]{0:T(128)} %counts_ref.3, s32[2]{0:T(128)} %offsets_ref.1, s32[2,5,8,512]{3,2,1,0:T(8,128)} %bitcast.17, bf16[384,153]{1,0:T(8,128)(2,1)} %bitcast.15, bf16[128,153]{1,0:T(8,128)(2,1)} %copy.16.upstream_ref), custom_call_target="tpu_custom_call" | custom-call | flops 8000000000 | bytes 8388608 | tf_op jit(solution)/shard_map/pallas_call | solution.py:366
  25.2 0.0 copy-start
  25.2 0.0 copy-start.1
  25.2 0.0 copy-start.2
  25.3 0.0 copy-start.3
  25.3 9.4 %all-to-all-done = bf16[16,48,1280]{2,1,0:T(8,128)(2,1)S(1)} async-done(((bf16[16,48,1280]{2,1,0:T(8,128)(2,1)}), bf16[16,48,1280]{2,1,0:T(8,128)(2,1)S(1)}, u32[]{:S(2)}, u32[]{:S(2)}) %all-to-all-start) | async-done | bytes 1966112 | tf_op jit(solution)/shard_map/all_to_all | solution.py:466
  34.6 7.3 %all-gather = bf16[1536,256]{1,0:T(8,128)(2,1)S(1)} all-gather(bf16[768,256]{1,0:T(8,128)(2,1)S(1)} %slice.4), channel_id=2, replica_groups={{0,16},{32,48},{64,80},{96,112},{128,144},{160,176},{192,208},{224,240}..., dimensions={0}, use_global_device_ids=true | all-gather | bytes 1179648 | tf_op jit(solution)/shard_map/all_gather | solution.py:468
  41.9 0.0 copy-done
  41.9 0.0 copy-done.1
  41.9 0.0 copy-done.2
  41.9 0.0 copy-done.3
  41.9 12.8 %shard_map.105 = (f32[16,88,128]{2,1,0:T(8,128)S(1)}, bf16[16,88,128]{2,1,0:T(8,128)(2,1)S(1)}, f32[160,128]{1,0:T(8,128)S(1)}) custom-call(s32[1]{0:T(128)} %bitcast.core_ref, s32[2]{0:T(128)S(1)} %copy-done.3, bf16[768,1280]{1,0:T(8,128)(2,1)S(1)} %bitcast.13, bf16[2,768,256]{2,1,0:T(8,128)(2,1)S(1)} %bitcast.14, s32[2,5,8,512]{3,2,1,0:T(8,128)S(1)} %bitcast.18, ...), custom_call_target="tpu_custom_call" | custom-call | flops 12000000000 | bytes 12582912 | tf_op jit(solution)/shard_map/pallas_call | solution.py:379
  54.8 2.3 %all-gather.1 = bf16[32,88,128]{2,1,0:T(8,128)(2,1)S(1)} all-gather(bf16[16,88,128]{2,1,0:T(8,128)(2,1)S(1)} %get-tuple-element.16), channel_id=3, replica_groups={{0,16},{32,48},{64,80},{96,112},{128,144},{160,176},{192,208},{224,240}..., dimensions={0}, use_global_device_ids=true | all-gather | bytes 1081344 | tf_op jit(solution)/shard_map/all_gather | solution.py:483
  57.1 0.1 shard_map.106
  57.2 11.2 %all_to_all.20.message_ref = bf16[16,72,128]{2,1,0:T(8,128)(2,1)S(1)} all-to-all(bf16[16,72,128]{2,1,0:T(8,128)(2,1)S(1)} %get-tuple-element.17), channel_id=1, replica_groups=mesh['batch'=32,'feat'=16] {'feat'}, dimensions={0} | all-to-all | bytes 589824 | tf_op jit(solution)/shard_map/all_to_all | solution.py:485
  68.3 0.8 shard_map.107
  69.1 16.5 %all-to-all-start.2 = ((bf16[16,88,128]{2,1,0:T(8,128)(2,1)}), bf16[16,88,128]{2,1,0:T(8,128)(2,1)S(1)}, u32[]{:S(2)}, u32[]{:S(2)}) async-start(bf16[16,88,128]{2,1,0:T(8,128)(2,1)} %get-tuple-element.20), calls=%async_computation.2 | async-start | bytes 720896 | tf_op jit(solution)/shard_map/all_to_all | solution.py:487
  85.6 1.9 %collective-permute-start.2 = (f32[160,128]{1,0:T(8,128)S(1)}, f32[160,128]{1,0:T(8,128)S(1)}, u32[]{:S(2)}, u32[]{:S(2)}) collective-permute-start(f32[160,128]{1,0:T(8,128)S(1)} %get-tuple-element.21.s0_ref), channel_id=1, source_target_pairs={{0,3},{1,0},{2,1},{3,2},{4,7},{5,4},{6,5},{7,6},{8,11},{9,8},{10,9... | collective-permute-start | bytes 245768 | tf_op jit(solution)/shard_map/ppermute | solution.py:436
  87.6 3.9 %collective-permute-start.1 = (f32[160,128]{1,0:T(8,128)S(1)}, f32[160,128]{1,0:T(8,128)S(1)}, u32[]{:S(2)}, u32[]{:S(2)}) collective-permute-start(f32[160,128]{1,0:T(8,128)S(1)} %get-tuple-element.21.s0_ref), channel_id=1, source_target_pairs={{0,2},{1,3},{2,0},{3,1},{4,6},{5,7},{6,4},{7,5},{8,10},{9,11},{10,... | collective-permute-start | bytes 245768 | tf_op jit(solution)/shard_map/ppermute | solution.py:436
  91.5 1.9 %collective-permute-start = (f32[160,128]{1,0:T(8,128)S(1)}, f32[160,128]{1,0:T(8,128)S(1)}, u32[]{:S(2)}, u32[]{:S(2)}) collective-permute-start(f32[160,128]{1,0:T(8,128)S(1)} %get-tuple-element.21.s0_ref), channel_id=1, source_target_pairs={{0,1},{1,2},{2,3},{3,0},{4,5},{5,6},{6,7},{7,4},{8,9},{9,10},{10,1... | collective-permute-start | bytes 245768 | tf_op jit(solution)/shard_map/ppermute | solution.py:436
  93.4 0.0 collective-permute-done.2.s3_ref
  93.4 1.1 collective-permute-done.1.s2_ref
  94.5 3.8 %collective-permute-done.s1_ref = f32[160,128]{1,0:T(8,128)S(1)} collective-permute-done((f32[160,128]{1,0:T(8,128)S(1)}, f32[160,128]{1,0:T(8,128)S(1)}, u32[]{:S(2)}, u32[]{:S(2)}) %collective-permute-start) | collective-permute-done | bytes 81952 | tf_op jit(solution)/shard_map/ppermute | solution.py:436
  98.3 2.4 %all-to-all-done.2.pieces_ref = bf16[16,88,128]{2,1,0:T(8,128)(2,1)S(1)} async-done(((bf16[16,88,128]{2,1,0:T(8,128)(2,1)}), bf16[16,88,128]{2,1,0:T(8,128)(2,1)S(1)}, u32[]{:S(2)}, u32[]{:S(2)}) %all-to-all-start.2) | async-done | bytes 360480 | tf_op jit(solution)/shard_map/all_to_all | solution.py:487
  100.7 0.7 shard_map.108
  101.5 12.8 %all-to-all-start.3 = ((bf16[8,88,128]{2,1,0:T(8,128)(2,1)}), bf16[8,88,128]{2,1,0:T(8,128)(2,1)S(1)}, u32[]{:S(2)}, u32[]{:S(2)}) async-start(bf16[8,88,128]{2,1,0:T(8,128)(2,1)} %get-tuple-element.22), calls=%async_computation.3 | async-start | bytes 360448 | tf_op jit(solution)/shard_map/all_to_all | solution.py:491
  114.2 2.5 %collective-permute-start.5 = (f32[160,128]{1,0:T(8,128)S(1)}, f32[160,128]{1,0:T(8,128)S(1)}, u32[]{:S(2)}, u32[]{:S(2)}) collective-permute-start(f32[160,128]{1,0:T(8,128)S(1)} %get-tuple-element.23.s0_ref), channel_id=1, source_target_pairs={{0,12},{1,13},{2,14},{3,15},{4,0},{5,1},{6,2},{7,3},{8,4},{9,5},{1... | collective-permute-start | bytes 245768 | tf_op jit(solution)/shard_map/ppermute | solution.py:436
  116.7 1.9 %collective-permute-start.4 = (f32[160,128]{1,0:T(8,128)S(1)}, f32[160,128]{1,0:T(8,128)S(1)}, u32[]{:S(2)}, u32[]{:S(2)}) collective-permute-start(f32[160,128]{1,0:T(8,128)S(1)} %get-tuple-element.23.s0_ref), channel_id=1, source_target_pairs={{0,8},{1,9},{2,10},{3,11},{4,12},{5,13},{6,14},{7,15},{8,0},{9,1},... | collective-permute-start | bytes 245768 | tf_op jit(solution)/shard_map/ppermute | solution.py:436
  118.6 2.8 %collective-permute-start.3 = (f32[160,128]{1,0:T(8,128)S(1)}, f32[160,128]{1,0:T(8,128)S(1)}, u32[]{:S(2)}, u32[]{:S(2)}) collective-permute-start(f32[160,128]{1,0:T(8,128)S(1)} %get-tuple-element.23.s0_ref), channel_id=1, source_target_pairs={{0,4},{1,5},{2,6},{3,7},{4,8},{5,9},{6,10},{7,11},{8,12},{9,13},{1... | collective-permute-start | bytes 245768 | tf_op jit(solution)/shard_map/ppermute | solution.py:436
  121.4 6.6 %all-to-all-done.3 = bf16[8,88,128]{2,1,0:T(8,128)(2,1)S(1)} async-done(((bf16[8,88,128]{2,1,0:T(8,128)(2,1)}), bf16[8,88,128]{2,1,0:T(8,128)(2,1)S(1)}, u32[]{:S(2)}, u32[]{:S(2)}) %all-to-all-start.3) | async-done | bytes 180256 | tf_op jit(solution)/shard_map/all_to_all | solution.py:491
  128.0 12.2 %all-gather.2 = bf16[32,88,128]{2,1,0:T(8,128)(2,1)S(1)} all-gather(bf16[8,88,128]{2,1,0:T(8,128)(2,1)S(1)} %all-to-all-done.3), channel_id=4, replica_groups={{0,16,32,48},{64,80,96,112},{128,144,160,176},{192,208,224,240},{256,27..., dimensions={0}, use_global_device_ids=true | all-gather | bytes 901120 | tf_op jit(solution)/shard_map/all_gather | solution.py:493
  140.2 0.0 collective-permute-done.5.s3_ref
  140.2 0.0 collective-permute-done.4.s2_ref
  140.2 0.0 collective-permute-done.3.s1_ref
  140.2 1.5 %shard_map.109 = (f32[6,48,1024]{2,1,0:T(8,128)}, f32[6,64,153]{2,1,0:T(8,128)}, f32[153,128]{1,0:T(8,128)}) custom-call(bf16[4,8,88,128]{3,2,1,0:T(8,128)(2,1)S(1)} %bitcast.10, f32[160,128]{1,0:T(8,128)S(1)} %get-tuple-element.23.s0_ref, f32[160,128]{1,0:T(8,128)S(1)} %collective-permute-done.3.s1_ref, f32[160,128]{1,0:T(8,128)S(1)} %collective-permute-done.4.s2_ref, ...), custom_call_target="tpu_custom_call" | custom-call | tf_op jit(solution)/shard_map/pallas_call | solution.py:440
  (1 shorter events, 0.0 us)
Async XLA Ops:
  3.1 7.8 %copy-start.5 = (f32[64]{0:T(128)S(1)}, f32[64]{0:T(128)}, u32[]{:S(2)}) copy-start(f32[64]{0:T(128)} %param.13) | copy-start | bytes 772
  3.1 7.9 %copy-start.4 = (bf16[128,153]{0,1:T(8,128)(2,1)S(1)}, bf16[128,153]{0,1:T(8,128)(2,1)}, u32[]{:S(2)}) copy-start(bf16[128,153]{0,1:T(8,128)(2,1)} %param.15) | copy-start | bytes 117508
  3.1 31.5 %all-to-all-start = ((bf16[16,48,1280]{2,1,0:T(8,128)(2,1)}), bf16[16,48,1280]{2,1,0:T(8,128)(2,1)S(1)}, u32[]{:S(2)}, u32[]{:S(2)}) async-start(bf16[16,48,1280]{2,1,0:T(8,128)(2,1)} %shard_map.103), calls=%async_computation | async-start | bytes 3932160 | tf_op jit(solution)/shard_map/all_to_all | solution.py:466
  25.2 16.7 %copy-start = (bf16[128,153]{1,0:T(8,128)(2,1)S(1)}, bf16[128,153]{1,0:T(8,128)(2,1)}, u32[]{:S(2)}) copy-start(bf16[128,153]{1,0:T(8,128)(2,1)} %copy.16.upstream_ref) | copy-start | bytes 117508
  25.2 16.7 %copy-start.1 = (bf16[6,64,153]{2,1,0:T(8,128)(2,1)S(1)}, bf16[6,64,153]{2,1,0:T(8,128)(2,1)}, u32[]{:S(2)}) copy-start(bf16[6,64,153]{2,1,0:T(8,128)(2,1)} %param.14) | copy-start | bytes 352516
  25.2 16.7 %copy-start.2 = (s32[2,5,512,8]{2,3,1,0:T(8,128)S(1)}, s32[2,5,512,8]{2,3,1,0:T(8,128)}, u32[]{:S(2)}) copy-start(s32[2,5,512,8]{2,3,1,0:T(8,128)} %param.9) | copy-start | bytes 491524
  25.3 16.7 %copy-start.3 = (s32[2]{0:T(128)S(1)}, s32[2]{0:T(128)}, u32[]{:S(2)}) copy-start(s32[2]{0:T(128)} %counts_ref.3) | copy-start | bytes 28
  69.1 31.6 %all-to-all-start.2 = ((bf16[16,88,128]{2,1,0:T(8,128)(2,1)}), bf16[16,88,128]{2,1,0:T(8,128)(2,1)S(1)}, u32[]{:S(2)}, u32[]{:S(2)}) async-start(bf16[16,88,128]{2,1,0:T(8,128)(2,1)} %get-tuple-element.20), calls=%async_computation.2 | async-start | bytes 720896 | tf_op jit(solution)/shard_map/all_to_all | solution.py:487
  85.6 7.8 %collective-permute-start.2 = (f32[160,128]{1,0:T(8,128)S(1)}, f32[160,128]{1,0:T(8,128)S(1)}, u32[]{:S(2)}, u32[]{:S(2)}) collective-permute-start(f32[160,128]{1,0:T(8,128)S(1)} %get-tuple-element.21.s0_ref), channel_id=1, source_target_pairs={{0,3},{1,0},{2,1},{3,2},{4,7},{5,4},{6,5},{7,6},{8,11},{9,8},{10,9... | collective-permute-start | bytes 245768 | tf_op jit(solution)/shard_map/ppermute | solution.py:436
  87.6 7.0 %collective-permute-start.1 = (f32[160,128]{1,0:T(8,128)S(1)}, f32[160,128]{1,0:T(8,128)S(1)}, u32[]{:S(2)}, u32[]{:S(2)}) collective-permute-start(f32[160,128]{1,0:T(8,128)S(1)} %get-tuple-element.21.s0_ref), channel_id=1, source_target_pairs={{0,2},{1,3},{2,0},{3,1},{4,6},{5,7},{6,4},{7,5},{8,10},{9,11},{10,... | collective-permute-start | bytes 245768 | tf_op jit(solution)/shard_map/ppermute | solution.py:436
  91.5 6.9 %collective-permute-start = (f32[160,128]{1,0:T(8,128)S(1)}, f32[160,128]{1,0:T(8,128)S(1)}, u32[]{:S(2)}, u32[]{:S(2)}) collective-permute-start(f32[160,128]{1,0:T(8,128)S(1)} %get-tuple-element.21.s0_ref), channel_id=1, source_target_pairs={{0,1},{1,2},{2,3},{3,0},{4,5},{5,6},{6,7},{7,4},{8,9},{9,10},{10,1... | collective-permute-start | bytes 245768 | tf_op jit(solution)/shard_map/ppermute | solution.py:436
  101.5 26.6 %all-to-all-start.3 = ((bf16[8,88,128]{2,1,0:T(8,128)(2,1)}), bf16[8,88,128]{2,1,0:T(8,128)(2,1)S(1)}, u32[]{:S(2)}, u32[]{:S(2)}) async-start(bf16[8,88,128]{2,1,0:T(8,128)(2,1)} %get-tuple-element.22), calls=%async_computation.3 | async-start | bytes 360448 | tf_op jit(solution)/shard_map/all_to_all | solution.py:491
  114.2 26.0 %collective-permute-start.5 = (f32[160,128]{1,0:T(8,128)S(1)}, f32[160,128]{1,0:T(8,128)S(1)}, u32[]{:S(2)}, u32[]{:S(2)}) collective-permute-start(f32[160,128]{1,0:T(8,128)S(1)} %get-tuple-element.23.s0_ref), channel_id=1, source_target_pairs={{0,12},{1,13},{2,14},{3,15},{4,0},{5,1},{6,2},{7,3},{8,4},{9,5},{1... | collective-permute-start | bytes 245768 | tf_op jit(solution)/shard_map/ppermute | solution.py:436
  116.7 23.5 %collective-permute-start.4 = (f32[160,128]{1,0:T(8,128)S(1)}, f32[160,128]{1,0:T(8,128)S(1)}, u32[]{:S(2)}, u32[]{:S(2)}) collective-permute-start(f32[160,128]{1,0:T(8,128)S(1)} %get-tuple-element.23.s0_ref), channel_id=1, source_target_pairs={{0,8},{1,9},{2,10},{3,11},{4,12},{5,13},{6,14},{7,15},{8,0},{9,1},... | collective-permute-start | bytes 245768 | tf_op jit(solution)/shard_map/ppermute | solution.py:436
  118.6 21.6 %collective-permute-start.3 = (f32[160,128]{1,0:T(8,128)S(1)}, f32[160,128]{1,0:T(8,128)S(1)}, u32[]{:S(2)}, u32[]{:S(2)}) collective-permute-start(f32[160,128]{1,0:T(8,128)S(1)} %get-tuple-element.23.s0_ref), channel_id=1, source_target_pairs={{0,4},{1,5},{2,6},{3,7},{4,8},{5,9},{6,10},{7,11},{8,12},{9,13},{1... | collective-permute-start | bytes 245768 | tf_op jit(solution)/shard_map/ppermute | solution.py:436

commit v7 on v4

--- a/solution.py
+++ b/solution.py
@@ -425,7 +425,8 @@
 
 
 def spread_out(score, hops):
-    return [score] + [lax.ppermute(score, "feat", hops(step)) for step in range(1, SIDE)]
+    sent = score.astype(BF16)
+    return [score] + [lax.ppermute(sent, "feat", hops(step)) for step in range(1, SIDE)]
 
 
 def unpack(shards, scores):

time: 142 us -> 142 us (level)
  no operation moved by 1% of the time
where the time goes in v7:
time: 142 us
  starting transfers between devices  52 us (37%)
  blocking collectives  32.9 us (23%)
  Pallas kernels  31.8 us (22%)
  waiting for transfers between devices  23.2 us (16%)
    all_to_all x1, starting transfers between devices, local(): pieces = lax.all_to_all(shards, 'batch', 0, 0, axis_index_groups=same_core)  16.5 us
    ppermute x6, starting transfers between devices, spread_out(): lax.ppermute(sent, 'feat', hops(step))  14.9 us
    pallas_call x1, Pallas kernels, adjacency(): pl.pallas_call(adjacency_kernel, out_shape=shape(GROUPS, GRAPH_ROWS, CAPA...  13.6 us
    pallas_call x1, Pallas kernels, layers(): pl.pallas_call(layer_kernel, out_shape=(shard, shape(Z, SHARD_ROWS, 2 * U...  12.8 us
    all_to_all x1, starting transfers between devices, local(): shards = lax.all_to_all(copies, 'batch', 0, 0, axis_index_groups=same_place)  12.8 us
    all_gather x1, blocking collectives, local(): shards = lax.all_gather(shards, 'batch', axis_index_groups=blocks)  12.2 us
    all_to_all x1, blocking collectives, local(): message = lax.all_to_all(message, 'feat', 0, 0)  11.2 us
    all_to_all x1, waiting for transfers between devices, local(): lax.all_to_all(pack(core, vertex_embeddings.T, weight_one), 'feat', 0, 0)  9.35 us
  transfers between devices with their start and end apart: 9, of which 5 were waited for; matrix products, arithmetic and copies ran while one was open for 1% of the time, Pallas kernels for 10%

profile of v7, /device:TPU:1, one launch (start us, length us, event | category | flops | bytes accessed | tf_op | source)
XLA Modules:
  0.0 141.7 jit_solution(12514040399362250298)
XLA Ops:
  0.6 2.4 %shard_map.103 = bf16[16,48,1280]{2,1,0:T(8,128)(2,1)} custom-call(s32[1]{0:T(128)} %bitcast.core_ref, bf16[48,1024]{1,0:T(8,128)(2,1)} %bitcast.19, bf16[6,48,1024]{2,1,0:T(8,128)(2,1)} %w_ref.1), custom_call_target="tpu_custom_call" | custom-call | tf_op jit(solution)/shard_map/pallas_call | solution.py:340
  3.0 0.0 copy-start.5
  3.0 0.0 copy-start.4
  3.1 7.7 %all-to-all-start = ((bf16[16,48,1280]{2,1,0:T(8,128)(2,1)}), bf16[16,48,1280]{2,1,0:T(8,128)(2,1)S(1)}, u32[]{:S(2)}, u32[]{:S(2)}) async-start(bf16[16,48,1280]{2,1,0:T(8,128)(2,1)} %shard_map.103), calls=%async_computation | async-start | bytes 3932160 | tf_op jit(solution)/shard_map/all_to_all | solution.py:459
  10.8 0.0 copy-done.5
  10.8 0.1 copy.15.bias_ref
  10.9 0.0 copy-done.4
  10.9 0.7 copy.16.upstream_ref
  11.6 13.6 %shard_map.104.adj_from = bf16[2,3104,512]{2,1,0:T(8,128)(2,1)} custom-call(s32[2]{0:T(128)} %counts_ref.3, s32[2]{0:T(128)} %offsets_ref.1, s32[2,5,8,512]{3,2,1,0:T(8,128)} %bitcast.17, bf16[384,153]{1,0:T(8,128)(2,1)} %bitcast.15, bf16[128,153]{1,0:T(8,128)(2,1)} %copy.16.upstream_ref), custom_call_target="tpu_custom_call" | custom-call | flops 8000000000 | bytes 8388608 | tf_op jit(solution)/shard_map/pallas_call | solution.py:358
  25.2 0.0 copy-start
  25.2 0.0 copy-start.1
  25.2 0.0 copy-start.2
  25.2 0.0 copy-start.3
  25.2 9.4 %all-to-all-done = bf16[16,48,1280]{2,1,0:T(8,128)(2,1)S(1)} async-done(((bf16[16,48,1280]{2,1,0:T(8,128)(2,1)}), bf16[16,48,1280]{2,1,0:T(8,128)(2,1)S(1)}, u32[]{:S(2)}, u32[]{:S(2)}) %all-to-all-start) | async-done | bytes 1966112 | tf_op jit(solution)/shard_map/all_to_all | solution.py:459
  34.6 7.3 %all-gather = bf16[1536,256]{1,0:T(8,128)(2,1)S(1)} all-gather(bf16[768,256]{1,0:T(8,128)(2,1)S(1)} %slice.4), channel_id=2, replica_groups={{0,16},{32,48},{64,80},{96,112},{128,144},{160,176},{192,208},{224,240}..., dimensions={0}, use_global_device_ids=true | all-gather | bytes 1179648 | tf_op jit(solution)/shard_map/all_gather | solution.py:461
  41.9 0.0 copy-done
  41.9 0.0 copy-done.1
  41.9 0.0 copy-done.2
  41.9 0.0 copy-done.3
  41.9 12.8 %shard_map.105 = (f32[16,88,128]{2,1,0:T(8,128)S(1)}, bf16[16,88,128]{2,1,0:T(8,128)(2,1)S(1)}, f32[160,128]{1,0:T(8,128)S(1)}) custom-call(s32[1]{0:T(128)} %bitcast.core_ref, s32[2]{0:T(128)S(1)} %copy-done.3, bf16[768,1280]{1,0:T(8,128)(2,1)S(1)} %bitcast.13, bf16[2,768,256]{2,1,0:T(8,128)(2,1)S(1)} %bitcast.14, s32[2,5,8,512]{3,2,1,0:T(8,128)S(1)} %bitcast.18, ...), custom_call_target="tpu_custom_call" | custom-call | flops 12000000000 | bytes 12582912 | tf_op jit(solution)/shard_map/pallas_call | solution.py:371
  54.7 2.3 %all-gather.1 = bf16[32,88,128]{2,1,0:T(8,128)(2,1)S(1)} all-gather(bf16[16,88,128]{2,1,0:T(8,128)(2,1)S(1)} %get-tuple-element.16), channel_id=3, replica_groups={{0,16},{32,48},{64,80},{96,112},{128,144},{160,176},{192,208},{224,240}..., dimensions={0}, use_global_device_ids=true | all-gather | bytes 1081344 | tf_op jit(solution)/shard_map/all_gather | solution.py:476
  57.1 0.1 shard_map.106
  57.1 11.2 %all_to_all.20.message_ref = bf16[16,72,128]{2,1,0:T(8,128)(2,1)S(1)} all-to-all(bf16[16,72,128]{2,1,0:T(8,128)(2,1)S(1)} %get-tuple-element.17), channel_id=1, replica_groups=mesh['batch'=32,'feat'=16] {'feat'}, dimensions={0} | all-to-all | bytes 589824 | tf_op jit(solution)/shard_map/all_to_all | solution.py:478
  68.3 0.8 shard_map.107
  69.1 16.5 %all-to-all-start.2 = ((bf16[16,88,128]{2,1,0:T(8,128)(2,1)}), bf16[16,88,128]{2,1,0:T(8,128)(2,1)S(1)}, u32[]{:S(2)}, u32[]{:S(2)}) async-start(bf16[16,88,128]{2,1,0:T(8,128)(2,1)} %get-tuple-element.20), calls=%async_computation.2 | async-start | bytes 720896 | tf_op jit(solution)/shard_map/all_to_all | solution.py:480
  85.6 1.9 %collective-permute-start.2 = (bf16[160,128]{1,0:T(8,128)(2,1)S(1)}, bf16[160,128]{1,0:T(8,128)(2,1)S(1)}, u32[]{:S(2)}, u32[]{:S(2)}) collective-permute-start(bf16[160,128]{1,0:T(8,128)(2,1)S(1)} %convert_element_type.6), channel_id=1, source_target_pairs={{0,3},{1,0},{2,1},{3,2},{4,7},{5,4},{6,5},{7,6},{8,11},{9,8},{10,9... | collective-permute-start | bytes 122888 | tf_op jit(solution)/shard_map/ppermute | solution.py:429
  87.5 3.9 %collective-permute-start.1 = (bf16[160,128]{1,0:T(8,128)(2,1)S(1)}, bf16[160,128]{1,0:T(8,128)(2,1)S(1)}, u32[]{:S(2)}, u32[]{:S(2)}) collective-permute-start(bf16[160,128]{1,0:T(8,128)(2,1)S(1)} %convert_element_type.6), channel_id=1, source_target_pairs={{0,2},{1,3},{2,0},{3,1},{4,6},{5,7},{6,4},{7,5},{8,10},{9,11},{10,... | collective-permute-start | bytes 122888 | tf_op jit(solution)/shard_map/ppermute | solution.py:429
  91.4 1.9 %collective-permute-start = (bf16[160,128]{1,0:T(8,128)(2,1)S(1)}, bf16[160,128]{1,0:T(8,128)(2,1)S(1)}, u32[]{:S(2)}, u32[]{:S(2)}) collective-permute-start(bf16[160,128]{1,0:T(8,128)(2,1)S(1)} %convert_element_type.6), channel_id=1, source_target_pairs={{0,1},{1,2},{2,3},{3,0},{4,5},{5,6},{6,7},{7,4},{8,9},{9,10},{10,1... | collective-permute-start | bytes 122888 | tf_op jit(solution)/shard_map/ppermute | solution.py:429
  93.4 0.0 collective-permute-done.2.s3_ref
  93.4 0.4 collective-permute-done.1.s2_ref
  93.8 3.9 %collective-permute-done.s1_ref = bf16[160,128]{1,0:T(8,128)(2,1)S(1)} collective-permute-done((bf16[160,128]{1,0:T(8,128)(2,1)S(1)}, bf16[160,128]{1,0:T(8,128)(2,1)S(1)}, u32[]{:S(2)}, u32[]{:S(2)}) %collective-permute-start) | collective-permute-done | bytes 40992 | tf_op jit(solution)/shard_map/ppermute | solution.py:429
  97.7 3.0 %all-to-all-done.2.pieces_ref = bf16[16,88,128]{2,1,0:T(8,128)(2,1)S(1)} async-done(((bf16[16,88,128]{2,1,0:T(8,128)(2,1)}), bf16[16,88,128]{2,1,0:T(8,128)(2,1)S(1)}, u32[]{:S(2)}, u32[]{:S(2)}) %all-to-all-start.2) | async-done | bytes 360480 | tf_op jit(solution)/shard_map/all_to_all | solution.py:480
  100.7 0.7 shard_map.108
  101.4 12.8 %all-to-all-start.3 = ((bf16[8,88,128]{2,1,0:T(8,128)(2,1)}), bf16[8,88,128]{2,1,0:T(8,128)(2,1)S(1)}, u32[]{:S(2)}, u32[]{:S(2)}) async-start(bf16[8,88,128]{2,1,0:T(8,128)(2,1)} %get-tuple-element.22), calls=%async_computation.3 | async-start | bytes 360448 | tf_op jit(solution)/shard_map/all_to_all | solution.py:484
  114.2 2.5 %collective-permute-start.5 = (bf16[160,128]{1,0:T(8,128)(2,1)S(1)}, bf16[160,128]{1,0:T(8,128)(2,1)S(1)}, u32[]{:S(2)}, u32[]{:S(2)}) collective-permute-start(bf16[160,128]{1,0:T(8,128)(2,1)S(1)} %convert_element_type.7), channel_id=1, source_target_pairs={{0,12},{1,13},{2,14},{3,15},{4,0},{5,1},{6,2},{7,3},{8,4},{9,5},{1... | collective-permute-start | bytes 122888 | tf_op jit(solution)/shard_map/ppermute | solution.py:429
  116.7 1.9 %collective-permute-start.4 = (bf16[160,128]{1,0:T(8,128)(2,1)S(1)}, bf16[160,128]{1,0:T(8,128)(2,1)S(1)}, u32[]{:S(2)}, u32[]{:S(2)}) collective-permute-start(bf16[160,128]{1,0:T(8,128)(2,1)S(1)} %convert_element_type.7), channel_id=1, source_target_pairs={{0,8},{1,9},{2,10},{3,11},{4,12},{5,13},{6,14},{7,15},{8,0},{9,1},... | collective-permute-start | bytes 122888 | tf_op jit(solution)/shard_map/ppermute | solution.py:429
  118.6 2.8 %collective-permute-start.3 = (bf16[160,128]{1,0:T(8,128)(2,1)S(1)}, bf16[160,128]{1,0:T(8,128)(2,1)S(1)}, u32[]{:S(2)}, u32[]{:S(2)}) collective-permute-start(bf16[160,128]{1,0:T(8,128)(2,1)S(1)} %convert_element_type.7), channel_id=1, source_target_pairs={{0,4},{1,5},{2,6},{3,7},{4,8},{5,9},{6,10},{7,11},{8,12},{9,13},{1... | collective-permute-start | bytes 122888 | tf_op jit(solution)/shard_map/ppermute | solution.py:429
  121.4 6.6 %all-to-all-done.3 = bf16[8,88,128]{2,1,0:T(8,128)(2,1)S(1)} async-done(((bf16[8,88,128]{2,1,0:T(8,128)(2,1)}), bf16[8,88,128]{2,1,0:T(8,128)(2,1)S(1)}, u32[]{:S(2)}, u32[]{:S(2)}) %all-to-all-start.3) | async-done | bytes 180256 | tf_op jit(solution)/shard_map/all_to_all | solution.py:484
  128.0 12.2 %all-gather.2 = bf16[32,88,128]{2,1,0:T(8,128)(2,1)S(1)} all-gather(bf16[8,88,128]{2,1,0:T(8,128)(2,1)S(1)} %all-to-all-done.3), channel_id=4, replica_groups={{0,16,32,48},{64,80,96,112},{128,144,160,176},{192,208,224,240},{256,27..., dimensions={0}, use_global_device_ids=true | all-gather | bytes 901120 | tf_op jit(solution)/shard_map/all_gather | solution.py:486
  140.2 0.0 collective-permute-done.5.s3_ref
  140.2 0.0 collective-permute-done.4.s2_ref
  140.2 0.0 collective-permute-done.3.s1_ref
  140.2 1.5 %shard_map.109 = (f32[6,48,1024]{2,1,0:T(8,128)}, f32[6,64,153]{2,1,0:T(8,128)}, f32[153,128]{1,0:T(8,128)}) custom-call(bf16[4,8,88,128]{3,2,1,0:T(8,128)(2,1)S(1)} %bitcast.10, f32[160,128]{1,0:T(8,128)S(1)} %get-tuple-element.23.s0_ref, bf16[160,128]{1,0:T(8,128)(2,1)S(1)} %collective-permute-done.3.s1_ref, ...), custom_call_target="tpu_custom_call" | custom-call | tf_op jit(solution)/shard_map/pallas_call | solution.py:433
  (3 shorter events, 0.0 us)
Async XLA Ops:
  3.0 7.8 %copy-start.5 = (f32[64]{0:T(128)S(1)}, f32[64]{0:T(128)}, u32[]{:S(2)}) copy-start(f32[64]{0:T(128)} %param.13) | copy-start | bytes 772
  3.0 7.9 %copy-start.4 = (bf16[128,153]{0,1:T(8,128)(2,1)S(1)}, bf16[128,153]{0,1:T(8,128)(2,1)}, u32[]{:S(2)}) copy-start(bf16[128,153]{0,1:T(8,128)(2,1)} %param.15) | copy-start | bytes 117508
  3.1 31.5 %all-to-all-start = ((bf16[16,48,1280]{2,1,0:T(8,128)(2,1)}), bf16[16,48,1280]{2,1,0:T(8,128)(2,1)S(1)}, u32[]{:S(2)}, u32[]{:S(2)}) async-start(bf16[16,48,1280]{2,1,0:T(8,128)(2,1)} %shard_map.103), calls=%async_computation | async-start | bytes 3932160 | tf_op jit(solution)/shard_map/all_to_all | solution.py:459
  25.2 16.7 %copy-start = (bf16[128,153]{1,0:T(8,128)(2,1)S(1)}, bf16[128,153]{1,0:T(8,128)(2,1)}, u32[]{:S(2)}) copy-start(bf16[128,153]{1,0:T(8,128)(2,1)} %copy.16.upstream_ref) | copy-start | bytes 117508
  25.2 16.7 %copy-start.1 = (bf16[6,64,153]{2,1,0:T(8,128)(2,1)S(1)}, bf16[6,64,153]{2,1,0:T(8,128)(2,1)}, u32[]{:S(2)}) copy-start(bf16[6,64,153]{2,1,0:T(8,128)(2,1)} %param.14) | copy-start | bytes 352516
  25.2 16.7 %copy-start.2 = (s32[2,5,512,8]{2,3,1,0:T(8,128)S(1)}, s32[2,5,512,8]{2,3,1,0:T(8,128)}, u32[]{:S(2)}) copy-start(s32[2,5,512,8]{2,3,1,0:T(8,128)} %param.9) | copy-start | bytes 491524
  25.2 16.7 %copy-start.3 = (s32[2]{0:T(128)S(1)}, s32[2]{0:T(128)}, u32[]{:S(2)}) copy-start(s32[2]{0:T(128)} %counts_ref.3) | copy-start | bytes 28
  69.1 31.6 %all-to-all-start.2 = ((bf16[16,88,128]{2,1,0:T(8,128)(2,1)}), bf16[16,88,128]{2,1,0:T(8,128)(2,1)S(1)}, u32[]{:S(2)}, u32[]{:S(2)}) async-start(bf16[16,88,128]{2,1,0:T(8,128)(2,1)} %get-tuple-element.20), calls=%async_computation.2 | async-start | bytes 720896 | tf_op jit(solution)/shard_map/all_to_all | solution.py:480
  85.6 7.8 %collective-permute-start.2 = (bf16[160,128]{1,0:T(8,128)(2,1)S(1)}, bf16[160,128]{1,0:T(8,128)(2,1)S(1)}, u32[]{:S(2)}, u32[]{:S(2)}) collective-permute-start(bf16[160,128]{1,0:T(8,128)(2,1)S(1)} %convert_element_type.6), channel_id=1, source_target_pairs={{0,3},{1,0},{2,1},{3,2},{4,7},{5,4},{6,5},{7,6},{8,11},{9,8},{10,9... | collective-permute-start | bytes 122888 | tf_op jit(solution)/shard_map/ppermute | solution.py:429
  87.5 6.3 %collective-permute-start.1 = (bf16[160,128]{1,0:T(8,128)(2,1)S(1)}, bf16[160,128]{1,0:T(8,128)(2,1)S(1)}, u32[]{:S(2)}, u32[]{:S(2)}) collective-permute-start(bf16[160,128]{1,0:T(8,128)(2,1)S(1)} %convert_element_type.6), channel_id=1, source_target_pairs={{0,2},{1,3},{2,0},{3,1},{4,6},{5,7},{6,4},{7,5},{8,10},{9,11},{10,... | collective-permute-start | bytes 122888 | tf_op jit(solution)/shard_map/ppermute | solution.py:429
  91.4 6.3 %collective-permute-start = (bf16[160,128]{1,0:T(8,128)(2,1)S(1)}, bf16[160,128]{1,0:T(8,128)(2,1)S(1)}, u32[]{:S(2)}, u32[]{:S(2)}) collective-permute-start(bf16[160,128]{1,0:T(8,128)(2,1)S(1)} %convert_element_type.6), channel_id=1, source_target_pairs={{0,1},{1,2},{2,3},{3,0},{4,5},{5,6},{6,7},{7,4},{8,9},{9,10},{10,1... | collective-permute-start | bytes 122888 | tf_op jit(solution)/shard_map/ppermute | solution.py:429
  101.4 26.6 %all-to-all-start.3 = ((bf16[8,88,128]{2,1,0:T(8,128)(2,1)}), bf16[8,88,128]{2,1,0:T(8,128)(2,1)S(1)}, u32[]{:S(2)}, u32[]{:S(2)}) async-start(bf16[8,88,128]{2,1,0:T(8,128)(2,1)} %get-tuple-element.22), calls=%async_computation.3 | async-start | bytes 360448 | tf_op jit(solution)/shard_map/all_to_all | solution.py:484
  114.2 26.0 %collective-permute-start.5 = (bf16[160,128]{1,0:T(8,128)(2,1)S(1)}, bf16[160,128]{1,0:T(8,128)(2,1)S(1)}, u32[]{:S(2)}, u32[]{:S(2)}) collective-permute-start(bf16[160,128]{1,0:T(8,128)(2,1)S(1)} %convert_element_type.7), channel_id=1, source_target_pairs={{0,12},{1,13},{2,14},{3,15},{4,0},{5,1},{6,2},{7,3},{8,4},{9,5},{1... | collective-permute-start | bytes 122888 | tf_op jit(solution)/shard_map/ppermute | solution.py:429
  116.7 23.5 %collective-permute-start.4 = (bf16[160,128]{1,0:T(8,128)(2,1)S(1)}, bf16[160,128]{1,0:T(8,128)(2,1)S(1)}, u32[]{:S(2)}, u32[]{:S(2)}) collective-permute-start(bf16[160,128]{1,0:T(8,128)(2,1)S(1)} %convert_element_type.7), channel_id=1, source_target_pairs={{0,8},{1,9},{2,10},{3,11},{4,12},{5,13},{6,14},{7,15},{8,0},{9,1},... | collective-permute-start | bytes 122888 | tf_op jit(solution)/shard_map/ppermute | solution.py:429
  118.6 21.6 %collective-permute-start.3 = (bf16[160,128]{1,0:T(8,128)(2,1)S(1)}, bf16[160,128]{1,0:T(8,128)(2,1)S(1)}, u32[]{:S(2)}, u32[]{:S(2)}) collective-permute-start(bf16[160,128]{1,0:T(8,128)(2,1)S(1)} %convert_element_type.7), channel_id=1, source_target_pairs={{0,4},{1,5},{2,6},{3,7},{4,8},{5,9},{6,10},{7,11},{8,12},{9,13},{1... | collective-permute-start | bytes 122888 | tf_op jit(solution)/shard_map/ppermute | solution.py:429
